TPU v7x, 32 devices: a whole 2x2x4 slice. The times are simulated.
32 devices in a mesh: dp: 8 (over z, y), grp: 4 (over x, core).
Axes of the slice: x: 2, y: 2, z: 4, core: 2. Of those that a mesh axis runs over, the one named last changes fastest.
Arguments:
- states: bfloat16 [4096, 2048], P(('dp', 'grp')), may hold values from -60 to 60
- projection: bfloat16 [2048, 768], replicated, may hold values from -0.125 to 0.125
- owner_group: int32 [4096, 1], P(('dp', 'grp')), may hold values from 0 to 7; in each aligned block of 128 rows (0 to 127, 128 to 255, ...) at most 32 rows name the same one
- cluster_sub: int32 [4096], P(('dp', 'grp')), may hold values from 0 to 3
- priority: int32 [4096], P(('dp', 'grp')), may hold values from 0 to 4095, each once
Outputs:
- dup_score: float32 [4096], P(('dp', 'grp'))
Inputs may be any that keep to these rules, and one draw needn't show every extreme that they name: `owner_group`: in each aligned block of 128 rows (the rows of one device) no owner is named by more than 32 rows; in some block some owner is named by exactly 32 rows.
All inputs are finite; a program needn't handle non-finite values.
Results may differ from a plain program's by a relative error of at most 0.0012.
Values may be sent and summed in bfloat16 or wider, within the bound.
No kernel may reach another device: no remote copies, remote signals or barrier semaphores. Data moves between devices by JAX's collectives and lax.ppermute only.
A program may use at most 64 MiB of HBM per device.

v0:
```python
import math

import jax
import jax.numpy as jnp
from jax import lax
from jax.experimental import pallas as pl
from jax.experimental.pallas import tpu as pltpu
from jax.sharding import Mesh, PartitionSpec as P

AXES = ("line", "mid", "grp")
NOTE_ROWS = 8
RADIX = 256
CHUNKS = 8
VMEM = pl.BlockSpec(memory_space=pltpu.VMEM)
HBM = pl.BlockSpec(memory_space=pltpu.HBM)


def embed_kernel(
    states_hbm, proj_hbm, owner_hbm, sub_hbm, prio_hbm, block_ref,
    states, proj, owner, sub, prio, big_sem, small_sem,
):
    rows, depth = states.shape
    width = proj.shape[1]
    span = depth // CHUNKS
    copies = []
    for i in range(CHUNKS):
        part = pl.ds(i * span, span)
        copies.append((
            pltpu.make_async_copy(states_hbm.at[:, part], states.at[:, part], big_sem.at[0, i]),
            pltpu.make_async_copy(proj_hbm.at[part], proj.at[part], big_sem.at[1, i]),
        ))
    small = [
        pltpu.make_async_copy(src, dst, small_sem.at[i])
        for i, (src, dst) in enumerate(((owner_hbm, owner), (sub_hbm, sub), (prio_hbm, prio)))
    ]
    for copy in [c for pair in copies for c in pair] + small:
        copy.start()
    projected = None
    for i, pair in enumerate(copies):
        for copy in pair:
            copy.wait()
        part = slice(i * span, (i + 1) * span)
        term = jnp.dot(states[:, part], proj[part, :], preferred_element_type=jnp.float32)
        projected = term if projected is None else projected + term
    square_sum = jnp.sum(projected * projected, axis=1, keepdims=True)
    embedding = projected * lax.rsqrt(square_sum + 1e-06)
    for copy in small:
        copy.wait()
    rank = prio[...]
    high = lax.shift_right_logical(rank, 8)
    fields = (owner[...] + 1, sub[...], high, rank - high * RADIX)
    notes = [f.astype(jnp.float32) for f in fields]
    notes.append(jnp.zeros((NOTE_ROWS - len(fields), rows), jnp.float32))
    tiles = [embedding[:, i:i + rows] for i in range(0, width, rows)]
    block_ref[...] = jnp.concatenate(tiles + notes, axis=0).astype(jnp.bfloat16)


def embed(states, projection, owner, sub, prio):
    rows, depth = states.shape
    width = projection.shape[1]
    high = rows * (width // rows) + NOTE_ROWS
    return pl.pallas_call(
        embed_kernel,
        in_specs=[HBM] * 5,
        out_specs=VMEM,
        out_shape=jax.ShapeDtypeStruct((high, rows), jnp.bfloat16),
        scratch_shapes=[
            pltpu.VMEM((rows, depth), jnp.bfloat16),
            pltpu.VMEM((depth, width), jnp.bfloat16),
            pltpu.VMEM((1, rows), jnp.int32),
            pltpu.VMEM((1, rows), jnp.int32),
            pltpu.VMEM((1, rows), jnp.int32),
            pltpu.SemaphoreType.DMA((2, CHUNKS)),
            pltpu.SemaphoreType.DMA((3,)),
        ],
        compiler_params=pltpu.CompilerParams(vmem_limit_bytes=60 << 20),
        name="embed",
    )(states, projection, owner, sub, prio)


def read_notes(ref):
    tail = ref[ref.shape[0] - NOTE_ROWS:, :].astype(jnp.float32)
    owner, sub, high, low = (tail[i:i + 1] for i in range(4))
    return (owner - 1.0) * 4.0 + sub, high * float(RADIX) + low


def read_rows(refs):
    rows = refs[0].shape[1]
    firsts = range(0, refs[0].shape[0] - NOTE_ROWS, rows)
    return jnp.concatenate(
        [jnp.concatenate([ref[first:first + rows, :] for ref in refs], axis=0) for first in firsts],
        axis=1,
    )


def score_kernel(row_count, lane_count, products, parts, has_lines, seen_rows, hold, *refs):
    refs = list(refs)
    row_refs = [refs.pop(0) for _ in range(row_count)]
    lane_refs = [refs.pop(0) for _ in range(lane_count)]
    seen_lines = refs.pop(0) if has_lines else None
    seen_backs = refs.pop(0) if seen_rows else None
    lines_out = refs.pop(0)
    rows = lines_out.shape[1]
    if hold:
        refs[-1][...] = row_refs[0][...]
    row_notes = [read_notes(ref) for ref in row_refs]
    lane_notes = [read_notes(ref) for ref in lane_refs]
    fill = jnp.zeros((-2 * row_count % 8, rows), jnp.float32)
    lines = [line for pair in row_notes for line in pair]
    columns = jnp.concatenate(lines + ([fill] if fill.size else []), axis=0).T
    best, back = [None] * lane_count, [None] * row_count

    def top(old, new):
        return new if old is None else jnp.maximum(old, new)

    for row_set, lane_set in products:
        cosine = lax.dot_general(
            read_rows([row_refs[i] for i in row_set]),
            read_rows([lane_refs[j] for j in lane_set]),
            (((1,), (1,)), ((), ())),
            preferred_element_type=jnp.float32,
        )
        for m, i in enumerate(row_set):
            row_cluster, row_prio = columns[:, 2 * i:2 * i + 1], columns[:, 2 * i + 1:2 * i + 2]
            for n, j in enumerate(lane_set):
                lane_cluster, lane_prio = lane_notes[j]
                here = cosine[m * rows:(m + 1) * rows, n * rows:(n + 1) * rows]
                same = jnp.where(row_cluster == lane_cluster, here, -1.0)
                earlier = row_prio < lane_prio
                best[j] = top(best[j], jnp.where(earlier, same, -1.0))
                if j > 0:
                    back[i] = top(back[i], jnp.where(earlier, -1.0, same))
    lane_ids = lax.broadcasted_iota(jnp.int32, (rows, rows), 1)
    table = jnp.full((rows, rows), -1.0, jnp.float32)
    for i, each in enumerate(back):
        if each is not None:
            table = jnp.where(lane_ids == i, jnp.max(each, axis=1, keepdims=True), table)
    table = table.T
    if seen_rows:
        table = jnp.maximum(table[:row_count], seen_backs[...])
    for first, stop in parts:
        refs.pop(0)[...] = table[first:stop]
    lines = jnp.concatenate([jnp.max(b, axis=0, keepdims=True) for b in best], axis=0)
    if has_lines:
        count = seen_lines.shape[0]
        first = jnp.maximum(lines[:count], seen_lines[...])
        lines = first if count == lane_count else jnp.concatenate([first, lines[count:]], axis=0)
    lines_out[...] = lines


def score(name, row_blocks, lane_blocks, products, parts, lines=None, backs=None, hold=False):
    high, rows = row_blocks[0].shape
    width = high - NOTE_ROWS
    inputs = [*row_blocks, *lane_blocks, *(seen for seen in (lines, backs) if seen is not None)]
    shapes = [(len(lane_blocks), rows)] + [(stop - first, rows) for first, stop in parts]
    outs = [jax.ShapeDtypeStruct(shape, jnp.float32) for shape in shapes]
    if hold:
        outs.append(jax.ShapeDtypeStruct((high, rows), row_blocks[0].dtype))
    counts = len(row_blocks), len(lane_blocks)
    rest = products, parts, lines is not None, backs is not None, hold
    macs = sum(len(r) * len(c) for r, c in products) * rows * rows * width
    return pl.pallas_call(
        lambda *refs: score_kernel(*counts, *rest, *refs),
        in_specs=[VMEM] * len(inputs),
        out_specs=[VMEM] * len(outs),
        out_shape=outs,
        compiler_params=pltpu.CompilerParams(vmem_limit_bytes=48 << 20),
        cost_estimate=pl.CostEstimate(
            flops=2 * macs, bytes_accessed=2 * sum(counts) * rows * width, transcendentals=0
        ),
        name=name,
    )(*inputs)


def tournament(line):
    moves = [[(i, (i + s) % line) for i in range(line)] for s in range(1, (line + 1) // 2)]
    if line % 2 == 0:
        half = line // 2
        pairs = [(i, i + half) if i % 2 else (i + half, i) for i in range(half)]
        sent, met = {a for a, _ in pairs}, {b for _, b in pairs}
        idle = [i for i in range(line) if i not in sent]
        free = [i for i in range(line) if i not in met]
        moves.append(pairs + list(zip(idle, free)))
    return moves


def on_device(states, projection, owner_group, cluster_sub, priority):
    line, grp = lax.axis_size("line"), lax.axis_size("grp")
    plane = lax.axis_size("mid") * grp
    rows = states.shape[0]

    def move(array, pairs):
        whole = [(a * plane + p, b * plane + p) for a, b in pairs for p in range(plane)]
        return lax.ppermute(array, AXES, whole)

    def swap(array, step):
        pairs = [(i, i // plane * plane + (i % plane ^ step)) for i in range(line * plane)]
        return lax.ppermute(array, AXES, pairs)

    block = embed(
        states,
        projection,
        owner_group.reshape(1, rows),
        cluster_sub.reshape(1, rows),
        priority.reshape(1, rows),
    )
    moves = tournament(line)
    visitors = [move(block, pairs) for pairs in moves]
    bits = [1 << i for i in range(1, plane.bit_length() - 1)]
    found = {0: block}
    for bit in reversed(bits):
        found |= {step | bit: swap(here, bit) for step, here in found.items()}
    row_blocks = [found[step] for step in sorted(found)]

    lanes = [block] + visitors
    every, count = tuple(range(len(lanes))), len(row_blocks)
    half = count // 2
    soon = (0, half)
    rest = tuple(i for i in range(count) if i not in soon)
    lines, held = score(
        "score_soon", [row_blocks[i] for i in soon], lanes[:1], [((0, 1), (0,))], [], hold=True
    )
    row_blocks[0] = lanes[0] = held
    products = [(rest, every), (soon, every[1:])]
    lines, backs = score("score_late", row_blocks, lanes, products, [(0, count)], lines)
    ready = lax.optimization_barrier((lanes[-1], row_blocks[1], held, *visitors[:-1]))[0]
    partner = [swap(lane, 1) for lane in lanes[:-1] + [ready]]
    products, parts = [(tuple(range(count)), every)], [(0, half), (half, count)]
    theirs, near, far = score("score_partner", row_blocks, partner, products, parts, None, backs)
    lines = jnp.maximum(lines, swap(theirs, 1))
    for bit in bits[:0:-1]:
        near = jnp.maximum(near, swap(far, bit))
        half = near.shape[0] // 2
        near, far = near[:half], near[half:]
    total = lines[:1]
    for i, pairs in reversed(list(enumerate(moves))):
        total = jnp.maximum(total, move(lines[i + 1:i + 2], [(b, a) for a, b in pairs]))
    total = lax.optimization_barrier(total)
    total = jnp.maximum(jnp.maximum(total, near), swap(far, bits[0]))
    return total.reshape(rows)


def solution(mesh):
    num_dp, num_grp = mesh.shape["dp"], mesh.shape["grp"]
    line = min(num_dp, 1 << (int(math.log2(num_dp * num_grp)) // 2))
    split = Mesh(mesh.devices.reshape(line, num_dp // line, num_grp), AXES)
    in_specs = (P(AXES, None), P(), P(AXES, None), P(AXES), P(AXES))
    return jax.shard_map(
        on_device, mesh=split, in_specs=in_specs, out_specs=P(AXES), check_vma=False
    )
```

profile of v0, /device:TPU:0, one launch (start us, length us, event | category | flops | bytes accessed | tf_op | source)
XLA Modules:
  0.0 31.0 jit_solution(11199975951357293442)
XLA Ops:
  0.0 3.3 %embed.1.refs_0_.refs_2_ = bf16[776,128]{1,0:T(8,128)(2,1)} custom-call(bf16[128,2048]{1,0:T(8,128)(2,1)} %states_hbm.1, bf16[2048,768]{1,0:T(8,128)(2,1)} %proj_hbm.1, s32[1,128]{1,0:T(1,128)} %bitcast.5, s32[1,128]{1,0:T(1,128)} %bitcast.6, s32[1,128]{1,0:T(1,128)} %bitcast.7), custom_call_target="tpu_custom_call" | custom-call | tf_op jit(solution)/shard_map/embed/pallas_call | solution.py:62
  3.3 3.0 %collective-permute-start = (bf16[776,128]{1,0:T(8,128)(2,1)}, bf16[776,128]{1,0:T(8,128)(2,1)S(1)}, u32[]{:S(2)}, u32[]{:S(2)}) collective-permute-start(bf16[776,128]{1,0:T(8,128)(2,1)} %embed.1.refs_0_.refs_2_), channel_id=1, source_target_pairs={{0,4},{1,5},{2,6},{3,7},{4,0},{5,1},{6,2},{7,3},{8,12},{9,13},{10,... | collective-permute-start | bytes 595976 | tf_op jit(solution)/shard_map/ppermute | solution.py:198
  6.3 1.5 %collective-permute-start.1 = (bf16[776,128]{1,0:T(8,128)(2,1)}, bf16[776,128]{1,0:T(8,128)(2,1)S(1)}, u32[]{:S(2)}, u32[]{:S(2)}) collective-permute-start(bf16[776,128]{1,0:T(8,128)(2,1)} %embed.1.refs_0_.refs_2_), channel_id=1, source_target_pairs={{0,2},{1,3},{2,0},{3,1},{4,6},{5,7},{6,4},{7,5},{8,10},{9,11},{10,... | collective-permute-start | bytes 595976 | tf_op jit(solution)/shard_map/ppermute | solution.py:198
  7.8 1.6 %collective-permute-start.3 = (bf16[776,128]{1,0:T(8,128)(2,1)}, bf16[776,128]{1,0:T(8,128)(2,1)S(1)}, u32[]{:S(2)}, u32[]{:S(2)}) collective-permute-start(bf16[776,128]{1,0:T(8,128)(2,1)} %embed.1.refs_0_.refs_2_), channel_id=1, source_target_pairs={{0,8},{1,9},{2,10},{3,11},{4,12},{5,13},{6,14},{7,15},{8,16},{9,17... | collective-permute-start | bytes 595976 | tf_op jit(solution)/shard_map/ppermute | solution.py:194
  9.4 1.6 %collective-permute-start.4 = (bf16[776,128]{1,0:T(8,128)(2,1)}, bf16[776,128]{1,0:T(8,128)(2,1)S(1)}, u32[]{:S(2)}, u32[]{:S(2)}) collective-permute-start(bf16[776,128]{1,0:T(8,128)(2,1)} %embed.1.refs_0_.refs_2_), channel_id=1, source_target_pairs={{16,0},{17,1},{18,2},{19,3},{20,4},{21,5},{22,6},{23,7},{8,24},{9,... | collective-permute-start | bytes 595976 | tf_op jit(solution)/shard_map/ppermute | solution.py:194
  11.0 0.5 %collective-permute-done.refs_1_.refs_2_ = bf16[776,128]{1,0:T(8,128)(2,1)S(1)} collective-permute-done((bf16[776,128]{1,0:T(8,128)(2,1)}, bf16[776,128]{1,0:T(8,128)(2,1)S(1)}, u32[]{:S(2)}, u32[]{:S(2)}) %collective-permute-start) | collective-permute-done | bytes 198688 | tf_op jit(solution)/shard_map/ppermute | solution.py:198
  11.5 1.7 %collective-permute-start.2 = (bf16[776,128]{1,0:T(8,128)(2,1)S(1)}, bf16[776,128]{1,0:T(8,128)(2,1)S(1)}, u32[]{:S(2)}, u32[]{:S(2)}) collective-permute-start(bf16[776,128]{1,0:T(8,128)(2,1)S(1)} %collective-permute-done.refs_1_.refs_2_), channel_id=1, source_target_pairs={{0,2},{1,3},{2,0},{3,1},{4,6},{5,7},{6,4},{7,5},{8,10},{9,11},{10,... | collective-permute-start | bytes 595976 | tf_op jit(solution)/shard_map/ppermute | solution.py:198
  13.2 0.9 %copy-done = bf16[776,128]{1,0:T(8,128)(2,1)S(1)} copy-done((bf16[776,128]{1,0:T(8,128)(2,1)S(1)}, bf16[776,128]{1,0:T(8,128)(2,1)}, u32[]{:S(2)}) %copy-start) | copy-done | bytes 198680
  14.1 0.3 %score_soon.1 = (f32[1,128]{1,0:T(1,128)S(1)}, bf16[776,128]{1,0:T(8,128)(2,1)S(1)}) custom-call(bf16[776,128]{1,0:T(8,128)(2,1)S(1)} %copy-done, bf16[776,128]{1,0:T(8,128)(2,1)S(1)} %collective-permute-done.refs_1_.refs_2_, bf16[776,128]{1,0:T(8,128)(2,1)S(1)} %copy-done), custom_call_target="tpu_custom_call" | custom-call | flops 50331648 | bytes 589824 | tf_op jit(solution)/shard_map/score_soon/pallas_call | solution.py:162
  14.5 3.3 %collective-permute-done.3.refs_5_ = bf16[776,128]{1,0:T(8,128)(2,1)S(1)} collective-permute-done((bf16[776,128]{1,0:T(8,128)(2,1)}, bf16[776,128]{1,0:T(8,128)(2,1)S(1)}, u32[]{:S(2)}, u32[]{:S(2)}) %collective-permute-start.3) | collective-permute-done | bytes 198688 | tf_op jit(solution)/shard_map/ppermute | solution.py:194
  17.8 2.6 %collective-permute-done.4.refs_6_ = bf16[776,128]{1,0:T(8,128)(2,1)S(1)} collective-permute-done((bf16[776,128]{1,0:T(8,128)(2,1)}, bf16[776,128]{1,0:T(8,128)(2,1)S(1)}, u32[]{:S(2)}, u32[]{:S(2)}) %collective-permute-start.4) | collective-permute-done | bytes 198688 | tf_op jit(solution)/shard_map/ppermute | solution.py:194
  20.3 0.5 %collective-permute-start.5 = (bf16[776,128]{1,0:T(8,128)(2,1)S(1)}, bf16[776,128]{1,0:T(8,128)(2,1)S(1)}, u32[]{:S(2)}, u32[]{:S(2)}) collective-permute-start(bf16[776,128]{1,0:T(8,128)(2,1)S(1)} %get-tuple-element.13.refs_0_.refs_4_), channel_id=1, source_target_pairs={{0,1},{1,0},{2,3},{3,2},{4,5},{5,4},{6,7},{7,6},{8,9},{9,8},{10,11... | collective-permute-start | bytes 595976 | tf_op jit(solution)/shard_map/ppermute | solution.py:198
  20.8 0.7 %score_late.1 = (f32[3,128]{1,0:T(4,128)S(1)}, f32[4,128]{1,0:T(4,128)S(1)}) custom-call(bf16[776,128]{1,0:T(8,128)(2,1)S(1)} %get-tuple-element.13.refs_0_.refs_4_, bf16[776,128]{1,0:T(8,128)(2,1)S(1)} %collective-permute-done.1.refs_1_, bf16[776,128]{1,0:T(8,128)(2,1)S(1)} %collective-permute-done.refs_1_.refs_2_, ...), custom_call_target="tpu_custom_call" | custom-call | flops 251658240 | bytes 1376256 | tf_op jit(solution)/shard_map/score_late/pallas_call | solution.py:162
  21.8 0.3 collective-permute-done.5.refs_4_
  22.3 0.7 %score_partner.1 = (f32[3,128]{1,0:T(4,128)S(1)}, f32[2,128]{1,0:T(2,128)S(1)}, f32[2,128]{1,0:T(2,128)S(1)}) custom-call(bf16[776,128]{1,0:T(8,128)(2,1)S(1)} %get-tuple-element.13.refs_0_.refs_4_, bf16[776,128]{1,0:T(8,128)(2,1)S(1)} %collective-permute-done.1.refs_1_, bf16[776,128]{1,0:T(8,128)(2,1)S(1)} %collective-permute-done.refs_1_.refs_2_, ...), custom_call_target="tpu_custom_call" | custom-call | flops 301989888 | bytes 1376256 | tf_op jit(solution)/shard_map/score_partner/pallas_call | solution.py:162
  23.3 0.5 %collective-permute-start.11 = (f32[2,128]{1,0:T(2,128)S(1)}, f32[2,128]{1,0:T(2,128)S(1)}, u32[]{:S(2)}, u32[]{:S(2)}) collective-permute-start(f32[2,128]{1,0:T(2,128)S(1)} %get-tuple-element.20), channel_id=1, source_target_pairs={{0,4},{1,5},{2,6},{3,7},{4,0},{5,1},{6,2},{7,3},{8,12},{9,13},{10,... | collective-permute-start | bytes 3080 | tf_op jit(solution)/shard_map/ppermute | solution.py:198
  23.8 0.4 %collective-permute-done.8 = f32[3,128]{1,0:T(4,128)S(1)} collective-permute-done((f32[3,128]{1,0:T(4,128)S(1)}, f32[3,128]{1,0:T(4,128)S(1)}, u32[]{:S(2)}, u32[]{:S(2)}) %collective-permute-start.8) | collective-permute-done | bytes 1568 | tf_op jit(solution)/shard_map/ppermute | solution.py:198
  24.3 1.7 %collective-permute-start.10 = (f32[1,128]{1,0:T(1,128)S(1)}, f32[1,128]{1,0:T(1,128)S(1)}, u32[]{:S(2)}, u32[]{:S(2)}) collective-permute-start(f32[1,128]{1,0:T(1,128)S(1)} %get-tuple-element.22), channel_id=1, source_target_pairs={{8,0},{9,1},{10,2},{11,3},{12,4},{13,5},{14,6},{15,7},{16,8},{17,9... | collective-permute-start | bytes 1544 | tf_op jit(solution)/shard_map/ppermute | solution.py:194
  26.0 0.9 %collective-permute-done.11 = f32[2,128]{1,0:T(2,128)S(1)} collective-permute-done((f32[2,128]{1,0:T(2,128)S(1)}, f32[2,128]{1,0:T(2,128)S(1)}, u32[]{:S(2)}, u32[]{:S(2)}) %collective-permute-start.11) | collective-permute-done | bytes 1056 | tf_op jit(solution)/shard_map/ppermute | solution.py:198
  26.9 0.5 %collective-permute-start.12 = (f32[1,128]{1,0:T(1,128)S(1)}, f32[1,128]{1,0:T(1,128)S(1)}, u32[]{:S(2)}, u32[]{:S(2)}) collective-permute-start(f32[1,128]{1,0:T(1,128)S(1)} %slice.19), channel_id=1, source_target_pairs={{0,2},{1,3},{2,0},{3,1},{4,6},{5,7},{6,4},{7,5},{8,10},{9,11},{10,... | collective-permute-start | bytes 1544 | tf_op jit(solution)/shard_map/ppermute | solution.py:198
  27.5 0.4 %collective-permute-done.10 = f32[1,128]{1,0:T(1,128)S(1)} collective-permute-done((f32[1,128]{1,0:T(1,128)S(1)}, f32[1,128]{1,0:T(1,128)S(1)}, u32[]{:S(2)}, u32[]{:S(2)}) %collective-permute-start.10) | collective-permute-done | bytes 544 | tf_op jit(solution)/shard_map/ppermute | solution.py:194
  27.8 1.7 %collective-permute-done.9 = f32[1,128]{1,0:T(1,128)S(1)} collective-permute-done((f32[1,128]{1,0:T(1,128)S(1)}, f32[1,128]{1,0:T(1,128)S(1)}, u32[]{:S(2)}, u32[]{:S(2)}) %collective-permute-start.9) | collective-permute-done | bytes 544 | tf_op jit(solution)/shard_map/ppermute | solution.py:194
  29.5 0.9 %collective-permute-done.12 = f32[1,128]{1,0:T(1,128)S(1)} collective-permute-done((f32[1,128]{1,0:T(1,128)S(1)}, f32[1,128]{1,0:T(1,128)S(1)}, u32[]{:S(2)}, u32[]{:S(2)}) %collective-permute-start.12) | collective-permute-done | bytes 544 | tf_op jit(solution)/shard_map/ppermute | solution.py:198
  30.5 0.5 %maximum_bitcast_fusion = f32[128]{0:T(128)} fusion(f32[1,128]{1,0:T(1,128)S(1)} %collective-permute-done.12, f32[1,128]{1,0:T(1,128)S(1)} %maximum_maximum_fusion, f32[2,128]{1,0:T(2,128)S(1)} %max.21), kind=kLoop, calls=%fused_computation | loop fusion | flops 256 | bytes 2048 | tf_op jit(solution)/shard_map/reshape | solution.py:240
  (14 shorter events, 0.9 us)
Async XLA Ops:
  3.3 8.2 %collective-permute-start = (bf16[776,128]{1,0:T(8,128)(2,1)}, bf16[776,128]{1,0:T(8,128)(2,1)S(1)}, u32[]{:S(2)}, u32[]{:S(2)}) collective-permute-start(bf16[776,128]{1,0:T(8,128)(2,1)} %embed.1.refs_0_.refs_2_), channel_id=1, source_target_pairs={{0,4},{1,5},{2,6},{3,7},{4,0},{5,1},{6,2},{7,3},{8,12},{9,13},{10,... | collective-permute-start | bytes 595976 | tf_op jit(solution)/shard_map/ppermute | solution.py:198
  6.3 8.1 %collective-permute-start.1 = (bf16[776,128]{1,0:T(8,128)(2,1)}, bf16[776,128]{1,0:T(8,128)(2,1)S(1)}, u32[]{:S(2)}, u32[]{:S(2)}) collective-permute-start(bf16[776,128]{1,0:T(8,128)(2,1)} %embed.1.refs_0_.refs_2_), channel_id=1, source_target_pairs={{0,2},{1,3},{2,0},{3,1},{4,6},{5,7},{6,4},{7,5},{8,10},{9,11},{10,... | collective-permute-start | bytes 595976 | tf_op jit(solution)/shard_map/ppermute | solution.py:198
  7.8 9.9 %collective-permute-start.3 = (bf16[776,128]{1,0:T(8,128)(2,1)}, bf16[776,128]{1,0:T(8,128)(2,1)S(1)}, u32[]{:S(2)}, u32[]{:S(2)}) collective-permute-start(bf16[776,128]{1,0:T(8,128)(2,1)} %embed.1.refs_0_.refs_2_), channel_id=1, source_target_pairs={{0,8},{1,9},{2,10},{3,11},{4,12},{5,13},{6,14},{7,15},{8,16},{9,17... | collective-permute-start | bytes 595976 | tf_op jit(solution)/shard_map/ppermute | solution.py:194
  9.4 10.9 %collective-permute-start.4 = (bf16[776,128]{1,0:T(8,128)(2,1)}, bf16[776,128]{1,0:T(8,128)(2,1)S(1)}, u32[]{:S(2)}, u32[]{:S(2)}) collective-permute-start(bf16[776,128]{1,0:T(8,128)(2,1)} %embed.1.refs_0_.refs_2_), channel_id=1, source_target_pairs={{16,0},{17,1},{18,2},{19,3},{20,4},{21,5},{22,6},{23,7},{8,24},{9,... | collective-permute-start | bytes 595976 | tf_op jit(solution)/shard_map/ppermute | solution.py:194
  11.5 9.4 %collective-permute-start.2 = (bf16[776,128]{1,0:T(8,128)(2,1)S(1)}, bf16[776,128]{1,0:T(8,128)(2,1)S(1)}, u32[]{:S(2)}, u32[]{:S(2)}) collective-permute-start(bf16[776,128]{1,0:T(8,128)(2,1)S(1)} %collective-permute-done.refs_1_.refs_2_), channel_id=1, source_target_pairs={{0,2},{1,3},{2,0},{3,1},{4,6},{5,7},{6,4},{7,5},{8,10},{9,11},{10,... | collective-permute-start | bytes 595976 | tf_op jit(solution)/shard_map/ppermute | solution.py:198
  13.2 0.9 %copy-start = (bf16[776,128]{1,0:T(8,128)(2,1)S(1)}, bf16[776,128]{1,0:T(8,128)(2,1)}, u32[]{:S(2)}) copy-start(bf16[776,128]{1,0:T(8,128)(2,1)} %embed.1.refs_0_.refs_2_) | copy-start | bytes 595972
  20.3 1.4 %collective-permute-start.7 = (bf16[776,128]{1,0:T(8,128)(2,1)S(1)}, bf16[776,128]{1,0:T(8,128)(2,1)S(1)}, u32[]{:S(2)}, u32[]{:S(2)}) collective-permute-start(bf16[776,128]{1,0:T(8,128)(2,1)S(1)} %collective-permute-done.4.refs_6_), channel_id=1, source_target_pairs={{0,1},{1,0},{2,3},{3,2},{4,5},{5,4},{6,7},{7,6},{8,9},{9,8},{10,11... | collective-permute-start | bytes 595976 | tf_op jit(solution)/shard_map/ppermute | solution.py:198
  20.3 1.7 %collective-permute-start.5 = (bf16[776,128]{1,0:T(8,128)(2,1)S(1)}, bf16[776,128]{1,0:T(8,128)(2,1)S(1)}, u32[]{:S(2)}, u32[]{:S(2)}) collective-permute-start(bf16[776,128]{1,0:T(8,128)(2,1)S(1)} %get-tuple-element.13.refs_0_.refs_4_), channel_id=1, source_target_pairs={{0,1},{1,0},{2,3},{3,2},{4,5},{5,4},{6,7},{7,6},{8,9},{9,8},{10,11... | collective-permute-start | bytes 595976 | tf_op jit(solution)/shard_map/ppermute | solution.py:198
  20.8 1.5 %collective-permute-start.6 = (bf16[776,128]{1,0:T(8,128)(2,1)S(1)}, bf16[776,128]{1,0:T(8,128)(2,1)S(1)}, u32[]{:S(2)}, u32[]{:S(2)}) collective-permute-start(bf16[776,128]{1,0:T(8,128)(2,1)S(1)} %collective-permute-done.3.refs_5_), channel_id=1, source_target_pairs={{0,1},{1,0},{2,3},{3,2},{4,5},{5,4},{6,7},{7,6},{8,9},{9,8},{10,11... | collective-permute-start | bytes 595976 | tf_op jit(solution)/shard_map/ppermute | solution.py:198
  23.1 1.2 %collective-permute-start.8 = (f32[3,128]{1,0:T(4,128)S(1)}, f32[3,128]{1,0:T(4,128)S(1)}, u32[]{:S(2)}, u32[]{:S(2)}) collective-permute-start(f32[3,128]{1,0:T(4,128)S(1)} %get-tuple-element.18), channel_id=1, source_target_pairs={{0,1},{1,0},{2,3},{3,2},{4,5},{5,4},{6,7},{7,6},{8,9},{9,8},{10,11... | collective-permute-start | bytes 4616 | tf_op jit(solution)/shard_map/ppermute | solution.py:198
  23.3 3.6 %collective-permute-start.11 = (f32[2,128]{1,0:T(2,128)S(1)}, f32[2,128]{1,0:T(2,128)S(1)}, u32[]{:S(2)}, u32[]{:S(2)}) collective-permute-start(f32[2,128]{1,0:T(2,128)S(1)} %get-tuple-element.20), channel_id=1, source_target_pairs={{0,4},{1,5},{2,6},{3,7},{4,0},{5,1},{6,2},{7,3},{8,12},{9,13},{10,... | collective-permute-start | bytes 3080 | tf_op jit(solution)/shard_map/ppermute | solution.py:198
  24.3 3.5 %collective-permute-start.10 = (f32[1,128]{1,0:T(1,128)S(1)}, f32[1,128]{1,0:T(1,128)S(1)}, u32[]{:S(2)}, u32[]{:S(2)}) collective-permute-start(f32[1,128]{1,0:T(1,128)S(1)} %get-tuple-element.22), channel_id=1, source_target_pairs={{8,0},{9,1},{10,2},{11,3},{12,4},{13,5},{14,6},{15,7},{16,8},{17,9... | collective-permute-start | bytes 1544 | tf_op jit(solution)/shard_map/ppermute | solution.py:194
  26.0 3.5 %collective-permute-start.9 = (f32[1,128]{1,0:T(1,128)S(1)}, f32[1,128]{1,0:T(1,128)S(1)}, u32[]{:S(2)}, u32[]{:S(2)}) collective-permute-start(f32[1,128]{1,0:T(1,128)S(1)} %get-tuple-element.21), channel_id=1, source_target_pairs={{0,16},{1,17},{2,18},{3,19},{4,20},{5,21},{6,22},{7,23},{24,8},{25... | collective-permute-start | bytes 1544 | tf_op jit(solution)/shard_map/ppermute | solution.py:194
  26.9 3.5 %collective-permute-start.12 = (f32[1,128]{1,0:T(1,128)S(1)}, f32[1,128]{1,0:T(1,128)S(1)}, u32[]{:S(2)}, u32[]{:S(2)}) collective-permute-start(f32[1,128]{1,0:T(1,128)S(1)} %slice.19), channel_id=1, source_target_pairs={{0,2},{1,3},{2,0},{3,1},{4,6},{5,7},{6,4},{7,5},{8,10},{9,11},{10,... | collective-permute-start | bytes 1544 | tf_op jit(solution)/shard_map/ppermute | solution.py:198
where the time goes:
time: 31.1 us; the launch traced here: 31 us
  starting transfers between devices  12.9 us (41%)
  waiting for transfers between devices  11.5 us (37%)
  Pallas kernels  5.03 us (16%)
  local copies, waits for them, and re-layouts  0.94 us (3%)
  other arithmetic  0.52 us (2%)
    ppermute x9, starting transfers between devices, swap(): return lax.ppermute(array, AXES, pairs)  8.06 us
    ppermute x4, waiting for transfers between devices, move(): return lax.ppermute(array, AXES, whole)  7.92 us
    ppermute x4, starting transfers between devices, move(): return lax.ppermute(array, AXES, whole)  4.87 us
    ppermute x9, waiting for transfers between devices, swap(): return lax.ppermute(array, AXES, pairs)  3.58 us
    pallas_call x1, Pallas kernels, embed(): pl.pallas_call(embed_kernel, in_specs=[HBM] * 5, out_specs=VMEM, out_shap...  3.29 us
    pallas_call x3, Pallas kernels, score(): pl.pallas_call(lambda *refs: score_kernel(*counts, *rest, *refs), in_spec...  1.73 us
    unnamed x2, local copies, waits for them, and re-layouts  0.93 us
  transfers between devices with their start and end apart: 13, of which 11 were waited for; matrix products, arithmetic and copies ran while one was open for 0% of the time, Pallas kernels for 3%

commit v1 on v0

--- a/solution.py
+++ b/solution.py
@@ -223,8 +223,9 @@
     row_blocks[0] = lanes[0] = held
     products = [(rest, every), (soon, every[1:])]
     lines, backs = score("score_late", row_blocks, lanes, products, [(0, count)], lines)
-    ready = lax.optimization_barrier((lanes[-1], row_blocks[1], held, *visitors[:-1]))[0]
-    partner = [swap(lane, 1) for lane in lanes[:-1] + [ready]]
+    partner = [lax.optimization_barrier((held, visitors[0]))[0]]
+    partner += [lax.optimization_barrier((visitor, row_blocks[1]))[0] for visitor in visitors]
+    partner = [swap(lane, 1) for lane in partner]
     products, parts = [(tuple(range(count)), every)], [(0, half), (half, count)]
     theirs, near, far = score("score_partner", row_blocks, partner, products, parts, None, backs)
     lines = jnp.maximum(lines, swap(theirs, 1))

time: 31.1 us -> 29.3 us (0.942)
  waiting for transfers between devices: 11.5 us -> 8.23 us
  starting transfers between devices: 12.9 us -> 14.4 us
    ppermute x4, waiting for transfers between devices: 7.92 us -> 5.9 us  [move(): return lax.ppermute(array, AXES, whole)]
    ppermute x9, waiting for transfers between devices: 3.58 us -> 2.33 us  [swap(): return lax.ppermute(array, AXES, pairs)]
    ppermute x9, starting transfers between devices: 8.06 us -> 8.92 us  [swap(): return lax.ppermute(array, AXES, pairs)]
    ppermute x4, starting transfers between devices: 4.87 us -> 5.44 us  [move(): return lax.ppermute(array, AXES, whole)]
  transfers between devices with their start and end apart: 13 -> 13, of which waited for: 11 -> 8; matrix products, arithmetic and copies ran while one was open for 0% -> 0% of each run, Pallas kernels for 3% -> 3%
where the time goes in v1:
time: 29.3 us; the launch traced here: 29.1 us
  starting transfers between devices  14.4 us (49%)
  waiting for transfers between devices  8.23 us (28%)
  Pallas kernels  5.03 us (17%)
  local copies, waits for them, and re-layouts  0.94 us (3%)
  other arithmetic  0.52 us (2%)
    ppermute x9, starting transfers between devices, swap(): return lax.ppermute(array, AXES, pairs)  8.92 us
    ppermute x4, waiting for transfers between devices, move(): return lax.ppermute(array, AXES, whole)  5.9 us
    ppermute x4, starting transfers between devices, move(): return lax.ppermute(array, AXES, whole)  5.44 us
    pallas_call x1, Pallas kernels, embed(): pl.pallas_call(embed_kernel, in_specs=[HBM] * 5, out_specs=VMEM, out_shap...  3.29 us
    ppermute x9, waiting for transfers between devices, swap(): return lax.ppermute(array, AXES, pairs)  2.33 us
    pallas_call x3, Pallas kernels, score(): pl.pallas_call(lambda *refs: score_kernel(*counts, *rest, *refs), in_spec...  1.74 us
    unnamed x2, local copies, waits for them, and re-layouts  0.93 us
  transfers between devices with their start and end apart: 13, of which 8 were waited for; matrix products, arithmetic and copies ran while one was open for 0% of the time, Pallas kernels for 3%

profile of v1, /device:TPU:0, one launch (start us, length us, event | category | flops | bytes accessed | tf_op | source)
XLA Modules:
  0.0 29.1 jit_solution(12666326478563147414)
XLA Ops:
  0.0 3.3 %embed.1.refs_0_.refs_2_ = bf16[776,128]{1,0:T(8,128)(2,1)} custom-call(bf16[128,2048]{1,0:T(8,128)(2,1)} %states_hbm.1, bf16[2048,768]{1,0:T(8,128)(2,1)} %proj_hbm.1, s32[1,128]{1,0:T(1,128)} %bitcast.5, s32[1,128]{1,0:T(1,128)} %bitcast.6, s32[1,128]{1,0:T(1,128)} %bitcast.7), custom_call_target="tpu_custom_call" | custom-call | tf_op jit(solution)/shard_map/embed/pallas_call | solution.py:62
  3.3 3.0 %collective-permute-start = (bf16[776,128]{1,0:T(8,128)(2,1)}, bf16[776,128]{1,0:T(8,128)(2,1)S(1)}, u32[]{:S(2)}, u32[]{:S(2)}) collective-permute-start(bf16[776,128]{1,0:T(8,128)(2,1)} %embed.1.refs_0_.refs_2_), channel_id=1, source_target_pairs={{0,4},{1,5},{2,6},{3,7},{4,0},{5,1},{6,2},{7,3},{8,12},{9,13},{10,... | collective-permute-start | bytes 595976 | tf_op jit(solution)/shard_map/ppermute | solution.py:198
  6.3 1.6 %collective-permute-start.3 = (bf16[776,128]{1,0:T(8,128)(2,1)}, bf16[776,128]{1,0:T(8,128)(2,1)S(1)}, u32[]{:S(2)}, u32[]{:S(2)}) collective-permute-start(bf16[776,128]{1,0:T(8,128)(2,1)} %embed.1.refs_0_.refs_2_), channel_id=1, source_target_pairs={{0,8},{1,9},{2,10},{3,11},{4,12},{5,13},{6,14},{7,15},{8,16},{9,17... | collective-permute-start | bytes 595976 | tf_op jit(solution)/shard_map/ppermute | solution.py:194
  7.9 1.5 %collective-permute-start.1 = (bf16[776,128]{1,0:T(8,128)(2,1)}, bf16[776,128]{1,0:T(8,128)(2,1)S(1)}, u32[]{:S(2)}, u32[]{:S(2)}) collective-permute-start(bf16[776,128]{1,0:T(8,128)(2,1)} %embed.1.refs_0_.refs_2_), channel_id=1, source_target_pairs={{0,2},{1,3},{2,0},{3,1},{4,6},{5,7},{6,4},{7,5},{8,10},{9,11},{10,... | collective-permute-start | bytes 595976 | tf_op jit(solution)/shard_map/ppermute | solution.py:198
  9.4 1.6 %collective-permute-start.4 = (bf16[776,128]{1,0:T(8,128)(2,1)}, bf16[776,128]{1,0:T(8,128)(2,1)S(1)}, u32[]{:S(2)}, u32[]{:S(2)}) collective-permute-start(bf16[776,128]{1,0:T(8,128)(2,1)} %embed.1.refs_0_.refs_2_), channel_id=1, source_target_pairs={{16,0},{17,1},{18,2},{19,3},{20,4},{21,5},{22,6},{23,7},{8,24},{9,... | collective-permute-start | bytes 595976 | tf_op jit(solution)/shard_map/ppermute | solution.py:194
  11.0 0.5 %collective-permute-done.refs_1_.refs_2_ = bf16[776,128]{1,0:T(8,128)(2,1)S(1)} collective-permute-done((bf16[776,128]{1,0:T(8,128)(2,1)}, bf16[776,128]{1,0:T(8,128)(2,1)S(1)}, u32[]{:S(2)}, u32[]{:S(2)}) %collective-permute-start) | collective-permute-done | bytes 198688 | tf_op jit(solution)/shard_map/ppermute | solution.py:198
  11.5 1.7 %collective-permute-start.2 = (bf16[776,128]{1,0:T(8,128)(2,1)S(1)}, bf16[776,128]{1,0:T(8,128)(2,1)S(1)}, u32[]{:S(2)}, u32[]{:S(2)}) collective-permute-start(bf16[776,128]{1,0:T(8,128)(2,1)S(1)} %collective-permute-done.refs_1_.refs_2_), channel_id=1, source_target_pairs={{0,2},{1,3},{2,0},{3,1},{4,6},{5,7},{6,4},{7,5},{8,10},{9,11},{10,... | collective-permute-start | bytes 595976 | tf_op jit(solution)/shard_map/ppermute | solution.py:198
  13.2 0.9 %copy-done = bf16[776,128]{1,0:T(8,128)(2,1)S(1)} copy-done((bf16[776,128]{1,0:T(8,128)(2,1)S(1)}, bf16[776,128]{1,0:T(8,128)(2,1)}, u32[]{:S(2)}) %copy-start) | copy-done | bytes 198680
  14.1 0.3 %score_soon.1 = (f32[1,128]{1,0:T(1,128)S(1)}, bf16[776,128]{1,0:T(8,128)(2,1)S(1)}) custom-call(bf16[776,128]{1,0:T(8,128)(2,1)S(1)} %copy-done, bf16[776,128]{1,0:T(8,128)(2,1)S(1)} %collective-permute-done.refs_1_.refs_2_, bf16[776,128]{1,0:T(8,128)(2,1)S(1)} %copy-done), custom_call_target="tpu_custom_call" | custom-call | flops 50331648 | bytes 589824 | tf_op jit(solution)/shard_map/score_soon/pallas_call | solution.py:162
  14.5 1.7 %collective-permute-done.3.refs_5_ = bf16[776,128]{1,0:T(8,128)(2,1)S(1)} collective-permute-done((bf16[776,128]{1,0:T(8,128)(2,1)}, bf16[776,128]{1,0:T(8,128)(2,1)S(1)}, u32[]{:S(2)}, u32[]{:S(2)}) %collective-permute-start.3) | collective-permute-done | bytes 198688 | tf_op jit(solution)/shard_map/ppermute | solution.py:194
  16.2 0.5 %collective-permute-start.6 = (bf16[776,128]{1,0:T(8,128)(2,1)S(1)}, bf16[776,128]{1,0:T(8,128)(2,1)S(1)}, u32[]{:S(2)}, u32[]{:S(2)}) collective-permute-start(bf16[776,128]{1,0:T(8,128)(2,1)S(1)} %collective-permute-done.3.refs_5_), channel_id=1, source_target_pairs={{0,1},{1,0},{2,3},{3,2},{4,5},{5,4},{6,7},{7,6},{8,9},{9,8},{10,11... | collective-permute-start | bytes 595976 | tf_op jit(solution)/shard_map/ppermute | solution.py:198
  16.7 2.4 %collective-permute-done.4.refs_6_ = bf16[776,128]{1,0:T(8,128)(2,1)S(1)} collective-permute-done((bf16[776,128]{1,0:T(8,128)(2,1)}, bf16[776,128]{1,0:T(8,128)(2,1)S(1)}, u32[]{:S(2)}, u32[]{:S(2)}) %collective-permute-start.4) | collective-permute-done | bytes 198688 | tf_op jit(solution)/shard_map/ppermute | solution.py:194
  19.1 0.7 %score_late.1 = (f32[3,128]{1,0:T(4,128)S(1)}, f32[4,128]{1,0:T(4,128)S(1)}) custom-call(bf16[776,128]{1,0:T(8,128)(2,1)S(1)} %get-tuple-element.18.refs_0_.refs_4_, bf16[776,128]{1,0:T(8,128)(2,1)S(1)} %collective-permute-done.1.refs_1_, bf16[776,128]{1,0:T(8,128)(2,1)S(1)} %collective-permute-done.refs_1_.refs_2_, ...), custom_call_target="tpu_custom_call" | custom-call | flops 251658240 | bytes 1376256 | tf_op jit(solution)/shard_map/score_late/pallas_call | solution.py:162
  19.8 0.8 %collective-permute-done.7.refs_6_ = bf16[776,128]{1,0:T(8,128)(2,1)S(1)} collective-permute-done((bf16[776,128]{1,0:T(8,128)(2,1)S(1)}, bf16[776,128]{1,0:T(8,128)(2,1)S(1)}, u32[]{:S(2)}, u32[]{:S(2)}) %collective-permute-start.7) | collective-permute-done | bytes 198688 | tf_op jit(solution)/shard_map/ppermute | solution.py:198
  20.5 0.7 %score_partner.1 = (f32[3,128]{1,0:T(4,128)S(1)}, f32[2,128]{1,0:T(2,128)S(1)}, f32[2,128]{1,0:T(2,128)S(1)}) custom-call(bf16[776,128]{1,0:T(8,128)(2,1)S(1)} %get-tuple-element.18.refs_0_.refs_4_, bf16[776,128]{1,0:T(8,128)(2,1)S(1)} %collective-permute-done.1.refs_1_, bf16[776,128]{1,0:T(8,128)(2,1)S(1)} %collective-permute-done.refs_1_.refs_2_, ...), custom_call_target="tpu_custom_call" | custom-call | flops 301989888 | bytes 1376256 | tf_op jit(solution)/shard_map/score_partner/pallas_call | solution.py:162
  21.3 0.2 collective-permute-start.8
  21.5 0.5 %collective-permute-start.11 = (f32[2,128]{1,0:T(2,128)S(1)}, f32[2,128]{1,0:T(2,128)S(1)}, u32[]{:S(2)}, u32[]{:S(2)}) collective-permute-start(f32[2,128]{1,0:T(2,128)S(1)} %get-tuple-element.24), channel_id=1, source_target_pairs={{0,4},{1,5},{2,6},{3,7},{4,0},{5,1},{6,2},{7,3},{8,12},{9,13},{10,... | collective-permute-start | bytes 3080 | tf_op jit(solution)/shard_map/ppermute | solution.py:198
  22.0 0.5 %collective-permute-done.8 = f32[3,128]{1,0:T(4,128)S(1)} collective-permute-done((f32[3,128]{1,0:T(4,128)S(1)}, f32[3,128]{1,0:T(4,128)S(1)}, u32[]{:S(2)}, u32[]{:S(2)}) %collective-permute-start.8) | collective-permute-done | bytes 1568 | tf_op jit(solution)/shard_map/ppermute | solution.py:198
  22.5 2.3 %collective-permute-start.10 = (f32[1,128]{1,0:T(1,128)S(1)}, f32[1,128]{1,0:T(1,128)S(1)}, u32[]{:S(2)}, u32[]{:S(2)}) collective-permute-start(f32[1,128]{1,0:T(1,128)S(1)} %get-tuple-element.26), channel_id=1, source_target_pairs={{8,0},{9,1},{10,2},{11,3},{12,4},{13,5},{14,6},{15,7},{16,8},{17,9... | collective-permute-start | bytes 1544 | tf_op jit(solution)/shard_map/ppermute | solution.py:194
  24.8 0.3 collective-permute-done.11
  25.1 1.5 %collective-permute-start.12 = (f32[1,128]{1,0:T(1,128)S(1)}, f32[1,128]{1,0:T(1,128)S(1)}, u32[]{:S(2)}, u32[]{:S(2)}) collective-permute-start(f32[1,128]{1,0:T(1,128)S(1)} %slice.19), channel_id=1, source_target_pairs={{0,2},{1,3},{2,0},{3,1},{4,6},{5,7},{6,4},{7,5},{8,10},{9,11},{10,... | collective-permute-start | bytes 1544 | tf_op jit(solution)/shard_map/ppermute | solution.py:198
  26.6 1.8 %collective-permute-done.9 = f32[1,128]{1,0:T(1,128)S(1)} collective-permute-done((f32[1,128]{1,0:T(1,128)S(1)}, f32[1,128]{1,0:T(1,128)S(1)}, u32[]{:S(2)}, u32[]{:S(2)}) %collective-permute-start.9) | collective-permute-done | bytes 544 | tf_op jit(solution)/shard_map/ppermute | solution.py:194
  28.3 0.3 collective-permute-done.12
  28.6 0.5 %maximum_bitcast_fusion = f32[128]{0:T(128)} fusion(f32[1,128]{1,0:T(1,128)S(1)} %collective-permute-done.12, f32[1,128]{1,0:T(1,128)S(1)} %maximum_maximum_fusion, f32[2,128]{1,0:T(2,128)S(1)} %max.21), kind=kLoop, calls=%fused_computation | loop fusion | flops 256 | bytes 2048 | tf_op jit(solution)/shard_map/reshape | solution.py:241
  (14 shorter events, 0.0 us)
Async XLA Ops:
  3.3 8.2 %collective-permute-start = (bf16[776,128]{1,0:T(8,128)(2,1)}, bf16[776,128]{1,0:T(8,128)(2,1)S(1)}, u32[]{:S(2)}, u32[]{:S(2)}) collective-permute-start(bf16[776,128]{1,0:T(8,128)(2,1)} %embed.1.refs_0_.refs_2_), channel_id=1, source_target_pairs={{0,4},{1,5},{2,6},{3,7},{4,0},{5,1},{6,2},{7,3},{8,12},{9,13},{10,... | collective-permute-start | bytes 595976 | tf_op jit(solution)/shard_map/ppermute | solution.py:198
  6.3 9.9 %collective-permute-start.3 = (bf16[776,128]{1,0:T(8,128)(2,1)}, bf16[776,128]{1,0:T(8,128)(2,1)S(1)}, u32[]{:S(2)}, u32[]{:S(2)}) collective-permute-start(bf16[776,128]{1,0:T(8,128)(2,1)} %embed.1.refs_0_.refs_2_), channel_id=1, source_target_pairs={{0,8},{1,9},{2,10},{3,11},{4,12},{5,13},{6,14},{7,15},{8,16},{9,17... | collective-permute-start | bytes 595976 | tf_op jit(solution)/shard_map/ppermute | solution.py:194
  7.9 8.3 %collective-permute-start.1 = (bf16[776,128]{1,0:T(8,128)(2,1)}, bf16[776,128]{1,0:T(8,128)(2,1)S(1)}, u32[]{:S(2)}, u32[]{:S(2)}) collective-permute-start(bf16[776,128]{1,0:T(8,128)(2,1)} %embed.1.refs_0_.refs_2_), channel_id=1, source_target_pairs={{0,2},{1,3},{2,0},{3,1},{4,6},{5,7},{6,4},{7,5},{8,10},{9,11},{10,... | collective-permute-start | bytes 595976 | tf_op jit(solution)/shard_map/ppermute | solution.py:198
  9.4 9.7 %collective-permute-start.4 = (bf16[776,128]{1,0:T(8,128)(2,1)}, bf16[776,128]{1,0:T(8,128)(2,1)S(1)}, u32[]{:S(2)}, u32[]{:S(2)}) collective-permute-start(bf16[776,128]{1,0:T(8,128)(2,1)} %embed.1.refs_0_.refs_2_), channel_id=1, source_target_pairs={{16,0},{17,1},{18,2},{19,3},{20,4},{21,5},{22,6},{23,7},{8,24},{9,... | collective-permute-start | bytes 595976 | tf_op jit(solution)/shard_map/ppermute | solution.py:194
  11.5 7.6 %collective-permute-start.2 = (bf16[776,128]{1,0:T(8,128)(2,1)S(1)}, bf16[776,128]{1,0:T(8,128)(2,1)S(1)}, u32[]{:S(2)}, u32[]{:S(2)}) collective-permute-start(bf16[776,128]{1,0:T(8,128)(2,1)S(1)} %collective-permute-done.refs_1_.refs_2_), channel_id=1, source_target_pairs={{0,2},{1,3},{2,0},{3,1},{4,6},{5,7},{6,4},{7,5},{8,10},{9,11},{10,... | collective-permute-start | bytes 595976 | tf_op jit(solution)/shard_map/ppermute | solution.py:198
  13.2 0.9 %copy-start = (bf16[776,128]{1,0:T(8,128)(2,1)S(1)}, bf16[776,128]{1,0:T(8,128)(2,1)}, u32[]{:S(2)}) copy-start(bf16[776,128]{1,0:T(8,128)(2,1)} %embed.1.refs_0_.refs_2_) | copy-start | bytes 595972
  16.2 3.6 %collective-permute-start.5 = (bf16[776,128]{1,0:T(8,128)(2,1)S(1)}, bf16[776,128]{1,0:T(8,128)(2,1)S(1)}, u32[]{:S(2)}, u32[]{:S(2)}) collective-permute-start(bf16[776,128]{1,0:T(8,128)(2,1)S(1)} %get-tuple-element.18.refs_0_.refs_4_), channel_id=1, source_target_pairs={{0,1},{1,0},{2,3},{3,2},{4,5},{5,4},{6,7},{7,6},{8,9},{9,8},{10,11... | collective-permute-start | bytes 595976 | tf_op jit(solution)/shard_map/ppermute | solution.py:198
  16.2 3.6 %collective-permute-start.6 = (bf16[776,128]{1,0:T(8,128)(2,1)S(1)}, bf16[776,128]{1,0:T(8,128)(2,1)S(1)}, u32[]{:S(2)}, u32[]{:S(2)}) collective-permute-start(bf16[776,128]{1,0:T(8,128)(2,1)S(1)} %collective-permute-done.3.refs_5_), channel_id=1, source_target_pairs={{0,1},{1,0},{2,3},{3,2},{4,5},{5,4},{6,7},{7,6},{8,9},{9,8},{10,11... | collective-permute-start | bytes 595976 | tf_op jit(solution)/shard_map/ppermute | solution.py:198
  19.1 1.4 %collective-permute-start.7 = (bf16[776,128]{1,0:T(8,128)(2,1)S(1)}, bf16[776,128]{1,0:T(8,128)(2,1)S(1)}, u32[]{:S(2)}, u32[]{:S(2)}) collective-permute-start(bf16[776,128]{1,0:T(8,128)(2,1)S(1)} %collective-permute-done.4.refs_6_), channel_id=1, source_target_pairs={{0,1},{1,0},{2,3},{3,2},{4,5},{5,4},{6,7},{7,6},{8,9},{9,8},{10,11... | collective-permute-start | bytes 595976 | tf_op jit(solution)/shard_map/ppermute | solution.py:198
  21.3 1.2 %collective-permute-start.8 = (f32[3,128]{1,0:T(4,128)S(1)}, f32[3,128]{1,0:T(4,128)S(1)}, u32[]{:S(2)}, u32[]{:S(2)}) collective-permute-start(f32[3,128]{1,0:T(4,128)S(1)} %get-tuple-element.22), channel_id=1, source_target_pairs={{0,1},{1,0},{2,3},{3,2},{4,5},{5,4},{6,7},{7,6},{8,9},{9,8},{10,11... | collective-permute-start | bytes 4616 | tf_op jit(solution)/shard_map/ppermute | solution.py:198
  21.5 3.6 %collective-permute-start.11 = (f32[2,128]{1,0:T(2,128)S(1)}, f32[2,128]{1,0:T(2,128)S(1)}, u32[]{:S(2)}, u32[]{:S(2)}) collective-permute-start(f32[2,128]{1,0:T(2,128)S(1)} %get-tuple-element.24), channel_id=1, source_target_pairs={{0,4},{1,5},{2,6},{3,7},{4,0},{5,1},{6,2},{7,3},{8,12},{9,13},{10,... | collective-permute-start | bytes 3080 | tf_op jit(solution)/shard_map/ppermute | solution.py:198
  22.5 4.1 %collective-permute-start.10 = (f32[1,128]{1,0:T(1,128)S(1)}, f32[1,128]{1,0:T(1,128)S(1)}, u32[]{:S(2)}, u32[]{:S(2)}) collective-permute-start(f32[1,128]{1,0:T(1,128)S(1)} %get-tuple-element.26), channel_id=1, source_target_pairs={{8,0},{9,1},{10,2},{11,3},{12,4},{13,5},{14,6},{15,7},{16,8},{17,9... | collective-permute-start | bytes 1544 | tf_op jit(solution)/shard_map/ppermute | solution.py:194
  24.8 3.5 %collective-permute-start.9 = (f32[1,128]{1,0:T(1,128)S(1)}, f32[1,128]{1,0:T(1,128)S(1)}, u32[]{:S(2)}, u32[]{:S(2)}) collective-permute-start(f32[1,128]{1,0:T(1,128)S(1)} %get-tuple-element.25), channel_id=1, source_target_pairs={{0,16},{1,17},{2,18},{3,19},{4,20},{5,21},{6,22},{7,23},{24,8},{25... | collective-permute-start | bytes 1544 | tf_op jit(solution)/shard_map/ppermute | solution.py:194
  25.1 3.5 %collective-permute-start.12 = (f32[1,128]{1,0:T(1,128)S(1)}, f32[1,128]{1,0:T(1,128)S(1)}, u32[]{:S(2)}, u32[]{:S(2)}) collective-permute-start(f32[1,128]{1,0:T(1,128)S(1)} %slice.19), channel_id=1, source_target_pairs={{0,2},{1,3},{2,0},{3,1},{4,6},{5,7},{6,4},{7,5},{8,10},{9,11},{10,... | collective-permute-start | bytes 1544 | tf_op jit(solution)/shard_map/ppermute | solution.py:198

commit v2 on v1

--- a/solution.py
+++ b/solution.py
@@ -73,9 +73,9 @@
             pltpu.SemaphoreType.DMA((2, CHUNKS)),
             pltpu.SemaphoreType.DMA((3,)),
         ],
-        compiler_params=pltpu.CompilerParams(vmem_limit_bytes=60 << 20),
+        compiler_params=pltpu.CompilerParams(vmem_limit_bytes=40 << 20),
         name="embed",
-    )(states, projection, owner, sub, prio)
+    )(*(pltpu.with_memory_space_constraint(x, pltpu.HBM) for x in (states, projection, owner, sub, prio)))
 
 
 def read_notes(ref):

time: 29.3 us -> 28.3 us (0.966)
  local copies, waits for them, and re-layouts: 0.94 us -> 0.01 us
  Pallas kernels: 5.03 us -> 4.37 us
  waiting for transfers between devices: 8.23 us -> 8.87 us
    unnamed x2 -> x0, local copies, waits for them, and re-layouts: 0.93 us -> none
    ppermute x4, waiting for transfers between devices: 5.9 us -> 6.79 us  [move(): return lax.ppermute(array, AXES, whole)]
    pallas_call x1, Pallas kernels: 3.29 us -> 2.62 us  [embed(): pl.pallas_call(embed_kernel, in_specs=[HBM] * 5, out_specs=VMEM, out_shap...]
  transfers between devices with their start and end apart: 13 -> 13, of which waited for: 8 -> 8; matrix products, arithmetic and copies ran while one was open for 0% -> 0% of each run, Pallas kernels for 3% -> 4%
where the time goes in v2:
time: 28.3 us; the launch traced here: 28.2 us
  starting transfers between devices  14.4 us (51%)
  waiting for transfers between devices  8.87 us (31%)
  Pallas kernels  4.37 us (15%)
  other arithmetic  0.52 us (2%)
    ppermute x9, starting transfers between devices, swap(): return lax.ppermute(array, AXES, pairs)  8.93 us
    ppermute x4, waiting for transfers between devices, move(): return lax.ppermute(array, AXES, whole)  6.79 us
    ppermute x4, starting transfers between devices, move(): return lax.ppermute(array, AXES, whole)  5.46 us
    pallas_call x1, Pallas kernels, embed(): pl.pallas_call(embed_kernel, in_specs=[HBM] * 5, out_specs=VMEM, out_shap...  2.62 us
    ppermute x9, waiting for transfers between devices, swap(): return lax.ppermute(array, AXES, pairs)  2.08 us
    pallas_call x3, Pallas kernels, score(): pl.pallas_call(lambda *refs: score_kernel(*counts, *rest, *refs), in_spec...  1.75 us
  transfers between devices with their start and end apart: 13, of which 8 were waited for; matrix products, arithmetic and copies ran while one was open for 0% of the time, Pallas kernels for 4%

profile of v2, /device:TPU:0, one launch (start us, length us, event | category | flops | bytes accessed | tf_op | source)
XLA Modules:
  0.0 28.2 jit_solution(15010632721095481927)
XLA Ops:
  0.0 2.6 %embed.1.refs_0_.refs_2_ = bf16[776,128]{1,0:T(8,128)(2,1)S(1)} custom-call(bf16[128,2048]{1,0:T(8,128)(2,1)} %states_hbm.1, bf16[2048,768]{1,0:T(8,128)(2,1)} %proj_hbm.1, s32[1,128]{1,0:T(1,128)} %bitcast.5, s32[1,128]{1,0:T(1,128)} %bitcast.6, s32[1,128]{1,0:T(1,128)} %bitcast.7), custom_call_target="tpu_custom_call" | custom-call | tf_op jit(solution)/shard_map/embed/pallas_call | solution.py:62
  2.6 3.0 %collective-permute-start = (bf16[776,128]{1,0:T(8,128)(2,1)S(1)}, bf16[776,128]{1,0:T(8,128)(2,1)S(1)}, u32[]{:S(2)}, u32[]{:S(2)}) collective-permute-start(bf16[776,128]{1,0:T(8,128)(2,1)S(1)} %embed.1.refs_0_.refs_2_), channel_id=1, source_target_pairs={{0,4},{1,5},{2,6},{3,7},{4,0},{5,1},{6,2},{7,3},{8,12},{9,13},{10,... | collective-permute-start | bytes 595976 | tf_op jit(solution)/shard_map/ppermute | solution.py:198
  5.7 1.6 %collective-permute-start.3 = (bf16[776,128]{1,0:T(8,128)(2,1)S(1)}, bf16[776,128]{1,0:T(8,128)(2,1)S(1)}, u32[]{:S(2)}, u32[]{:S(2)}) collective-permute-start(bf16[776,128]{1,0:T(8,128)(2,1)S(1)} %embed.1.refs_0_.refs_2_), channel_id=1, source_target_pairs={{0,8},{1,9},{2,10},{3,11},{4,12},{5,13},{6,14},{7,15},{8,16},{9,17... | collective-permute-start | bytes 595976 | tf_op jit(solution)/shard_map/ppermute | solution.py:194
  7.2 1.5 %collective-permute-start.1 = (bf16[776,128]{1,0:T(8,128)(2,1)S(1)}, bf16[776,128]{1,0:T(8,128)(2,1)S(1)}, u32[]{:S(2)}, u32[]{:S(2)}) collective-permute-start(bf16[776,128]{1,0:T(8,128)(2,1)S(1)} %embed.1.refs_0_.refs_2_), channel_id=1, source_target_pairs={{0,2},{1,3},{2,0},{3,1},{4,6},{5,7},{6,4},{7,5},{8,10},{9,11},{10,... | collective-permute-start | bytes 595976 | tf_op jit(solution)/shard_map/ppermute | solution.py:198
  8.7 1.6 %collective-permute-start.4 = (bf16[776,128]{1,0:T(8,128)(2,1)S(1)}, bf16[776,128]{1,0:T(8,128)(2,1)S(1)}, u32[]{:S(2)}, u32[]{:S(2)}) collective-permute-start(bf16[776,128]{1,0:T(8,128)(2,1)S(1)} %embed.1.refs_0_.refs_2_), channel_id=1, source_target_pairs={{16,0},{17,1},{18,2},{19,3},{20,4},{21,5},{22,6},{23,7},{8,24},{9,... | collective-permute-start | bytes 595976 | tf_op jit(solution)/shard_map/ppermute | solution.py:194
  10.3 0.3 %collective-permute-done.refs_1_.refs_2_ = bf16[776,128]{1,0:T(8,128)(2,1)S(1)} collective-permute-done((bf16[776,128]{1,0:T(8,128)(2,1)S(1)}, bf16[776,128]{1,0:T(8,128)(2,1)S(1)}, u32[]{:S(2)}, u32[]{:S(2)}) %collective-permute-start) | collective-permute-done | bytes 198688 | tf_op jit(solution)/shard_map/ppermute | solution.py:198
  10.6 1.7 %collective-permute-start.2 = (bf16[776,128]{1,0:T(8,128)(2,1)S(1)}, bf16[776,128]{1,0:T(8,128)(2,1)S(1)}, u32[]{:S(2)}, u32[]{:S(2)}) collective-permute-start(bf16[776,128]{1,0:T(8,128)(2,1)S(1)} %collective-permute-done.refs_1_.refs_2_), channel_id=1, source_target_pairs={{0,2},{1,3},{2,0},{3,1},{4,6},{5,7},{6,4},{7,5},{8,10},{9,11},{10,... | collective-permute-start | bytes 595976 | tf_op jit(solution)/shard_map/ppermute | solution.py:198
  12.3 0.3 %score_soon.1 = (f32[1,128]{1,0:T(1,128)S(1)}, bf16[776,128]{1,0:T(8,128)(2,1)S(1)}) custom-call(bf16[776,128]{1,0:T(8,128)(2,1)S(1)} %embed.1.refs_0_.refs_2_, bf16[776,128]{1,0:T(8,128)(2,1)S(1)} %collective-permute-done.refs_1_.refs_2_, bf16[776,128]{1,0:T(8,128)(2,1)S(1)} %embed.1.refs_0_.refs_2_), custom_call_target="tpu_custom_call" | custom-call | flops 50331648 | bytes 589824 | tf_op jit(solution)/shard_map/score_soon/pallas_call | solution.py:162
  12.7 2.7 %collective-permute-done.3.refs_5_ = bf16[776,128]{1,0:T(8,128)(2,1)S(1)} collective-permute-done((bf16[776,128]{1,0:T(8,128)(2,1)S(1)}, bf16[776,128]{1,0:T(8,128)(2,1)S(1)}, u32[]{:S(2)}, u32[]{:S(2)}) %collective-permute-start.3) | collective-permute-done | bytes 198688 | tf_op jit(solution)/shard_map/ppermute | solution.py:194
  15.3 0.5 %collective-permute-start.6 = (bf16[776,128]{1,0:T(8,128)(2,1)S(1)}, bf16[776,128]{1,0:T(8,128)(2,1)S(1)}, u32[]{:S(2)}, u32[]{:S(2)}) collective-permute-start(bf16[776,128]{1,0:T(8,128)(2,1)S(1)} %collective-permute-done.3.refs_5_), channel_id=1, source_target_pairs={{0,1},{1,0},{2,3},{3,2},{4,5},{5,4},{6,7},{7,6},{8,9},{9,8},{10,11... | collective-permute-start | bytes 595976 | tf_op jit(solution)/shard_map/ppermute | solution.py:198
  15.8 2.3 %collective-permute-done.4.refs_6_ = bf16[776,128]{1,0:T(8,128)(2,1)S(1)} collective-permute-done((bf16[776,128]{1,0:T(8,128)(2,1)S(1)}, bf16[776,128]{1,0:T(8,128)(2,1)S(1)}, u32[]{:S(2)}, u32[]{:S(2)}) %collective-permute-start.4) | collective-permute-done | bytes 198688 | tf_op jit(solution)/shard_map/ppermute | solution.py:194
  18.2 0.0 collective-permute-start.7
  18.2 0.7 %score_late.1 = (f32[3,128]{1,0:T(4,128)S(1)}, f32[4,128]{1,0:T(4,128)S(1)}) custom-call(bf16[776,128]{1,0:T(8,128)(2,1)S(1)} %get-tuple-element.18.refs_0_.refs_4_, bf16[776,128]{1,0:T(8,128)(2,1)S(1)} %collective-permute-done.1.refs_1_, bf16[776,128]{1,0:T(8,128)(2,1)S(1)} %collective-permute-done.refs_1_.refs_2_, ...), custom_call_target="tpu_custom_call" | custom-call | flops 251658240 | bytes 1376256 | tf_op jit(solution)/shard_map/score_late/pallas_call | solution.py:162
  18.9 0.8 %collective-permute-done.7.refs_6_ = bf16[776,128]{1,0:T(8,128)(2,1)S(1)} collective-permute-done((bf16[776,128]{1,0:T(8,128)(2,1)S(1)}, bf16[776,128]{1,0:T(8,128)(2,1)S(1)}, u32[]{:S(2)}, u32[]{:S(2)}) %collective-permute-start.7) | collective-permute-done | bytes 198688 | tf_op jit(solution)/shard_map/ppermute | solution.py:198
  19.6 0.8 %score_partner.1 = (f32[3,128]{1,0:T(4,128)S(1)}, f32[2,128]{1,0:T(2,128)S(1)}, f32[2,128]{1,0:T(2,128)S(1)}) custom-call(bf16[776,128]{1,0:T(8,128)(2,1)S(1)} %get-tuple-element.18.refs_0_.refs_4_, bf16[776,128]{1,0:T(8,128)(2,1)S(1)} %collective-permute-done.1.refs_1_, bf16[776,128]{1,0:T(8,128)(2,1)S(1)} %collective-permute-done.refs_1_.refs_2_, ...), custom_call_target="tpu_custom_call" | custom-call | flops 301989888 | bytes 1376256 | tf_op jit(solution)/shard_map/score_partner/pallas_call | solution.py:162
  20.4 0.2 collective-permute-start.8
  20.6 0.5 %collective-permute-start.11 = (f32[2,128]{1,0:T(2,128)S(1)}, f32[2,128]{1,0:T(2,128)S(1)}, u32[]{:S(2)}, u32[]{:S(2)}) collective-permute-start(f32[2,128]{1,0:T(2,128)S(1)} %get-tuple-element.24), channel_id=1, source_target_pairs={{0,4},{1,5},{2,6},{3,7},{4,0},{5,1},{6,2},{7,3},{8,12},{9,13},{10,... | collective-permute-start | bytes 3080 | tf_op jit(solution)/shard_map/ppermute | solution.py:198
  21.1 0.5 %collective-permute-done.8 = f32[3,128]{1,0:T(4,128)S(1)} collective-permute-done((f32[3,128]{1,0:T(4,128)S(1)}, f32[3,128]{1,0:T(4,128)S(1)}, u32[]{:S(2)}, u32[]{:S(2)}) %collective-permute-start.8) | collective-permute-done | bytes 1568 | tf_op jit(solution)/shard_map/ppermute | solution.py:198
  21.6 2.3 %collective-permute-start.10 = (f32[1,128]{1,0:T(1,128)S(1)}, f32[1,128]{1,0:T(1,128)S(1)}, u32[]{:S(2)}, u32[]{:S(2)}) collective-permute-start(f32[1,128]{1,0:T(1,128)S(1)} %get-tuple-element.26), channel_id=1, source_target_pairs={{8,0},{9,1},{10,2},{11,3},{12,4},{13,5},{14,6},{15,7},{16,8},{17,9... | collective-permute-start | bytes 1544 | tf_op jit(solution)/shard_map/ppermute | solution.py:194
  23.9 0.2 collective-permute-done.11
  24.1 1.5 %collective-permute-start.12 = (f32[1,128]{1,0:T(1,128)S(1)}, f32[1,128]{1,0:T(1,128)S(1)}, u32[]{:S(2)}, u32[]{:S(2)}) collective-permute-start(f32[1,128]{1,0:T(1,128)S(1)} %slice.19), channel_id=1, source_target_pairs={{0,2},{1,3},{2,0},{3,1},{4,6},{5,7},{6,4},{7,5},{8,10},{9,11},{10,... | collective-permute-start | bytes 1544 | tf_op jit(solution)/shard_map/ppermute | solution.py:198
  25.6 1.8 %collective-permute-done.9 = f32[1,128]{1,0:T(1,128)S(1)} collective-permute-done((f32[1,128]{1,0:T(1,128)S(1)}, f32[1,128]{1,0:T(1,128)S(1)}, u32[]{:S(2)}, u32[]{:S(2)}) %collective-permute-start.9) | collective-permute-done | bytes 544 | tf_op jit(solution)/shard_map/ppermute | solution.py:194
  27.4 0.3 collective-permute-done.12
  27.7 0.5 %maximum_bitcast_fusion = f32[128]{0:T(128)} fusion(f32[1,128]{1,0:T(1,128)S(1)} %collective-permute-done.12, f32[1,128]{1,0:T(1,128)S(1)} %maximum_maximum_fusion, f32[2,128]{1,0:T(2,128)S(1)} %max.21), kind=kLoop, calls=%fused_computation | loop fusion | flops 256 | bytes 2048 | tf_op jit(solution)/shard_map/reshape | solution.py:241
  (12 shorter events, 0.0 us)
Async XLA Ops:
  2.6 8.0 %collective-permute-start = (bf16[776,128]{1,0:T(8,128)(2,1)S(1)}, bf16[776,128]{1,0:T(8,128)(2,1)S(1)}, u32[]{:S(2)}, u32[]{:S(2)}) collective-permute-start(bf16[776,128]{1,0:T(8,128)(2,1)S(1)} %embed.1.refs_0_.refs_2_), channel_id=1, source_target_pairs={{0,4},{1,5},{2,6},{3,7},{4,0},{5,1},{6,2},{7,3},{8,12},{9,13},{10,... | collective-permute-start | bytes 595976 | tf_op jit(solution)/shard_map/ppermute | solution.py:198
  5.7 9.7 %collective-permute-start.3 = (bf16[776,128]{1,0:T(8,128)(2,1)S(1)}, bf16[776,128]{1,0:T(8,128)(2,1)S(1)}, u32[]{:S(2)}, u32[]{:S(2)}) collective-permute-start(bf16[776,128]{1,0:T(8,128)(2,1)S(1)} %embed.1.refs_0_.refs_2_), channel_id=1, source_target_pairs={{0,8},{1,9},{2,10},{3,11},{4,12},{5,13},{6,14},{7,15},{8,16},{9,17... | collective-permute-start | bytes 595976 | tf_op jit(solution)/shard_map/ppermute | solution.py:194
  7.2 8.1 %collective-permute-start.1 = (bf16[776,128]{1,0:T(8,128)(2,1)S(1)}, bf16[776,128]{1,0:T(8,128)(2,1)S(1)}, u32[]{:S(2)}, u32[]{:S(2)}) collective-permute-start(bf16[776,128]{1,0:T(8,128)(2,1)S(1)} %embed.1.refs_0_.refs_2_), channel_id=1, source_target_pairs={{0,2},{1,3},{2,0},{3,1},{4,6},{5,7},{6,4},{7,5},{8,10},{9,11},{10,... | collective-permute-start | bytes 595976 | tf_op jit(solution)/shard_map/ppermute | solution.py:198
  8.7 9.4 %collective-permute-start.4 = (bf16[776,128]{1,0:T(8,128)(2,1)S(1)}, bf16[776,128]{1,0:T(8,128)(2,1)S(1)}, u32[]{:S(2)}, u32[]{:S(2)}) collective-permute-start(bf16[776,128]{1,0:T(8,128)(2,1)S(1)} %embed.1.refs_0_.refs_2_), channel_id=1, source_target_pairs={{16,0},{17,1},{18,2},{19,3},{20,4},{21,5},{22,6},{23,7},{8,24},{9,... | collective-permute-start | bytes 595976 | tf_op jit(solution)/shard_map/ppermute | solution.py:194
  10.6 7.6 %collective-permute-start.2 = (bf16[776,128]{1,0:T(8,128)(2,1)S(1)}, bf16[776,128]{1,0:T(8,128)(2,1)S(1)}, u32[]{:S(2)}, u32[]{:S(2)}) collective-permute-start(bf16[776,128]{1,0:T(8,128)(2,1)S(1)} %collective-permute-done.refs_1_.refs_2_), channel_id=1, source_target_pairs={{0,2},{1,3},{2,0},{3,1},{4,6},{5,7},{6,4},{7,5},{8,10},{9,11},{10,... | collective-permute-start | bytes 595976 | tf_op jit(solution)/shard_map/ppermute | solution.py:198
  15.3 3.5 %collective-permute-start.5 = (bf16[776,128]{1,0:T(8,128)(2,1)S(1)}, bf16[776,128]{1,0:T(8,128)(2,1)S(1)}, u32[]{:S(2)}, u32[]{:S(2)}) collective-permute-start(bf16[776,128]{1,0:T(8,128)(2,1)S(1)} %get-tuple-element.18.refs_0_.refs_4_), channel_id=1, source_target_pairs={{0,1},{1,0},{2,3},{3,2},{4,5},{5,4},{6,7},{7,6},{8,9},{9,8},{10,11... | collective-permute-start | bytes 595976 | tf_op jit(solution)/shard_map/ppermute | solution.py:198
  15.3 3.5 %collective-permute-start.6 = (bf16[776,128]{1,0:T(8,128)(2,1)S(1)}, bf16[776,128]{1,0:T(8,128)(2,1)S(1)}, u32[]{:S(2)}, u32[]{:S(2)}) collective-permute-start(bf16[776,128]{1,0:T(8,128)(2,1)S(1)} %collective-permute-done.3.refs_5_), channel_id=1, source_target_pairs={{0,1},{1,0},{2,3},{3,2},{4,5},{5,4},{6,7},{7,6},{8,9},{9,8},{10,11... | collective-permute-start | bytes 595976 | tf_op jit(solution)/shard_map/ppermute | solution.py:198
  18.2 1.4 %collective-permute-start.7 = (bf16[776,128]{1,0:T(8,128)(2,1)S(1)}, bf16[776,128]{1,0:T(8,128)(2,1)S(1)}, u32[]{:S(2)}, u32[]{:S(2)}) collective-permute-start(bf16[776,128]{1,0:T(8,128)(2,1)S(1)} %collective-permute-done.4.refs_6_), channel_id=1, source_target_pairs={{0,1},{1,0},{2,3},{3,2},{4,5},{5,4},{6,7},{7,6},{8,9},{9,8},{10,11... | collective-permute-start | bytes 595976 | tf_op jit(solution)/shard_map/ppermute | solution.py:198
  20.4 1.2 %collective-permute-start.8 = (f32[3,128]{1,0:T(4,128)S(1)}, f32[3,128]{1,0:T(4,128)S(1)}, u32[]{:S(2)}, u32[]{:S(2)}) collective-permute-start(f32[3,128]{1,0:T(4,128)S(1)} %get-tuple-element.22), channel_id=1, source_target_pairs={{0,1},{1,0},{2,3},{3,2},{4,5},{5,4},{6,7},{7,6},{8,9},{9,8},{10,11... | collective-permute-start | bytes 4616 | tf_op jit(solution)/shard_map/ppermute | solution.py:198
  20.6 3.6 %collective-permute-start.11 = (f32[2,128]{1,0:T(2,128)S(1)}, f32[2,128]{1,0:T(2,128)S(1)}, u32[]{:S(2)}, u32[]{:S(2)}) collective-permute-start(f32[2,128]{1,0:T(2,128)S(1)} %get-tuple-element.24), channel_id=1, source_target_pairs={{0,4},{1,5},{2,6},{3,7},{4,0},{5,1},{6,2},{7,3},{8,12},{9,13},{10,... | collective-permute-start | bytes 3080 | tf_op jit(solution)/shard_map/ppermute | solution.py:198
  21.6 4.1 %collective-permute-start.10 = (f32[1,128]{1,0:T(1,128)S(1)}, f32[1,128]{1,0:T(1,128)S(1)}, u32[]{:S(2)}, u32[]{:S(2)}) collective-permute-start(f32[1,128]{1,0:T(1,128)S(1)} %get-tuple-element.26), channel_id=1, source_target_pairs={{8,0},{9,1},{10,2},{11,3},{12,4},{13,5},{14,6},{15,7},{16,8},{17,9... | collective-permute-start | bytes 1544 | tf_op jit(solution)/shard_map/ppermute | solution.py:194
  23.9 3.5 %collective-permute-start.9 = (f32[1,128]{1,0:T(1,128)S(1)}, f32[1,128]{1,0:T(1,128)S(1)}, u32[]{:S(2)}, u32[]{:S(2)}) collective-permute-start(f32[1,128]{1,0:T(1,128)S(1)} %get-tuple-element.25), channel_id=1, source_target_pairs={{0,16},{1,17},{2,18},{3,19},{4,20},{5,21},{6,22},{7,23},{24,8},{25... | collective-permute-start | bytes 1544 | tf_op jit(solution)/shard_map/ppermute | solution.py:194
  24.1 3.5 %collective-permute-start.12 = (f32[1,128]{1,0:T(1,128)S(1)}, f32[1,128]{1,0:T(1,128)S(1)}, u32[]{:S(2)}, u32[]{:S(2)}) collective-permute-start(f32[1,128]{1,0:T(1,128)S(1)} %slice.19), channel_id=1, source_target_pairs={{0,2},{1,3},{2,0},{3,1},{4,6},{5,7},{6,4},{7,5},{8,10},{9,11},{10,... | collective-permute-start | bytes 1544 | tf_op jit(solution)/shard_map/ppermute | solution.py:198

commit v3 on v2

--- a/solution.py
+++ b/solution.py
@@ -93,7 +93,7 @@
     )
 
 
-def score_kernel(row_count, lane_count, products, parts, has_lines, seen_rows, hold, *refs):
+def score_kernel(row_count, lane_count, products, parts, has_lines, seen_rows, hold, home, *refs):
     refs = list(refs)
     row_refs = [refs.pop(0) for _ in range(row_count)]
     lane_refs = [refs.pop(0) for _ in range(lane_count)]
@@ -128,7 +128,7 @@
                 same = jnp.where(row_cluster == lane_cluster, here, -1.0)
                 earlier = row_prio < lane_prio
                 best[j] = top(best[j], jnp.where(earlier, same, -1.0))
-                if j > 0:
+                if j >= home:
                     back[i] = top(back[i], jnp.where(earlier, -1.0, same))
     lane_ids = lax.broadcasted_iota(jnp.int32, (rows, rows), 1)
     table = jnp.full((rows, rows), -1.0, jnp.float32)
@@ -148,7 +148,7 @@
     lines_out[...] = lines
 
 
-def score(name, row_blocks, lane_blocks, products, parts, lines=None, backs=None, hold=False):
+def score(name, row_blocks, lane_blocks, products, parts, lines=None, backs=None, hold=False, home=1):
     high, rows = row_blocks[0].shape
     width = high - NOTE_ROWS
     inputs = [*row_blocks, *lane_blocks, *(seen for seen in (lines, backs) if seen is not None)]
@@ -157,7 +157,7 @@
     if hold:
         outs.append(jax.ShapeDtypeStruct((high, rows), row_blocks[0].dtype))
     counts = len(row_blocks), len(lane_blocks)
-    rest = products, parts, lines is not None, backs is not None, hold
+    rest = products, parts, lines is not None, backs is not None, hold, home
     macs = sum(len(r) * len(c) for r, c in products) * rows * rows * width
     return pl.pallas_call(
         lambda *refs: score_kernel(*counts, *rest, *refs),
@@ -223,20 +223,28 @@
     row_blocks[0] = lanes[0] = held
     products = [(rest, every), (soon, every[1:])]
     lines, backs = score("score_late", row_blocks, lanes, products, [(0, count)], lines)
-    partner = [lax.optimization_barrier((held, visitors[0]))[0]]
-    partner += [lax.optimization_barrier((visitor, row_blocks[1]))[0] for visitor in visitors]
+    partner = [held]
+    partner += [visitor for visitor in visitors[:-1]]
+    partner += [lax.optimization_barrier((visitors[-1], row_blocks[1]))[0]]
     partner = [swap(lane, 1) for lane in partner]
-    products, parts = [(tuple(range(count)), every)], [(0, half), (half, count)]
-    theirs, near, far = score("score_partner", row_blocks, partner, products, parts, None, backs)
-    lines = jnp.maximum(lines, swap(theirs, 1))
+    theirs, backs = score(
+        "score_partner", row_blocks, partner[:-1], [(tuple(range(count)), every[:-1])], [(0, count)], None, backs
+    )
+    parts = [(0, half), (half, count)]
+    last, near, far = score(
+        "score_last", row_blocks, partner[-1:], [(tuple(range(count)), (0,))], parts, None, backs, home=0
+    )
+    first = jnp.maximum(lines[:-1], swap(theirs, 1))
+    last = lax.optimization_barrier((swap(last, 1), first))[0]
+    lines = [first[i:i + 1] for i in every[:-1]] + [jnp.maximum(lines[-1:], last)]
     for bit in bits[:0:-1]:
         near = jnp.maximum(near, swap(far, bit))
         half = near.shape[0] // 2
         near, far = near[:half], near[half:]
-    total = lines[:1]
-    for i, pairs in reversed(list(enumerate(moves))):
-        total = jnp.maximum(total, move(lines[i + 1:i + 2], [(b, a) for a, b in pairs]))
-    total = lax.optimization_barrier(total)
+    total = lines[0]
+    for i, pairs in enumerate(moves):
+        home = move(lines[i + 1], [(b, a) for a, b in pairs])
+        total = lax.optimization_barrier(jnp.maximum(total, home))
     total = jnp.maximum(jnp.maximum(total, near), swap(far, bits[0]))
     return total.reshape(rows)
 

time: 28.3 us -> 28.5 us (level)
  waiting for transfers between devices: 8.87 us -> 8.31 us
  Pallas kernels: 4.37 us -> 4.7 us
  starting transfers between devices: 14.4 us -> 14.7 us
    ppermute x9 -> x10, waiting for transfers between devices: 2.08 us -> 0.93 us  [swap(): return lax.ppermute(array, AXES, pairs)]
    ppermute x4, waiting for transfers between devices: 6.79 us -> 7.37 us  [move(): return lax.ppermute(array, AXES, whole)]
    pallas_call x3 -> x4, Pallas kernels: 1.75 us -> 2.08 us  [score(): pl.pallas_call(lambda *refs: score_kernel(*counts, *rest, *refs), in_spec...]
    ppermute x9 -> x10, starting transfers between devices: 8.93 us -> 9.04 us  [swap(): return lax.ppermute(array, AXES, pairs)]
  transfers between devices with their start and end apart: 13 -> 14, of which waited for: 8 -> 6; matrix products, arithmetic and copies ran while one was open for 0% -> 0% of each run, Pallas kernels for 4% -> 7%
where the time goes in v3:
time: 28.5 us; the launch traced here: 28.3 us
  starting transfers between devices  14.7 us (52%)
  waiting for transfers between devices  8.31 us (29%)
  Pallas kernels  4.7 us (16%)
  other arithmetic  0.53 us (2%)
    ppermute x10, starting transfers between devices, swap(): return lax.ppermute(array, AXES, pairs)  9.04 us
    ppermute x4, waiting for transfers between devices, move(): return lax.ppermute(array, AXES, whole)  7.37 us
    ppermute x4, starting transfers between devices, move(): return lax.ppermute(array, AXES, whole)  5.68 us
    pallas_call x1, Pallas kernels, embed(): pl.pallas_call(embed_kernel, in_specs=[HBM] * 5, out_specs=VMEM, out_shap...  2.62 us
    pallas_call x4, Pallas kernels, score(): pl.pallas_call(lambda *refs: score_kernel(*counts, *rest, *refs), in_spec...  2.08 us
    ppermute x10, waiting for transfers between devices, swap(): return lax.ppermute(array, AXES, pairs)  0.93 us
  transfers between devices with their start and end apart: 14, of which 6 were waited for; matrix products, arithmetic and copies ran while one was open for 0% of the time, Pallas kernels for 7%

profile of v3, /device:TPU:0, one launch (start us, length us, event | category | flops | bytes accessed | tf_op | source)
XLA Modules:
  0.0 28.3 jit_solution(10965447775425427964)
XLA Ops:
  0.0 2.6 %embed.1.refs_0_.refs_2_ = bf16[776,128]{1,0:T(8,128)(2,1)S(1)} custom-call(bf16[128,2048]{1,0:T(8,128)(2,1)} %states_hbm.1, bf16[2048,768]{1,0:T(8,128)(2,1)} %proj_hbm.1, s32[1,128]{1,0:T(1,128)} %bitcast.5, s32[1,128]{1,0:T(1,128)} %bitcast.6, s32[1,128]{1,0:T(1,128)} %bitcast.7), custom_call_target="tpu_custom_call" | custom-call | tf_op jit(solution)/shard_map/embed/pallas_call | solution.py:62
  2.6 3.0 %collective-permute-start = (bf16[776,128]{1,0:T(8,128)(2,1)S(1)}, bf16[776,128]{1,0:T(8,128)(2,1)S(1)}, u32[]{:S(2)}, u32[]{:S(2)}) collective-permute-start(bf16[776,128]{1,0:T(8,128)(2,1)S(1)} %embed.1.refs_0_.refs_2_), channel_id=1, source_target_pairs={{0,4},{1,5},{2,6},{3,7},{4,0},{5,1},{6,2},{7,3},{8,12},{9,13},{10,... | collective-permute-start | bytes 595976 | tf_op jit(solution)/shard_map/ppermute | solution.py:198
  5.7 1.6 %collective-permute-start.3 = (bf16[776,128]{1,0:T(8,128)(2,1)S(1)}, bf16[776,128]{1,0:T(8,128)(2,1)S(1)}, u32[]{:S(2)}, u32[]{:S(2)}) collective-permute-start(bf16[776,128]{1,0:T(8,128)(2,1)S(1)} %embed.1.refs_0_.refs_2_), channel_id=1, source_target_pairs={{0,8},{1,9},{2,10},{3,11},{4,12},{5,13},{6,14},{7,15},{8,16},{9,17... | collective-permute-start | bytes 595976 | tf_op jit(solution)/shard_map/ppermute | solution.py:194
  7.2 1.5 %collective-permute-start.1 = (bf16[776,128]{1,0:T(8,128)(2,1)S(1)}, bf16[776,128]{1,0:T(8,128)(2,1)S(1)}, u32[]{:S(2)}, u32[]{:S(2)}) collective-permute-start(bf16[776,128]{1,0:T(8,128)(2,1)S(1)} %embed.1.refs_0_.refs_2_), channel_id=1, source_target_pairs={{0,2},{1,3},{2,0},{3,1},{4,6},{5,7},{6,4},{7,5},{8,10},{9,11},{10,... | collective-permute-start | bytes 595976 | tf_op jit(solution)/shard_map/ppermute | solution.py:198
  8.7 1.6 %collective-permute-start.4 = (bf16[776,128]{1,0:T(8,128)(2,1)S(1)}, bf16[776,128]{1,0:T(8,128)(2,1)S(1)}, u32[]{:S(2)}, u32[]{:S(2)}) collective-permute-start(bf16[776,128]{1,0:T(8,128)(2,1)S(1)} %embed.1.refs_0_.refs_2_), channel_id=1, source_target_pairs={{16,0},{17,1},{18,2},{19,3},{20,4},{21,5},{22,6},{23,7},{8,24},{9,... | collective-permute-start | bytes 595976 | tf_op jit(solution)/shard_map/ppermute | solution.py:194
  10.3 0.3 %collective-permute-done.refs_1_.refs_2_ = bf16[776,128]{1,0:T(8,128)(2,1)S(1)} collective-permute-done((bf16[776,128]{1,0:T(8,128)(2,1)S(1)}, bf16[776,128]{1,0:T(8,128)(2,1)S(1)}, u32[]{:S(2)}, u32[]{:S(2)}) %collective-permute-start) | collective-permute-done | bytes 198688 | tf_op jit(solution)/shard_map/ppermute | solution.py:198
  10.6 1.7 %collective-permute-start.2 = (bf16[776,128]{1,0:T(8,128)(2,1)S(1)}, bf16[776,128]{1,0:T(8,128)(2,1)S(1)}, u32[]{:S(2)}, u32[]{:S(2)}) collective-permute-start(bf16[776,128]{1,0:T(8,128)(2,1)S(1)} %collective-permute-done.refs_1_.refs_2_), channel_id=1, source_target_pairs={{0,2},{1,3},{2,0},{3,1},{4,6},{5,7},{6,4},{7,5},{8,10},{9,11},{10,... | collective-permute-start | bytes 595976 | tf_op jit(solution)/shard_map/ppermute | solution.py:198
  12.3 0.3 %score_soon.1 = (f32[1,128]{1,0:T(1,128)S(1)}, bf16[776,128]{1,0:T(8,128)(2,1)S(1)}) custom-call(bf16[776,128]{1,0:T(8,128)(2,1)S(1)} %embed.1.refs_0_.refs_2_, bf16[776,128]{1,0:T(8,128)(2,1)S(1)} %collective-permute-done.refs_1_.refs_2_, bf16[776,128]{1,0:T(8,128)(2,1)S(1)} %embed.1.refs_0_.refs_2_), custom_call_target="tpu_custom_call" | custom-call | flops 50331648 | bytes 589824 | tf_op jit(solution)/shard_map/score_soon/pallas_call | solution.py:162
  12.7 0.1 collective-permute-start.5
  12.7 2.6 %collective-permute-done.3.refs_5_ = bf16[776,128]{1,0:T(8,128)(2,1)S(1)} collective-permute-done((bf16[776,128]{1,0:T(8,128)(2,1)S(1)}, bf16[776,128]{1,0:T(8,128)(2,1)S(1)}, u32[]{:S(2)}, u32[]{:S(2)}) %collective-permute-start.3) | collective-permute-done | bytes 198688 | tf_op jit(solution)/shard_map/ppermute | solution.py:194
  15.3 2.8 %collective-permute-done.4.refs_6_ = bf16[776,128]{1,0:T(8,128)(2,1)S(1)} collective-permute-done((bf16[776,128]{1,0:T(8,128)(2,1)S(1)}, bf16[776,128]{1,0:T(8,128)(2,1)S(1)}, u32[]{:S(2)}, u32[]{:S(2)}) %collective-permute-start.4) | collective-permute-done | bytes 198688 | tf_op jit(solution)/shard_map/ppermute | solution.py:194
  18.2 0.0 collective-permute-start.9
  18.2 0.7 %score_late.1 = (f32[3,128]{1,0:T(4,128)S(1)}, f32[4,128]{1,0:T(4,128)S(1)}) custom-call(bf16[776,128]{1,0:T(8,128)(2,1)S(1)} %get-tuple-element.16.refs_0_.refs_4_, bf16[776,128]{1,0:T(8,128)(2,1)S(1)} %collective-permute-done.1.refs_1_, bf16[776,128]{1,0:T(8,128)(2,1)S(1)} %collective-permute-done.refs_1_.refs_2_, ...), custom_call_target="tpu_custom_call" | custom-call | flops 251658240 | bytes 1376256 | tf_op jit(solution)/shard_map/score_late/pallas_call | solution.py:162
  18.9 0.6 %score_partner.1 = (f32[2,128]{1,0:T(2,128)S(1)}, f32[4,128]{1,0:T(4,128)S(1)}) custom-call(bf16[776,128]{1,0:T(8,128)(2,1)S(1)} %get-tuple-element.16.refs_0_.refs_4_, bf16[776,128]{1,0:T(8,128)(2,1)S(1)} %collective-permute-done.1.refs_1_, bf16[776,128]{1,0:T(8,128)(2,1)S(1)} %collective-permute-done.refs_1_.refs_2_, ...), custom_call_target="tpu_custom_call" | custom-call | flops 201326592 | bytes 1179648 | tf_op jit(solution)/shard_map/score_partner/pallas_call | solution.py:162
  19.4 0.5 %collective-permute-start.7 = (f32[2,128]{1,0:T(2,128)S(1)}, f32[2,128]{1,0:T(2,128)S(1)}, u32[]{:S(2)}, u32[]{:S(2)}) collective-permute-start(f32[2,128]{1,0:T(2,128)S(1)} %get-tuple-element.20), channel_id=1, source_target_pairs={{0,1},{1,0},{2,3},{3,2},{4,5},{5,4},{6,7},{7,6},{8,9},{9,8},{10,11... | collective-permute-start | bytes 3080 | tf_op jit(solution)/shard_map/ppermute | solution.py:198
  20.0 0.5 %score_last.1 = (f32[1,128]{1,0:T(1,128)S(1)}, f32[2,128]{1,0:T(2,128)S(1)}, f32[2,128]{1,0:T(2,128)S(1)}) custom-call(bf16[776,128]{1,0:T(8,128)(2,1)S(1)} %get-tuple-element.16.refs_0_.refs_4_, bf16[776,128]{1,0:T(8,128)(2,1)S(1)} %collective-permute-done.1.refs_1_, bf16[776,128]{1,0:T(8,128)(2,1)S(1)} %collective-permute-done.refs_1_.refs_2_, ...), custom_call_target="tpu_custom_call" | custom-call | flops 100663296 | bytes 983040 | tf_op jit(solution)/shard_map/score_last/pallas_call | solution.py:162
  20.5 0.1 collective-permute-start.10
  20.5 0.6 %collective-permute-start.12 = (f32[2,128]{1,0:T(2,128)S(1)}, f32[2,128]{1,0:T(2,128)S(1)}, u32[]{:S(2)}, u32[]{:S(2)}) collective-permute-start(f32[2,128]{1,0:T(2,128)S(1)} %get-tuple-element.26), channel_id=1, source_target_pairs={{0,4},{1,5},{2,6},{3,7},{4,0},{5,1},{6,2},{7,3},{8,12},{9,13},{10,... | collective-permute-start | bytes 3080 | tf_op jit(solution)/shard_map/ppermute | solution.py:198
  21.1 0.5 %collective-permute-done.10 = f32[1,128]{1,0:T(1,128)S(1)} collective-permute-done((f32[1,128]{1,0:T(1,128)S(1)}, f32[1,128]{1,0:T(1,128)S(1)}, u32[]{:S(2)}, u32[]{:S(2)}) %collective-permute-start.10) | collective-permute-done | bytes 544 | tf_op jit(solution)/shard_map/ppermute | solution.py:198
  21.6 2.5 %collective-permute-start.8 = (f32[1,128]{1,0:T(1,128)S(1)}, f32[1,128]{1,0:T(1,128)S(1)}, u32[]{:S(2)}, u32[]{:S(2)}) collective-permute-start(f32[1,128]{1,0:T(1,128)S(1)} %slice.20), channel_id=1, source_target_pairs={{8,0},{9,1},{10,2},{11,3},{12,4},{13,5},{14,6},{15,7},{16,8},{17,9... | collective-permute-start | bytes 1544 | tf_op jit(solution)/shard_map/ppermute | solution.py:194
  24.2 1.6 %collective-permute-start.13 = (f32[1,128]{1,0:T(1,128)S(1)}, f32[1,128]{1,0:T(1,128)S(1)}, u32[]{:S(2)}, u32[]{:S(2)}) collective-permute-start(f32[1,128]{1,0:T(1,128)S(1)} %slice.23), channel_id=1, source_target_pairs={{0,2},{1,3},{2,0},{3,1},{4,6},{5,7},{6,4},{7,5},{8,10},{9,11},{10,... | collective-permute-start | bytes 1544 | tf_op jit(solution)/shard_map/ppermute | solution.py:198
  25.8 1.9 %collective-permute-done.11 = f32[1,128]{1,0:T(1,128)S(1)} collective-permute-done((f32[1,128]{1,0:T(1,128)S(1)}, f32[1,128]{1,0:T(1,128)S(1)}, u32[]{:S(2)}, u32[]{:S(2)}) %collective-permute-start.11) | collective-permute-done | bytes 544 | tf_op jit(solution)/shard_map/ppermute | solution.py:194
  27.7 0.1 collective-permute-done.13
  27.8 0.5 %maximum_bitcast_fusion = f32[128]{0:T(128)} fusion(f32[1,128]{1,0:T(1,128)S(1)} %collective-permute-done.13, f32[1,128]{1,0:T(1,128)S(1)} %max.24, f32[2,128]{1,0:T(2,128)S(1)} %max.25), kind=kLoop, calls=%fused_computation.1 | loop fusion | flops 256 | bytes 2048 | tf_op jit(solution)/shard_map/reshape | solution.py:249
  (17 shorter events, 0.1 us)
Async XLA Ops:
  2.6 8.0 %collective-permute-start = (bf16[776,128]{1,0:T(8,128)(2,1)S(1)}, bf16[776,128]{1,0:T(8,128)(2,1)S(1)}, u32[]{:S(2)}, u32[]{:S(2)}) collective-permute-start(bf16[776,128]{1,0:T(8,128)(2,1)S(1)} %embed.1.refs_0_.refs_2_), channel_id=1, source_target_pairs={{0,4},{1,5},{2,6},{3,7},{4,0},{5,1},{6,2},{7,3},{8,12},{9,13},{10,... | collective-permute-start | bytes 595976 | tf_op jit(solution)/shard_map/ppermute | solution.py:198
  5.7 9.7 %collective-permute-start.3 = (bf16[776,128]{1,0:T(8,128)(2,1)S(1)}, bf16[776,128]{1,0:T(8,128)(2,1)S(1)}, u32[]{:S(2)}, u32[]{:S(2)}) collective-permute-start(bf16[776,128]{1,0:T(8,128)(2,1)S(1)} %embed.1.refs_0_.refs_2_), channel_id=1, source_target_pairs={{0,8},{1,9},{2,10},{3,11},{4,12},{5,13},{6,14},{7,15},{8,16},{9,17... | collective-permute-start | bytes 595976 | tf_op jit(solution)/shard_map/ppermute | solution.py:194
  7.2 8.1 %collective-permute-start.1 = (bf16[776,128]{1,0:T(8,128)(2,1)S(1)}, bf16[776,128]{1,0:T(8,128)(2,1)S(1)}, u32[]{:S(2)}, u32[]{:S(2)}) collective-permute-start(bf16[776,128]{1,0:T(8,128)(2,1)S(1)} %embed.1.refs_0_.refs_2_), channel_id=1, source_target_pairs={{0,2},{1,3},{2,0},{3,1},{4,6},{5,7},{6,4},{7,5},{8,10},{9,11},{10,... | collective-permute-start | bytes 595976 | tf_op jit(solution)/shard_map/ppermute | solution.py:198
  8.7 9.4 %collective-permute-start.4 = (bf16[776,128]{1,0:T(8,128)(2,1)S(1)}, bf16[776,128]{1,0:T(8,128)(2,1)S(1)}, u32[]{:S(2)}, u32[]{:S(2)}) collective-permute-start(bf16[776,128]{1,0:T(8,128)(2,1)S(1)} %embed.1.refs_0_.refs_2_), channel_id=1, source_target_pairs={{16,0},{17,1},{18,2},{19,3},{20,4},{21,5},{22,6},{23,7},{8,24},{9,... | collective-permute-start | bytes 595976 | tf_op jit(solution)/shard_map/ppermute | solution.py:194
  10.6 7.6 %collective-permute-start.2 = (bf16[776,128]{1,0:T(8,128)(2,1)S(1)}, bf16[776,128]{1,0:T(8,128)(2,1)S(1)}, u32[]{:S(2)}, u32[]{:S(2)}) collective-permute-start(bf16[776,128]{1,0:T(8,128)(2,1)S(1)} %collective-permute-done.refs_1_.refs_2_), channel_id=1, source_target_pairs={{0,2},{1,3},{2,0},{3,1},{4,6},{5,7},{6,4},{7,5},{8,10},{9,11},{10,... | collective-permute-start | bytes 595976 | tf_op jit(solution)/shard_map/ppermute | solution.py:198
  12.7 6.2 %collective-permute-start.5 = (bf16[776,128]{1,0:T(8,128)(2,1)S(1)}, bf16[776,128]{1,0:T(8,128)(2,1)S(1)}, u32[]{:S(2)}, u32[]{:S(2)}) collective-permute-start(bf16[776,128]{1,0:T(8,128)(2,1)S(1)} %get-tuple-element.16.refs_0_.refs_4_), channel_id=1, source_target_pairs={{0,1},{1,0},{2,3},{3,2},{4,5},{5,4},{6,7},{7,6},{8,9},{9,8},{10,11... | collective-permute-start | bytes 595976 | tf_op jit(solution)/shard_map/ppermute | solution.py:198
  15.3 3.5 %collective-permute-start.6 = (bf16[776,128]{1,0:T(8,128)(2,1)S(1)}, bf16[776,128]{1,0:T(8,128)(2,1)S(1)}, u32[]{:S(2)}, u32[]{:S(2)}) collective-permute-start(bf16[776,128]{1,0:T(8,128)(2,1)S(1)} %collective-permute-done.3.refs_5_), channel_id=1, source_target_pairs={{0,1},{1,0},{2,3},{3,2},{4,5},{5,4},{6,7},{7,6},{8,9},{9,8},{10,11... | collective-permute-start | bytes 595976 | tf_op jit(solution)/shard_map/ppermute | solution.py:198
  18.2 1.8 %collective-permute-start.9 = (bf16[776,128]{1,0:T(8,128)(2,1)S(1)}, bf16[776,128]{1,0:T(8,128)(2,1)S(1)}, u32[]{:S(2)}, u32[]{:S(2)}) collective-permute-start(bf16[776,128]{1,0:T(8,128)(2,1)S(1)} %collective-permute-done.4.refs_6_), channel_id=1, source_target_pairs={{0,1},{1,0},{2,3},{3,2},{4,5},{5,4},{6,7},{7,6},{8,9},{9,8},{10,11... | collective-permute-start | bytes 595976 | tf_op jit(solution)/shard_map/ppermute | solution.py:198
  19.4 1.7 %collective-permute-start.7 = (f32[2,128]{1,0:T(2,128)S(1)}, f32[2,128]{1,0:T(2,128)S(1)}, u32[]{:S(2)}, u32[]{:S(2)}) collective-permute-start(f32[2,128]{1,0:T(2,128)S(1)} %get-tuple-element.20), channel_id=1, source_target_pairs={{0,1},{1,0},{2,3},{3,2},{4,5},{5,4},{6,7},{7,6},{8,9},{9,8},{10,11... | collective-permute-start | bytes 3080 | tf_op jit(solution)/shard_map/ppermute | solution.py:198
  20.5 1.2 %collective-permute-start.10 = (f32[1,128]{1,0:T(1,128)S(1)}, f32[1,128]{1,0:T(1,128)S(1)}, u32[]{:S(2)}, u32[]{:S(2)}) collective-permute-start(f32[1,128]{1,0:T(1,128)S(1)} %get-tuple-element.23), channel_id=1, source_target_pairs={{0,1},{1,0},{2,3},{3,2},{4,5},{5,4},{6,7},{7,6},{8,9},{9,8},{10,11... | collective-permute-start | bytes 1544 | tf_op jit(solution)/shard_map/ppermute | solution.py:198
  20.5 3.6 %collective-permute-start.12 = (f32[2,128]{1,0:T(2,128)S(1)}, f32[2,128]{1,0:T(2,128)S(1)}, u32[]{:S(2)}, u32[]{:S(2)}) collective-permute-start(f32[2,128]{1,0:T(2,128)S(1)} %get-tuple-element.26), channel_id=1, source_target_pairs={{0,4},{1,5},{2,6},{3,7},{4,0},{5,1},{6,2},{7,3},{8,12},{9,13},{10,... | collective-permute-start | bytes 3080 | tf_op jit(solution)/shard_map/ppermute | solution.py:198
  21.6 4.1 %collective-permute-start.8 = (f32[1,128]{1,0:T(1,128)S(1)}, f32[1,128]{1,0:T(1,128)S(1)}, u32[]{:S(2)}, u32[]{:S(2)}) collective-permute-start(f32[1,128]{1,0:T(1,128)S(1)} %slice.20), channel_id=1, source_target_pairs={{8,0},{9,1},{10,2},{11,3},{12,4},{13,5},{14,6},{15,7},{16,8},{17,9... | collective-permute-start | bytes 1544 | tf_op jit(solution)/shard_map/ppermute | solution.py:194
  24.2 3.5 %collective-permute-start.11 = (f32[1,128]{1,0:T(1,128)S(1)}, f32[1,128]{1,0:T(1,128)S(1)}, u32[]{:S(2)}, u32[]{:S(2)}) collective-permute-start(f32[1,128]{1,0:T(1,128)S(1)} %slice_maximum_fusion.1), channel_id=1, source_target_pairs={{0,16},{1,17},{2,18},{3,19},{4,20},{5,21},{6,22},{7,23},{24,8},{25... | collective-permute-start | bytes 1544 | tf_op jit(solution)/shard_map/ppermute | solution.py:194
  24.2 3.6 %collective-permute-start.13 = (f32[1,128]{1,0:T(1,128)S(1)}, f32[1,128]{1,0:T(1,128)S(1)}, u32[]{:S(2)}, u32[]{:S(2)}) collective-permute-start(f32[1,128]{1,0:T(1,128)S(1)} %slice.23), channel_id=1, source_target_pairs={{0,2},{1,3},{2,0},{3,1},{4,6},{5,7},{6,4},{7,5},{8,10},{9,11},{10,... | collective-permute-start | bytes 1544 | tf_op jit(solution)/shard_map/ppermute | solution.py:198

commit v4 on v2

--- a/solution.py
+++ b/solution.py
@@ -10,7 +10,7 @@
 AXES = ("line", "mid", "grp")
 NOTE_ROWS = 8
 RADIX = 256
-CHUNKS = 8
+CHUNKS = 4
 VMEM = pl.BlockSpec(memory_space=pltpu.VMEM)
 HBM = pl.BlockSpec(memory_space=pltpu.HBM)
 
@@ -22,23 +22,23 @@
     rows, depth = states.shape
     width = proj.shape[1]
     span = depth // CHUNKS
-    copies = []
-    for i in range(CHUNKS):
-        part = pl.ds(i * span, span)
-        copies.append((
-            pltpu.make_async_copy(states_hbm.at[:, part], states.at[:, part], big_sem.at[0, i]),
-            pltpu.make_async_copy(proj_hbm.at[part], proj.at[part], big_sem.at[1, i]),
-        ))
+    whole = pltpu.make_async_copy(states_hbm, states, big_sem.at[CHUNKS])
+    copies = [
+        pltpu.make_async_copy(
+            proj_hbm.at[pl.ds(i * span, span)], proj.at[pl.ds(i * span, span)], big_sem.at[i]
+        )
+        for i in range(CHUNKS)
+    ]
     small = [
         pltpu.make_async_copy(src, dst, small_sem.at[i])
         for i, (src, dst) in enumerate(((owner_hbm, owner), (sub_hbm, sub), (prio_hbm, prio)))
     ]
-    for copy in [c for pair in copies for c in pair] + small:
+    for copy in [whole] + copies + small:
         copy.start()
+    whole.wait()
     projected = None
-    for i, pair in enumerate(copies):
-        for copy in pair:
-            copy.wait()
+    for i, copy in enumerate(copies):
+        copy.wait()
         part = slice(i * span, (i + 1) * span)
         term = jnp.dot(states[:, part], proj[part, :], preferred_element_type=jnp.float32)
         projected = term if projected is None else projected + term
@@ -70,7 +70,7 @@
             pltpu.VMEM((1, rows), jnp.int32),
             pltpu.VMEM((1, rows), jnp.int32),
             pltpu.VMEM((1, rows), jnp.int32),
-            pltpu.SemaphoreType.DMA((2, CHUNKS)),
+            pltpu.SemaphoreType.DMA((CHUNKS + 1,)),
             pltpu.SemaphoreType.DMA((3,)),
         ],
         compiler_params=pltpu.CompilerParams(vmem_limit_bytes=40 << 20),
@@ -223,8 +223,9 @@
     row_blocks[0] = lanes[0] = held
     products = [(rest, every), (soon, every[1:])]
     lines, backs = score("score_late", row_blocks, lanes, products, [(0, count)], lines)
-    partner = [lax.optimization_barrier((held, visitors[0]))[0]]
-    partner += [lax.optimization_barrier((visitor, row_blocks[1]))[0] for visitor in visitors]
+    partner = [held]
+    partner += [lax.optimization_barrier((visitor, held))[0] for visitor in visitors[:-1]]
+    partner += [lax.optimization_barrier((visitors[-1], row_blocks[1]))[0]]
     partner = [swap(lane, 1) for lane in partner]
     products, parts = [(tuple(range(count)), every)], [(0, half), (half, count)]
     theirs, near, far = score("score_partner", row_blocks, partner, products, parts, None, backs)

time: 28.3 us -> 28.3 us (level)
  starting transfers between devices: 14.4 us -> 13.7 us
  waiting for transfers between devices: 8.87 us -> 9.57 us
    ppermute x9, waiting for transfers between devices: 2.08 us -> 2.63 us  [swap(): return lax.ppermute(array, AXES, pairs)]
    ppermute x9, starting transfers between devices: 8.93 us -> 8.5 us  [swap(): return lax.ppermute(array, AXES, pairs)]
where the time goes in v4:
time: 28.3 us; the launch traced here: 28.1 us
  starting transfers between devices  13.7 us (48%)
  waiting for transfers between devices  9.57 us (34%)
  Pallas kernels  4.29 us (15%)
  other arithmetic  0.52 us (2%)
    ppermute x9, starting transfers between devices, swap(): return lax.ppermute(array, AXES, pairs)  8.5 us
    ppermute x4, waiting for transfers between devices, move(): return lax.ppermute(array, AXES, whole)  6.95 us
    ppermute x4, starting transfers between devices, move(): return lax.ppermute(array, AXES, whole)  5.18 us
    ppermute x9, waiting for transfers between devices, swap(): return lax.ppermute(array, AXES, pairs)  2.63 us
    pallas_call x1, Pallas kernels, embed(): pl.pallas_call(embed_kernel, in_specs=[HBM] * 5, out_specs=VMEM, out_shap...  2.55 us
    pallas_call x3, Pallas kernels, score(): pl.pallas_call(lambda *refs: score_kernel(*counts, *rest, *refs), in_spec...  1.75 us
  transfers between devices with their start and end apart: 13, of which 8 were waited for; matrix products, arithmetic and copies ran while one was open for 0% of the time, Pallas kernels for 4%

profile of v4, /device:TPU:0, one launch (start us, length us, event | category | flops | bytes accessed | tf_op | source)
XLA Modules:
  0.0 28.1 jit_solution(13886541459611685320)
XLA Ops:
  0.0 2.5 %embed.1.refs_0_.refs_2_ = bf16[776,128]{1,0:T(8,128)(2,1)S(1)} custom-call(bf16[128,2048]{1,0:T(8,128)(2,1)} %states_hbm.1, bf16[2048,768]{1,0:T(8,128)(2,1)} %proj_hbm.1, s32[1,128]{1,0:T(1,128)} %bitcast.5, s32[1,128]{1,0:T(1,128)} %bitcast.6, s32[1,128]{1,0:T(1,128)} %bitcast.7), custom_call_target="tpu_custom_call" | custom-call | tf_op jit(solution)/shard_map/embed/pallas_call | solution.py:62
  2.6 3.0 %collective-permute-start = (bf16[776,128]{1,0:T(8,128)(2,1)S(1)}, bf16[776,128]{1,0:T(8,128)(2,1)S(1)}, u32[]{:S(2)}, u32[]{:S(2)}) collective-permute-start(bf16[776,128]{1,0:T(8,128)(2,1)S(1)} %embed.1.refs_0_.refs_2_), channel_id=1, source_target_pairs={{0,4},{1,5},{2,6},{3,7},{4,0},{5,1},{6,2},{7,3},{8,12},{9,13},{10,... | collective-permute-start | bytes 595976 | tf_op jit(solution)/shard_map/ppermute | solution.py:198
  5.6 1.6 %collective-permute-start.3 = (bf16[776,128]{1,0:T(8,128)(2,1)S(1)}, bf16[776,128]{1,0:T(8,128)(2,1)S(1)}, u32[]{:S(2)}, u32[]{:S(2)}) collective-permute-start(bf16[776,128]{1,0:T(8,128)(2,1)S(1)} %embed.1.refs_0_.refs_2_), channel_id=1, source_target_pairs={{0,8},{1,9},{2,10},{3,11},{4,12},{5,13},{6,14},{7,15},{8,16},{9,17... | collective-permute-start | bytes 595976 | tf_op jit(solution)/shard_map/ppermute | solution.py:194
  7.2 1.5 %collective-permute-start.1 = (bf16[776,128]{1,0:T(8,128)(2,1)S(1)}, bf16[776,128]{1,0:T(8,128)(2,1)S(1)}, u32[]{:S(2)}, u32[]{:S(2)}) collective-permute-start(bf16[776,128]{1,0:T(8,128)(2,1)S(1)} %embed.1.refs_0_.refs_2_), channel_id=1, source_target_pairs={{0,2},{1,3},{2,0},{3,1},{4,6},{5,7},{6,4},{7,5},{8,10},{9,11},{10,... | collective-permute-start | bytes 595976 | tf_op jit(solution)/shard_map/ppermute | solution.py:198
  8.7 1.6 %collective-permute-start.4 = (bf16[776,128]{1,0:T(8,128)(2,1)S(1)}, bf16[776,128]{1,0:T(8,128)(2,1)S(1)}, u32[]{:S(2)}, u32[]{:S(2)}) collective-permute-start(bf16[776,128]{1,0:T(8,128)(2,1)S(1)} %embed.1.refs_0_.refs_2_), channel_id=1, source_target_pairs={{16,0},{17,1},{18,2},{19,3},{20,4},{21,5},{22,6},{23,7},{8,24},{9,... | collective-permute-start | bytes 595976 | tf_op jit(solution)/shard_map/ppermute | solution.py:194
  10.2 0.3 %collective-permute-done.refs_1_.refs_2_ = bf16[776,128]{1,0:T(8,128)(2,1)S(1)} collective-permute-done((bf16[776,128]{1,0:T(8,128)(2,1)S(1)}, bf16[776,128]{1,0:T(8,128)(2,1)S(1)}, u32[]{:S(2)}, u32[]{:S(2)}) %collective-permute-start) | collective-permute-done | bytes 198688 | tf_op jit(solution)/shard_map/ppermute | solution.py:198
  10.5 1.7 %collective-permute-start.2 = (bf16[776,128]{1,0:T(8,128)(2,1)S(1)}, bf16[776,128]{1,0:T(8,128)(2,1)S(1)}, u32[]{:S(2)}, u32[]{:S(2)}) collective-permute-start(bf16[776,128]{1,0:T(8,128)(2,1)S(1)} %collective-permute-done.refs_1_.refs_2_), channel_id=1, source_target_pairs={{0,2},{1,3},{2,0},{3,1},{4,6},{5,7},{6,4},{7,5},{8,10},{9,11},{10,... | collective-permute-start | bytes 595976 | tf_op jit(solution)/shard_map/ppermute | solution.py:198
  12.2 0.3 %score_soon.1 = (f32[1,128]{1,0:T(1,128)S(1)}, bf16[776,128]{1,0:T(8,128)(2,1)S(1)}) custom-call(bf16[776,128]{1,0:T(8,128)(2,1)S(1)} %embed.1.refs_0_.refs_2_, bf16[776,128]{1,0:T(8,128)(2,1)S(1)} %collective-permute-done.refs_1_.refs_2_, bf16[776,128]{1,0:T(8,128)(2,1)S(1)} %embed.1.refs_0_.refs_2_), custom_call_target="tpu_custom_call" | custom-call | flops 50331648 | bytes 589824 | tf_op jit(solution)/shard_map/score_soon/pallas_call | solution.py:162
  12.6 0.1 collective-permute-start.5
  12.7 2.6 %collective-permute-done.3.refs_5_ = bf16[776,128]{1,0:T(8,128)(2,1)S(1)} collective-permute-done((bf16[776,128]{1,0:T(8,128)(2,1)S(1)}, bf16[776,128]{1,0:T(8,128)(2,1)S(1)}, u32[]{:S(2)}, u32[]{:S(2)}) %collective-permute-start.3) | collective-permute-done | bytes 198688 | tf_op jit(solution)/shard_map/ppermute | solution.py:194
  15.3 0.0 collective-permute-start.6
  15.3 2.8 %collective-permute-done.4.refs_6_ = bf16[776,128]{1,0:T(8,128)(2,1)S(1)} collective-permute-done((bf16[776,128]{1,0:T(8,128)(2,1)S(1)}, bf16[776,128]{1,0:T(8,128)(2,1)S(1)}, u32[]{:S(2)}, u32[]{:S(2)}) %collective-permute-start.4) | collective-permute-done | bytes 198688 | tf_op jit(solution)/shard_map/ppermute | solution.py:194
  18.1 0.7 %score_late.1 = (f32[3,128]{1,0:T(4,128)S(1)}, f32[4,128]{1,0:T(4,128)S(1)}) custom-call(bf16[776,128]{1,0:T(8,128)(2,1)S(1)} %get-tuple-element.14.refs_0_.refs_4_, bf16[776,128]{1,0:T(8,128)(2,1)S(1)} %collective-permute-done.1.refs_1_, bf16[776,128]{1,0:T(8,128)(2,1)S(1)} %collective-permute-done.refs_1_.refs_2_, ...), custom_call_target="tpu_custom_call" | custom-call | flops 251658240 | bytes 1376256 | tf_op jit(solution)/shard_map/score_late/pallas_call | solution.py:162
  18.8 0.8 %collective-permute-done.7.refs_6_ = bf16[776,128]{1,0:T(8,128)(2,1)S(1)} collective-permute-done((bf16[776,128]{1,0:T(8,128)(2,1)S(1)}, bf16[776,128]{1,0:T(8,128)(2,1)S(1)}, u32[]{:S(2)}, u32[]{:S(2)}) %collective-permute-start.7) | collective-permute-done | bytes 198688 | tf_op jit(solution)/shard_map/ppermute | solution.py:198
  19.5 0.8 %score_partner.1 = (f32[3,128]{1,0:T(4,128)S(1)}, f32[2,128]{1,0:T(2,128)S(1)}, f32[2,128]{1,0:T(2,128)S(1)}) custom-call(bf16[776,128]{1,0:T(8,128)(2,1)S(1)} %get-tuple-element.14.refs_0_.refs_4_, bf16[776,128]{1,0:T(8,128)(2,1)S(1)} %collective-permute-done.1.refs_1_, bf16[776,128]{1,0:T(8,128)(2,1)S(1)} %collective-permute-done.refs_1_.refs_2_, ...), custom_call_target="tpu_custom_call" | custom-call | flops 301989888 | bytes 1376256 | tf_op jit(solution)/shard_map/score_partner/pallas_call | solution.py:162
  20.3 0.2 collective-permute-start.8
  20.5 0.5 %collective-permute-start.11 = (f32[2,128]{1,0:T(2,128)S(1)}, f32[2,128]{1,0:T(2,128)S(1)}, u32[]{:S(2)}, u32[]{:S(2)}) collective-permute-start(f32[2,128]{1,0:T(2,128)S(1)} %get-tuple-element.22), channel_id=1, source_target_pairs={{0,4},{1,5},{2,6},{3,7},{4,0},{5,1},{6,2},{7,3},{8,12},{9,13},{10,... | collective-permute-start | bytes 3080 | tf_op jit(solution)/shard_map/ppermute | solution.py:198
  21.0 0.5 %collective-permute-done.8 = f32[3,128]{1,0:T(4,128)S(1)} collective-permute-done((f32[3,128]{1,0:T(4,128)S(1)}, f32[3,128]{1,0:T(4,128)S(1)}, u32[]{:S(2)}, u32[]{:S(2)}) %collective-permute-start.8) | collective-permute-done | bytes 1568 | tf_op jit(solution)/shard_map/ppermute | solution.py:198
  21.5 2.0 %collective-permute-start.10 = (f32[1,128]{1,0:T(1,128)S(1)}, f32[1,128]{1,0:T(1,128)S(1)}, u32[]{:S(2)}, u32[]{:S(2)}) collective-permute-start(f32[1,128]{1,0:T(1,128)S(1)} %get-tuple-element.24), channel_id=1, source_target_pairs={{8,0},{9,1},{10,2},{11,3},{12,4},{13,5},{14,6},{15,7},{16,8},{17,9... | collective-permute-start | bytes 1544 | tf_op jit(solution)/shard_map/ppermute | solution.py:194
  23.5 0.5 %collective-permute-done.11 = f32[2,128]{1,0:T(2,128)S(1)} collective-permute-done((f32[2,128]{1,0:T(2,128)S(1)}, f32[2,128]{1,0:T(2,128)S(1)}, u32[]{:S(2)}, u32[]{:S(2)}) %collective-permute-start.11) | collective-permute-done | bytes 1056 | tf_op jit(solution)/shard_map/ppermute | solution.py:198
  24.1 1.5 %collective-permute-start.12 = (f32[1,128]{1,0:T(1,128)S(1)}, f32[1,128]{1,0:T(1,128)S(1)}, u32[]{:S(2)}, u32[]{:S(2)}) collective-permute-start(f32[1,128]{1,0:T(1,128)S(1)} %slice.19), channel_id=1, source_target_pairs={{0,2},{1,3},{2,0},{3,1},{4,6},{5,7},{6,4},{7,5},{8,10},{9,11},{10,... | collective-permute-start | bytes 1544 | tf_op jit(solution)/shard_map/ppermute | solution.py:198
  25.6 1.5 %collective-permute-done.9 = f32[1,128]{1,0:T(1,128)S(1)} collective-permute-done((f32[1,128]{1,0:T(1,128)S(1)}, f32[1,128]{1,0:T(1,128)S(1)}, u32[]{:S(2)}, u32[]{:S(2)}) %collective-permute-start.9) | collective-permute-done | bytes 544 | tf_op jit(solution)/shard_map/ppermute | solution.py:194
  27.1 0.5 %collective-permute-done.12 = f32[1,128]{1,0:T(1,128)S(1)} collective-permute-done((f32[1,128]{1,0:T(1,128)S(1)}, f32[1,128]{1,0:T(1,128)S(1)}, u32[]{:S(2)}, u32[]{:S(2)}) %collective-permute-start.12) | collective-permute-done | bytes 544 | tf_op jit(solution)/shard_map/ppermute | solution.py:198
  27.6 0.5 %maximum_bitcast_fusion = f32[128]{0:T(128)} fusion(f32[1,128]{1,0:T(1,128)S(1)} %collective-permute-done.12, f32[1,128]{1,0:T(1,128)S(1)} %maximum_maximum_fusion, f32[2,128]{1,0:T(2,128)S(1)} %max.21), kind=kLoop, calls=%fused_computation | loop fusion | flops 256 | bytes 2048 | tf_op jit(solution)/shard_map/reshape | solution.py:242
  (12 shorter events, 0.0 us)
Async XLA Ops:
  2.6 8.0 %collective-permute-start = (bf16[776,128]{1,0:T(8,128)(2,1)S(1)}, bf16[776,128]{1,0:T(8,128)(2,1)S(1)}, u32[]{:S(2)}, u32[]{:S(2)}) collective-permute-start(bf16[776,128]{1,0:T(8,128)(2,1)S(1)} %embed.1.refs_0_.refs_2_), channel_id=1, source_target_pairs={{0,4},{1,5},{2,6},{3,7},{4,0},{5,1},{6,2},{7,3},{8,12},{9,13},{10,... | collective-permute-start | bytes 595976 | tf_op jit(solution)/shard_map/ppermute | solution.py:198
  5.6 9.7 %collective-permute-start.3 = (bf16[776,128]{1,0:T(8,128)(2,1)S(1)}, bf16[776,128]{1,0:T(8,128)(2,1)S(1)}, u32[]{:S(2)}, u32[]{:S(2)}) collective-permute-start(bf16[776,128]{1,0:T(8,128)(2,1)S(1)} %embed.1.refs_0_.refs_2_), channel_id=1, source_target_pairs={{0,8},{1,9},{2,10},{3,11},{4,12},{5,13},{6,14},{7,15},{8,16},{9,17... | collective-permute-start | bytes 595976 | tf_op jit(solution)/shard_map/ppermute | solution.py:194
  7.2 8.1 %collective-permute-start.1 = (bf16[776,128]{1,0:T(8,128)(2,1)S(1)}, bf16[776,128]{1,0:T(8,128)(2,1)S(1)}, u32[]{:S(2)}, u32[]{:S(2)}) collective-permute-start(bf16[776,128]{1,0:T(8,128)(2,1)S(1)} %embed.1.refs_0_.refs_2_), channel_id=1, source_target_pairs={{0,2},{1,3},{2,0},{3,1},{4,6},{5,7},{6,4},{7,5},{8,10},{9,11},{10,... | collective-permute-start | bytes 595976 | tf_op jit(solution)/shard_map/ppermute | solution.py:198
  8.7 9.5 %collective-permute-start.4 = (bf16[776,128]{1,0:T(8,128)(2,1)S(1)}, bf16[776,128]{1,0:T(8,128)(2,1)S(1)}, u32[]{:S(2)}, u32[]{:S(2)}) collective-permute-start(bf16[776,128]{1,0:T(8,128)(2,1)S(1)} %embed.1.refs_0_.refs_2_), channel_id=1, source_target_pairs={{16,0},{17,1},{18,2},{19,3},{20,4},{21,5},{22,6},{23,7},{8,24},{9,... | collective-permute-start | bytes 595976 | tf_op jit(solution)/shard_map/ppermute | solution.py:194
  10.5 7.6 %collective-permute-start.2 = (bf16[776,128]{1,0:T(8,128)(2,1)S(1)}, bf16[776,128]{1,0:T(8,128)(2,1)S(1)}, u32[]{:S(2)}, u32[]{:S(2)}) collective-permute-start(bf16[776,128]{1,0:T(8,128)(2,1)S(1)} %collective-permute-done.refs_1_.refs_2_), channel_id=1, source_target_pairs={{0,2},{1,3},{2,0},{3,1},{4,6},{5,7},{6,4},{7,5},{8,10},{9,11},{10,... | collective-permute-start | bytes 595976 | tf_op jit(solution)/shard_map/ppermute | solution.py:198
  12.6 6.2 %collective-permute-start.5 = (bf16[776,128]{1,0:T(8,128)(2,1)S(1)}, bf16[776,128]{1,0:T(8,128)(2,1)S(1)}, u32[]{:S(2)}, u32[]{:S(2)}) collective-permute-start(bf16[776,128]{1,0:T(8,128)(2,1)S(1)} %get-tuple-element.14.refs_0_.refs_4_), channel_id=1, source_target_pairs={{0,1},{1,0},{2,3},{3,2},{4,5},{5,4},{6,7},{7,6},{8,9},{9,8},{10,11... | collective-permute-start | bytes 595976 | tf_op jit(solution)/shard_map/ppermute | solution.py:198
  15.3 3.5 %collective-permute-start.6 = (bf16[776,128]{1,0:T(8,128)(2,1)S(1)}, bf16[776,128]{1,0:T(8,128)(2,1)S(1)}, u32[]{:S(2)}, u32[]{:S(2)}) collective-permute-start(bf16[776,128]{1,0:T(8,128)(2,1)S(1)} %collective-permute-done.3.refs_5_), channel_id=1, source_target_pairs={{0,1},{1,0},{2,3},{3,2},{4,5},{5,4},{6,7},{7,6},{8,9},{9,8},{10,11... | collective-permute-start | bytes 595976 | tf_op jit(solution)/shard_map/ppermute | solution.py:198
  18.1 1.4 %collective-permute-start.7 = (bf16[776,128]{1,0:T(8,128)(2,1)S(1)}, bf16[776,128]{1,0:T(8,128)(2,1)S(1)}, u32[]{:S(2)}, u32[]{:S(2)}) collective-permute-start(bf16[776,128]{1,0:T(8,128)(2,1)S(1)} %collective-permute-done.4.refs_6_), channel_id=1, source_target_pairs={{0,1},{1,0},{2,3},{3,2},{4,5},{5,4},{6,7},{7,6},{8,9},{9,8},{10,11... | collective-permute-start | bytes 595976 | tf_op jit(solution)/shard_map/ppermute | solution.py:198
  20.3 1.2 %collective-permute-start.8 = (f32[3,128]{1,0:T(4,128)S(1)}, f32[3,128]{1,0:T(4,128)S(1)}, u32[]{:S(2)}, u32[]{:S(2)}) collective-permute-start(f32[3,128]{1,0:T(4,128)S(1)} %get-tuple-element.20), channel_id=1, source_target_pairs={{0,1},{1,0},{2,3},{3,2},{4,5},{5,4},{6,7},{7,6},{8,9},{9,8},{10,11... | collective-permute-start | bytes 4616 | tf_op jit(solution)/shard_map/ppermute | solution.py:198
  20.5 3.6 %collective-permute-start.11 = (f32[2,128]{1,0:T(2,128)S(1)}, f32[2,128]{1,0:T(2,128)S(1)}, u32[]{:S(2)}, u32[]{:S(2)}) collective-permute-start(f32[2,128]{1,0:T(2,128)S(1)} %get-tuple-element.22), channel_id=1, source_target_pairs={{0,4},{1,5},{2,6},{3,7},{4,0},{5,1},{6,2},{7,3},{8,12},{9,13},{10,... | collective-permute-start | bytes 3080 | tf_op jit(solution)/shard_map/ppermute | solution.py:198
  21.5 4.1 %collective-permute-start.10 = (f32[1,128]{1,0:T(1,128)S(1)}, f32[1,128]{1,0:T(1,128)S(1)}, u32[]{:S(2)}, u32[]{:S(2)}) collective-permute-start(f32[1,128]{1,0:T(1,128)S(1)} %get-tuple-element.24), channel_id=1, source_target_pairs={{8,0},{9,1},{10,2},{11,3},{12,4},{13,5},{14,6},{15,7},{16,8},{17,9... | collective-permute-start | bytes 1544 | tf_op jit(solution)/shard_map/ppermute | solution.py:194
  23.5 3.5 %collective-permute-start.9 = (f32[1,128]{1,0:T(1,128)S(1)}, f32[1,128]{1,0:T(1,128)S(1)}, u32[]{:S(2)}, u32[]{:S(2)}) collective-permute-start(f32[1,128]{1,0:T(1,128)S(1)} %get-tuple-element.23), channel_id=1, source_target_pairs={{0,16},{1,17},{2,18},{3,19},{4,20},{5,21},{6,22},{7,23},{24,8},{25... | collective-permute-start | bytes 1544 | tf_op jit(solution)/shard_map/ppermute | solution.py:194
  24.1 3.5 %collective-permute-start.12 = (f32[1,128]{1,0:T(1,128)S(1)}, f32[1,128]{1,0:T(1,128)S(1)}, u32[]{:S(2)}, u32[]{:S(2)}) collective-permute-start(f32[1,128]{1,0:T(1,128)S(1)} %slice.19), channel_id=1, source_target_pairs={{0,2},{1,3},{2,0},{3,1},{4,6},{5,7},{6,4},{7,5},{8,10},{9,11},{10,... | collective-permute-start | bytes 1544 | tf_op jit(solution)/shard_map/ppermute | solution.py:198

commit v5 on v4

--- a/solution.py
+++ b/solution.py
@@ -9,6 +9,7 @@
 
 AXES = ("line", "mid", "grp")
 NOTE_ROWS = 8
+MORE_ROWS = 56
 RADIX = 256
 CHUNKS = 4
 VMEM = pl.BlockSpec(memory_space=pltpu.VMEM)
@@ -16,7 +17,7 @@
 
 
 def embed_kernel(
-    states_hbm, proj_hbm, owner_hbm, sub_hbm, prio_hbm, block_ref,
+    states_hbm, proj_hbm, owner_hbm, sub_hbm, prio_hbm, block_ref, tall_ref,
     states, proj, owner, sub, prio, big_sem, small_sem,
 ):
     rows, depth = states.shape
@@ -52,7 +53,10 @@
     notes = [f.astype(jnp.float32) for f in fields]
     notes.append(jnp.zeros((NOTE_ROWS - len(fields), rows), jnp.float32))
     tiles = [embedding[:, i:i + rows] for i in range(0, width, rows)]
-    block_ref[...] = jnp.concatenate(tiles + notes, axis=0).astype(jnp.bfloat16)
+    block = jnp.concatenate(tiles + notes, axis=0).astype(jnp.bfloat16)
+    block_ref[...] = block
+    tall_ref[:block.shape[0], :] = block
+    tall_ref[block.shape[0]:, :] = block[:tall_ref.shape[0] - block.shape[0]]
 
 
 def embed(states, projection, owner, sub, prio):
@@ -62,8 +66,8 @@
     return pl.pallas_call(
         embed_kernel,
         in_specs=[HBM] * 5,
-        out_specs=VMEM,
-        out_shape=jax.ShapeDtypeStruct((high, rows), jnp.bfloat16),
+        out_specs=[VMEM] * 2,
+        out_shape=[jax.ShapeDtypeStruct((tall, rows), jnp.bfloat16) for tall in (high, high + MORE_ROWS)],
         scratch_shapes=[
             pltpu.VMEM((rows, depth), jnp.bfloat16),
             pltpu.VMEM((depth, width), jnp.bfloat16),
@@ -79,16 +83,19 @@
 
 
 def read_notes(ref):
-    tail = ref[ref.shape[0] - NOTE_ROWS:, :].astype(jnp.float32)
+    first = ref.shape[0] // ref.shape[1] * ref.shape[1]
+    tail = ref[first:first + NOTE_ROWS, :].astype(jnp.float32)
     owner, sub, high, low = (tail[i:i + 1] for i in range(4))
     return (owner - 1.0) * 4.0 + sub, high * float(RADIX) + low
 
 
 def read_rows(refs):
     rows = refs[0].shape[1]
-    firsts = range(0, refs[0].shape[0] - NOTE_ROWS, rows)
     return jnp.concatenate(
-        [jnp.concatenate([ref[first:first + rows, :] for ref in refs], axis=0) for first in firsts],
+        [
+            jnp.concatenate([ref[i * rows:(i + 1) * rows, :] for ref in refs], axis=0)
+            for i in range(refs[0].shape[0] // rows)
+        ],
         axis=1,
     )
 
@@ -197,7 +204,7 @@
         pairs = [(i, i // plane * plane + (i % plane ^ step)) for i in range(line * plane)]
         return lax.ppermute(array, AXES, pairs)
 
-    block = embed(
+    block, tall = embed(
         states,
         projection,
         owner_group.reshape(1, rows),
@@ -205,7 +212,7 @@
         priority.reshape(1, rows),
     )
     moves = tournament(line)
-    visitors = [move(block, pairs) for pairs in moves]
+    visitors = [move(tall, moves[0])] + [move(block, pairs) for pairs in moves[1:]]
     bits = [1 << i for i in range(1, plane.bit_length() - 1)]
     found = {0: block}
     for bit in reversed(bits):

time: 28.3 us -> 28.2 us (level)
  waiting for transfers between devices: 9.57 us -> 7.39 us
  starting transfers between devices: 13.7 us -> 15.8 us
    ppermute x4, waiting for transfers between devices: 6.95 us -> 4.3 us  [move(): return lax.ppermute(array, AXES, whole)]
    ppermute x4, starting transfers between devices: 5.18 us -> 7.49 us  [move(): return lax.ppermute(array, AXES, whole)]
    ppermute x9, waiting for transfers between devices: 2.63 us -> 3.09 us  [swap(): return lax.ppermute(array, AXES, pairs)]
  transfers between devices with their start and end apart: 13 -> 13, of which waited for: 8 -> 6; matrix products, arithmetic and copies ran while one was open for 0% -> 0% of each run, Pallas kernels for 4% -> 4%
where the time goes in v5:
time: 28.2 us; the launch traced here: 28.1 us
  starting transfers between devices  15.8 us (56%)
  waiting for transfers between devices  7.39 us (26%)
  Pallas kernels  4.31 us (15%)
  other arithmetic  0.52 us (2%)
    ppermute x9, starting transfers between devices, swap(): return lax.ppermute(array, AXES, pairs)  8.3 us
    ppermute x4, starting transfers between devices, move(): return lax.ppermute(array, AXES, whole)  7.49 us
    ppermute x4, waiting for transfers between devices, move(): return lax.ppermute(array, AXES, whole)  4.3 us
    ppermute x9, waiting for transfers between devices, swap(): return lax.ppermute(array, AXES, pairs)  3.09 us
    pallas_call x1, Pallas kernels, embed(): pl.pallas_call(embed_kernel, in_specs=[HBM] * 5, out_specs=[VMEM] * 2, ou...  2.56 us
    pallas_call x3, Pallas kernels, score(): pl.pallas_call(lambda *refs: score_kernel(*counts, *rest, *refs), in_spec...  1.75 us
  transfers between devices with their start and end apart: 13, of which 6 were waited for; matrix products, arithmetic and copies ran while one was open for 0% of the time, Pallas kernels for 4%

profile of v5, /device:TPU:0, one launch (start us, length us, event | category | flops | bytes accessed | tf_op | source)
XLA Modules:
  0.0 28.1 jit_solution(1983767964094283407)
XLA Ops:
  0.0 2.6 %embed.1 = (bf16[776,128]{1,0:T(8,128)(2,1)S(1)}, bf16[832,128]{1,0:T(8,128)(2,1)S(1)}) custom-call(bf16[128,2048]{1,0:T(8,128)(2,1)} %states_hbm.1, bf16[2048,768]{1,0:T(8,128)(2,1)} %proj_hbm.1, s32[1,128]{1,0:T(1,128)} %bitcast.5, s32[1,128]{1,0:T(1,128)} %bitcast.6, s32[1,128]{1,0:T(1,128)} %bitcast.7), custom_call_target="tpu_custom_call" | custom-call | tf_op jit(solution)/shard_map/embed/pallas_call | solution.py:66
  2.6 3.1 %collective-permute-start.3 = (bf16[832,128]{1,0:T(8,128)(2,1)S(1)}, bf16[832,128]{1,0:T(8,128)(2,1)S(1)}, u32[]{:S(2)}, u32[]{:S(2)}) collective-permute-start(bf16[832,128]{1,0:T(8,128)(2,1)S(1)} %get-tuple-element.18), channel_id=1, source_target_pairs={{0,8},{1,9},{2,10},{3,11},{4,12},{5,13},{6,14},{7,15},{8,16},{9,17... | collective-permute-start | bytes 638984 | tf_op jit(solution)/shard_map/ppermute | solution.py:201
  5.6 1.5 %collective-permute-start = (bf16[776,128]{1,0:T(8,128)(2,1)S(1)}, bf16[776,128]{1,0:T(8,128)(2,1)S(1)}, u32[]{:S(2)}, u32[]{:S(2)}) collective-permute-start(bf16[776,128]{1,0:T(8,128)(2,1)S(1)} %get-tuple-element.16.refs_0_.refs_2_), channel_id=1, source_target_pairs={{0,4},{1,5},{2,6},{3,7},{4,0},{5,1},{6,2},{7,3},{8,12},{9,13},{10,... | collective-permute-start | bytes 595976 | tf_op jit(solution)/shard_map/ppermute | solution.py:205
  7.2 1.5 %collective-permute-start.1 = (bf16[776,128]{1,0:T(8,128)(2,1)S(1)}, bf16[776,128]{1,0:T(8,128)(2,1)S(1)}, u32[]{:S(2)}, u32[]{:S(2)}) collective-permute-start(bf16[776,128]{1,0:T(8,128)(2,1)S(1)} %get-tuple-element.16.refs_0_.refs_2_), channel_id=1, source_target_pairs={{0,2},{1,3},{2,0},{3,1},{4,6},{5,7},{6,4},{7,5},{8,10},{9,11},{10,... | collective-permute-start | bytes 595976 | tf_op jit(solution)/shard_map/ppermute | solution.py:205
  8.7 1.6 %collective-permute-start.4 = (bf16[776,128]{1,0:T(8,128)(2,1)S(1)}, bf16[776,128]{1,0:T(8,128)(2,1)S(1)}, u32[]{:S(2)}, u32[]{:S(2)}) collective-permute-start(bf16[776,128]{1,0:T(8,128)(2,1)S(1)} %get-tuple-element.16.refs_0_.refs_2_), channel_id=1, source_target_pairs={{16,0},{17,1},{18,2},{19,3},{20,4},{21,5},{22,6},{23,7},{8,24},{9,... | collective-permute-start | bytes 595976 | tf_op jit(solution)/shard_map/ppermute | solution.py:201
  10.2 1.8 %collective-permute-done.refs_1_.refs_2_ = bf16[776,128]{1,0:T(8,128)(2,1)S(1)} collective-permute-done((bf16[776,128]{1,0:T(8,128)(2,1)S(1)}, bf16[776,128]{1,0:T(8,128)(2,1)S(1)}, u32[]{:S(2)}, u32[]{:S(2)}) %collective-permute-start) | collective-permute-done | bytes 198688 | tf_op jit(solution)/shard_map/ppermute | solution.py:205
  12.1 1.5 %collective-permute-start.2 = (bf16[776,128]{1,0:T(8,128)(2,1)S(1)}, bf16[776,128]{1,0:T(8,128)(2,1)S(1)}, u32[]{:S(2)}, u32[]{:S(2)}) collective-permute-start(bf16[776,128]{1,0:T(8,128)(2,1)S(1)} %collective-permute-done.refs_1_.refs_2_), channel_id=1, source_target_pairs={{0,2},{1,3},{2,0},{3,1},{4,6},{5,7},{6,4},{7,5},{8,10},{9,11},{10,... | collective-permute-start | bytes 595976 | tf_op jit(solution)/shard_map/ppermute | solution.py:205
  13.5 0.3 %score_soon.1 = (f32[1,128]{1,0:T(1,128)S(1)}, bf16[776,128]{1,0:T(8,128)(2,1)S(1)}) custom-call(bf16[776,128]{1,0:T(8,128)(2,1)S(1)} %get-tuple-element.16.refs_0_.refs_2_, bf16[776,128]{1,0:T(8,128)(2,1)S(1)} %collective-permute-done.refs_1_.refs_2_, bf16[776,128]{1,0:T(8,128)(2,1)S(1)} %get-tuple-element.16.refs_0_.refs_2_), custom_call_target="tpu_custom_call" | custom-call | flops 50331648 | bytes 589824 | tf_op jit(solution)/shard_map/score_soon/pallas_call | solution.py:169
  13.9 0.0 collective-permute-done.3.refs_5_
  13.9 0.1 collective-permute-start.6
  14.0 0.5 %collective-permute-start.5 = (bf16[776,128]{1,0:T(8,128)(2,1)S(1)}, bf16[776,128]{1,0:T(8,128)(2,1)S(1)}, u32[]{:S(2)}, u32[]{:S(2)}) collective-permute-start(bf16[776,128]{1,0:T(8,128)(2,1)S(1)} %get-tuple-element.17.refs_0_.refs_4_), channel_id=1, source_target_pairs={{0,1},{1,0},{2,3},{3,2},{4,5},{5,4},{6,7},{7,6},{8,9},{9,8},{10,11... | collective-permute-start | bytes 595976 | tf_op jit(solution)/shard_map/ppermute | solution.py:205
  14.5 2.7 %collective-permute-done.4.refs_6_ = bf16[776,128]{1,0:T(8,128)(2,1)S(1)} collective-permute-done((bf16[776,128]{1,0:T(8,128)(2,1)S(1)}, bf16[776,128]{1,0:T(8,128)(2,1)S(1)}, u32[]{:S(2)}, u32[]{:S(2)}) %collective-permute-start.4) | collective-permute-done | bytes 198688 | tf_op jit(solution)/shard_map/ppermute | solution.py:201
  17.2 0.6 %collective-permute-done.2.refs_3_ = bf16[776,128]{1,0:T(8,128)(2,1)S(1)} collective-permute-done((bf16[776,128]{1,0:T(8,128)(2,1)S(1)}, bf16[776,128]{1,0:T(8,128)(2,1)S(1)}, u32[]{:S(2)}, u32[]{:S(2)}) %collective-permute-start.2) | collective-permute-done | bytes 198688 | tf_op jit(solution)/shard_map/ppermute | solution.py:205
  17.7 0.7 %score_late.1 = (f32[3,128]{1,0:T(4,128)S(1)}, f32[4,128]{1,0:T(4,128)S(1)}) custom-call(bf16[776,128]{1,0:T(8,128)(2,1)S(1)} %get-tuple-element.17.refs_0_.refs_4_, bf16[776,128]{1,0:T(8,128)(2,1)S(1)} %collective-permute-done.1.refs_1_, bf16[776,128]{1,0:T(8,128)(2,1)S(1)} %collective-permute-done.refs_1_.refs_2_, ...), custom_call_target="tpu_custom_call" | custom-call | flops 251658240 | bytes 1376256 | tf_op jit(solution)/shard_map/score_late/pallas_call | solution.py:169
  18.4 0.2 collective-permute-done.7.refs_6_
  18.6 0.7 %score_partner.1 = (f32[3,128]{1,0:T(4,128)S(1)}, f32[2,128]{1,0:T(2,128)S(1)}, f32[2,128]{1,0:T(2,128)S(1)}) custom-call(bf16[776,128]{1,0:T(8,128)(2,1)S(1)} %get-tuple-element.17.refs_0_.refs_4_, bf16[776,128]{1,0:T(8,128)(2,1)S(1)} %collective-permute-done.1.refs_1_, bf16[776,128]{1,0:T(8,128)(2,1)S(1)} %collective-permute-done.refs_1_.refs_2_, ...), custom_call_target="tpu_custom_call" | custom-call | flops 301989888 | bytes 1376256 | tf_op jit(solution)/shard_map/score_partner/pallas_call | solution.py:169
  19.4 0.2 collective-permute-start.8
  19.6 1.5 %collective-permute-start.11 = (f32[2,128]{1,0:T(2,128)S(1)}, f32[2,128]{1,0:T(2,128)S(1)}, u32[]{:S(2)}, u32[]{:S(2)}) collective-permute-start(f32[2,128]{1,0:T(2,128)S(1)} %get-tuple-element.26), channel_id=1, source_target_pairs={{0,4},{1,5},{2,6},{3,7},{4,0},{5,1},{6,2},{7,3},{8,12},{9,13},{10,... | collective-permute-start | bytes 3080 | tf_op jit(solution)/shard_map/ppermute | solution.py:205
  21.1 2.4 %collective-permute-start.10 = (f32[1,128]{1,0:T(1,128)S(1)}, f32[1,128]{1,0:T(1,128)S(1)}, u32[]{:S(2)}, u32[]{:S(2)}) collective-permute-start(f32[1,128]{1,0:T(1,128)S(1)} %get-tuple-element.28), channel_id=1, source_target_pairs={{8,0},{9,1},{10,2},{11,3},{12,4},{13,5},{14,6},{15,7},{16,8},{17,9... | collective-permute-start | bytes 1544 | tf_op jit(solution)/shard_map/ppermute | solution.py:201
  23.5 0.4 %collective-permute-start.9 = (f32[1,128]{1,0:T(1,128)S(1)}, f32[1,128]{1,0:T(1,128)S(1)}, u32[]{:S(2)}, u32[]{:S(2)}) collective-permute-start(f32[1,128]{1,0:T(1,128)S(1)} %get-tuple-element.27), channel_id=1, source_target_pairs={{0,16},{1,17},{2,18},{3,19},{4,20},{5,21},{6,22},{7,23},{24,8},{25... | collective-permute-start | bytes 1544 | tf_op jit(solution)/shard_map/ppermute | solution.py:201
  23.9 1.5 %collective-permute-start.12 = (f32[1,128]{1,0:T(1,128)S(1)}, f32[1,128]{1,0:T(1,128)S(1)}, u32[]{:S(2)}, u32[]{:S(2)}) collective-permute-start(f32[1,128]{1,0:T(1,128)S(1)} %slice.19), channel_id=1, source_target_pairs={{0,2},{1,3},{2,0},{3,1},{4,6},{5,7},{6,4},{7,5},{8,10},{9,11},{10,... | collective-permute-start | bytes 1544 | tf_op jit(solution)/shard_map/ppermute | solution.py:205
  25.5 1.6 %collective-permute-done.9 = f32[1,128]{1,0:T(1,128)S(1)} collective-permute-done((f32[1,128]{1,0:T(1,128)S(1)}, f32[1,128]{1,0:T(1,128)S(1)}, u32[]{:S(2)}, u32[]{:S(2)}) %collective-permute-start.9) | collective-permute-done | bytes 544 | tf_op jit(solution)/shard_map/ppermute | solution.py:201
  27.1 0.5 %collective-permute-done.12 = f32[1,128]{1,0:T(1,128)S(1)} collective-permute-done((f32[1,128]{1,0:T(1,128)S(1)}, f32[1,128]{1,0:T(1,128)S(1)}, u32[]{:S(2)}, u32[]{:S(2)}) %collective-permute-start.12) | collective-permute-done | bytes 544 | tf_op jit(solution)/shard_map/ppermute | solution.py:205
  27.6 0.5 %maximum_bitcast_fusion = f32[128]{0:T(128)} fusion(f32[1,128]{1,0:T(1,128)S(1)} %collective-permute-done.12, f32[1,128]{1,0:T(1,128)S(1)} %maximum_maximum_fusion, f32[2,128]{1,0:T(2,128)S(1)} %max.21), kind=kLoop, calls=%fused_computation | loop fusion | flops 256 | bytes 2048 | tf_op jit(solution)/shard_map/reshape | solution.py:249
  (12 shorter events, 0.0 us)
Async XLA Ops:
  2.6 11.3 %collective-permute-start.3 = (bf16[832,128]{1,0:T(8,128)(2,1)S(1)}, bf16[832,128]{1,0:T(8,128)(2,1)S(1)}, u32[]{:S(2)}, u32[]{:S(2)}) collective-permute-start(bf16[832,128]{1,0:T(8,128)(2,1)S(1)} %get-tuple-element.18), channel_id=1, source_target_pairs={{0,8},{1,9},{2,10},{3,11},{4,12},{5,13},{6,14},{7,15},{8,16},{9,17... | collective-permute-start | bytes 638984 | tf_op jit(solution)/shard_map/ppermute | solution.py:201
  5.6 6.4 %collective-permute-start = (bf16[776,128]{1,0:T(8,128)(2,1)S(1)}, bf16[776,128]{1,0:T(8,128)(2,1)S(1)}, u32[]{:S(2)}, u32[]{:S(2)}) collective-permute-start(bf16[776,128]{1,0:T(8,128)(2,1)S(1)} %get-tuple-element.16.refs_0_.refs_2_), channel_id=1, source_target_pairs={{0,4},{1,5},{2,6},{3,7},{4,0},{5,1},{6,2},{7,3},{8,12},{9,13},{10,... | collective-permute-start | bytes 595976 | tf_op jit(solution)/shard_map/ppermute | solution.py:205
  7.2 7.3 %collective-permute-start.1 = (bf16[776,128]{1,0:T(8,128)(2,1)S(1)}, bf16[776,128]{1,0:T(8,128)(2,1)S(1)}, u32[]{:S(2)}, u32[]{:S(2)}) collective-permute-start(bf16[776,128]{1,0:T(8,128)(2,1)S(1)} %get-tuple-element.16.refs_0_.refs_2_), channel_id=1, source_target_pairs={{0,2},{1,3},{2,0},{3,1},{4,6},{5,7},{6,4},{7,5},{8,10},{9,11},{10,... | collective-permute-start | bytes 595976 | tf_op jit(solution)/shard_map/ppermute | solution.py:205
  8.7 8.5 %collective-permute-start.4 = (bf16[776,128]{1,0:T(8,128)(2,1)S(1)}, bf16[776,128]{1,0:T(8,128)(2,1)S(1)}, u32[]{:S(2)}, u32[]{:S(2)}) collective-permute-start(bf16[776,128]{1,0:T(8,128)(2,1)S(1)} %get-tuple-element.16.refs_0_.refs_2_), channel_id=1, source_target_pairs={{16,0},{17,1},{18,2},{19,3},{20,4},{21,5},{22,6},{23,7},{8,24},{9,... | collective-permute-start | bytes 595976 | tf_op jit(solution)/shard_map/ppermute | solution.py:201
  12.1 5.7 %collective-permute-start.2 = (bf16[776,128]{1,0:T(8,128)(2,1)S(1)}, bf16[776,128]{1,0:T(8,128)(2,1)S(1)}, u32[]{:S(2)}, u32[]{:S(2)}) collective-permute-start(bf16[776,128]{1,0:T(8,128)(2,1)S(1)} %collective-permute-done.refs_1_.refs_2_), channel_id=1, source_target_pairs={{0,2},{1,3},{2,0},{3,1},{4,6},{5,7},{6,4},{7,5},{8,10},{9,11},{10,... | collective-permute-start | bytes 595976 | tf_op jit(solution)/shard_map/ppermute | solution.py:205
  13.9 4.7 %collective-permute-start.6 = (bf16[832,128]{1,0:T(8,128)(2,1)S(1)}, bf16[832,128]{1,0:T(8,128)(2,1)S(1)}, u32[]{:S(2)}, u32[]{:S(2)}) collective-permute-start(bf16[832,128]{1,0:T(8,128)(2,1)S(1)} %collective-permute-done.3.refs_5_), channel_id=1, source_target_pairs={{0,1},{1,0},{2,3},{3,2},{4,5},{5,4},{6,7},{7,6},{8,9},{9,8},{10,11... | collective-permute-start | bytes 638984 | tf_op jit(solution)/shard_map/ppermute | solution.py:205
  14.0 4.5 %collective-permute-start.5 = (bf16[776,128]{1,0:T(8,128)(2,1)S(1)}, bf16[776,128]{1,0:T(8,128)(2,1)S(1)}, u32[]{:S(2)}, u32[]{:S(2)}) collective-permute-start(bf16[776,128]{1,0:T(8,128)(2,1)S(1)} %get-tuple-element.17.refs_0_.refs_4_), channel_id=1, source_target_pairs={{0,1},{1,0},{2,3},{3,2},{4,5},{5,4},{6,7},{7,6},{8,9},{9,8},{10,11... | collective-permute-start | bytes 595976 | tf_op jit(solution)/shard_map/ppermute | solution.py:205
  17.2 1.4 %collective-permute-start.7 = (bf16[776,128]{1,0:T(8,128)(2,1)S(1)}, bf16[776,128]{1,0:T(8,128)(2,1)S(1)}, u32[]{:S(2)}, u32[]{:S(2)}) collective-permute-start(bf16[776,128]{1,0:T(8,128)(2,1)S(1)} %collective-permute-done.4.refs_6_), channel_id=1, source_target_pairs={{0,1},{1,0},{2,3},{3,2},{4,5},{5,4},{6,7},{7,6},{8,9},{9,8},{10,11... | collective-permute-start | bytes 595976 | tf_op jit(solution)/shard_map/ppermute | solution.py:205
  19.4 1.7 %collective-permute-start.8 = (f32[3,128]{1,0:T(4,128)S(1)}, f32[3,128]{1,0:T(4,128)S(1)}, u32[]{:S(2)}, u32[]{:S(2)}) collective-permute-start(f32[3,128]{1,0:T(4,128)S(1)} %get-tuple-element.24), channel_id=1, source_target_pairs={{0,1},{1,0},{2,3},{3,2},{4,5},{5,4},{6,7},{7,6},{8,9},{9,8},{10,11... | collective-permute-start | bytes 4616 | tf_op jit(solution)/shard_map/ppermute | solution.py:205
  19.6 4.4 %collective-permute-start.11 = (f32[2,128]{1,0:T(2,128)S(1)}, f32[2,128]{1,0:T(2,128)S(1)}, u32[]{:S(2)}, u32[]{:S(2)}) collective-permute-start(f32[2,128]{1,0:T(2,128)S(1)} %get-tuple-element.26), channel_id=1, source_target_pairs={{0,4},{1,5},{2,6},{3,7},{4,0},{5,1},{6,2},{7,3},{8,12},{9,13},{10,... | collective-permute-start | bytes 3080 | tf_op jit(solution)/shard_map/ppermute | solution.py:205
  21.1 4.4 %collective-permute-start.10 = (f32[1,128]{1,0:T(1,128)S(1)}, f32[1,128]{1,0:T(1,128)S(1)}, u32[]{:S(2)}, u32[]{:S(2)}) collective-permute-start(f32[1,128]{1,0:T(1,128)S(1)} %get-tuple-element.28), channel_id=1, source_target_pairs={{8,0},{9,1},{10,2},{11,3},{12,4},{13,5},{14,6},{15,7},{16,8},{17,9... | collective-permute-start | bytes 1544 | tf_op jit(solution)/shard_map/ppermute | solution.py:201
  23.5 3.5 %collective-permute-start.9 = (f32[1,128]{1,0:T(1,128)S(1)}, f32[1,128]{1,0:T(1,128)S(1)}, u32[]{:S(2)}, u32[]{:S(2)}) collective-permute-start(f32[1,128]{1,0:T(1,128)S(1)} %get-tuple-element.27), channel_id=1, source_target_pairs={{0,16},{1,17},{2,18},{3,19},{4,20},{5,21},{6,22},{7,23},{24,8},{25... | collective-permute-start | bytes 1544 | tf_op jit(solution)/shard_map/ppermute | solution.py:201
  23.9 3.6 %collective-permute-start.12 = (f32[1,128]{1,0:T(1,128)S(1)}, f32[1,128]{1,0:T(1,128)S(1)}, u32[]{:S(2)}, u32[]{:S(2)}) collective-permute-start(f32[1,128]{1,0:T(1,128)S(1)} %slice.19), channel_id=1, source_target_pairs={{0,2},{1,3},{2,0},{3,1},{4,6},{5,7},{6,4},{7,5},{8,10},{9,11},{10,... | collective-permute-start | bytes 1544 | tf_op jit(solution)/shard_map/ppermute | solution.py:205

commit v6 on v5

--- a/solution.py
+++ b/solution.py
@@ -9,7 +9,7 @@
 
 AXES = ("line", "mid", "grp")
 NOTE_ROWS = 8
-MORE_ROWS = 56
+MORE_ROWS = 48
 RADIX = 256
 CHUNKS = 4
 VMEM = pl.BlockSpec(memory_space=pltpu.VMEM)
@@ -222,17 +222,15 @@
     lanes = [block] + visitors
     every, count = tuple(range(len(lanes))), len(row_blocks)
     half = count // 2
-    soon = (0, half)
-    rest = tuple(i for i in range(count) if i not in soon)
-    lines, held = score(
-        "score_soon", [row_blocks[i] for i in soon], lanes[:1], [((0, 1), (0,))], [], hold=True
+    soon, early = tuple(range(half + 1)), every[:-1]
+    rest = tuple(range(half + 1, count))
+    lines, backs, held = score(
+        "score_soon", [row_blocks[i] for i in soon], lanes[:-1], [(soon, early)], [(0, count)], hold=True
     )
     row_blocks[0] = lanes[0] = held
-    products = [(rest, every), (soon, every[1:])]
-    lines, backs = score("score_late", row_blocks, lanes, products, [(0, count)], lines)
-    partner = [held]
-    partner += [lax.optimization_barrier((visitor, held))[0] for visitor in visitors[:-1]]
-    partner += [lax.optimization_barrier((visitors[-1], row_blocks[1]))[0]]
+    products = [(rest, every), (soon, every[-1:])]
+    lines, backs = score("score_late", row_blocks, lanes, products, [(0, count)], lines, backs)
+    partner = [block, *visitors[:-1], lax.optimization_barrier((visitors[-1], held))[0]]
     partner = [swap(lane, 1) for lane in partner]
     products, parts = [(tuple(range(count)), every)], [(0, half), (half, count)]
     theirs, near, far = score("score_partner", row_blocks, partner, products, parts, None, backs)

time: 28.2 us -> 29 us (1.028)
  waiting for transfers between devices: 7.39 us -> 7.75 us
  starting transfers between devices: 15.8 us -> 16.1 us
    ppermute x9, waiting for transfers between devices: 3.09 us -> 4.09 us  [swap(): return lax.ppermute(array, AXES, pairs)]
    ppermute x4, starting transfers between devices: 7.49 us -> 8.36 us  [move(): return lax.ppermute(array, AXES, whole)]
    ppermute x4, waiting for transfers between devices: 4.3 us -> 3.67 us  [move(): return lax.ppermute(array, AXES, whole)]
    ppermute x9, starting transfers between devices: 8.3 us -> 7.75 us  [swap(): return lax.ppermute(array, AXES, pairs)]
where the time goes in v6:
time: 29 us; the launch traced here: 28.9 us
  starting transfers between devices  16.1 us (56%)
  waiting for transfers between devices  7.75 us (27%)
  Pallas kernels  4.47 us (15%)
  other arithmetic  0.52 us (2%)
    ppermute x4, starting transfers between devices, move(): return lax.ppermute(array, AXES, whole)  8.36 us
    ppermute x9, starting transfers between devices, swap(): return lax.ppermute(array, AXES, pairs)  7.75 us
    ppermute x9, waiting for transfers between devices, swap(): return lax.ppermute(array, AXES, pairs)  4.09 us
    ppermute x4, waiting for transfers between devices, move(): return lax.ppermute(array, AXES, whole)  3.67 us
    pallas_call x1, Pallas kernels, embed(): pl.pallas_call(embed_kernel, in_specs=[HBM] * 5, out_specs=[VMEM] * 2, ou...  2.56 us
    pallas_call x3, Pallas kernels, score(): pl.pallas_call(lambda *refs: score_kernel(*counts, *rest, *refs), in_spec...  1.91 us
  transfers between devices with their start and end apart: 13, of which 6 were waited for; matrix products, arithmetic and copies ran while one was open for 0% of the time, Pallas kernels for 4%

profile of v6, /device:TPU:0, one launch (start us, length us, event | category | flops | bytes accessed | tf_op | source)
XLA Modules:
  0.0 28.9 jit_solution(8593179309301329299)
XLA Ops:
  0.0 2.6 %embed.1 = (bf16[776,128]{1,0:T(8,128)(2,1)S(1)}, bf16[824,128]{1,0:T(8,128)(2,1)S(1)}) custom-call(bf16[128,2048]{1,0:T(8,128)(2,1)} %states_hbm.1, bf16[2048,768]{1,0:T(8,128)(2,1)} %proj_hbm.1, s32[1,128]{1,0:T(1,128)} %bitcast.5, s32[1,128]{1,0:T(1,128)} %bitcast.6, s32[1,128]{1,0:T(1,128)} %bitcast.7), custom_call_target="tpu_custom_call" | custom-call | tf_op jit(solution)/shard_map/embed/pallas_call | solution.py:66
  2.6 3.1 %collective-permute-start.2 = (bf16[824,128]{1,0:T(8,128)(2,1)S(1)}, bf16[824,128]{1,0:T(8,128)(2,1)S(1)}, u32[]{:S(2)}, u32[]{:S(2)}) collective-permute-start(bf16[824,128]{1,0:T(8,128)(2,1)S(1)} %get-tuple-element.17), channel_id=1, source_target_pairs={{0,8},{1,9},{2,10},{3,11},{4,12},{5,13},{6,14},{7,15},{8,16},{9,17... | collective-permute-start | bytes 632840 | tf_op jit(solution)/shard_map/ppermute | solution.py:201
  5.6 1.5 %collective-permute-start.1 = (bf16[776,128]{1,0:T(8,128)(2,1)S(1)}, bf16[776,128]{1,0:T(8,128)(2,1)S(1)}, u32[]{:S(2)}, u32[]{:S(2)}) collective-permute-start(bf16[776,128]{1,0:T(8,128)(2,1)S(1)} %get-tuple-element.16.refs_0_.refs_3_), channel_id=1, source_target_pairs={{0,4},{1,5},{2,6},{3,7},{4,0},{5,1},{6,2},{7,3},{8,12},{9,13},{10,... | collective-permute-start | bytes 595976 | tf_op jit(solution)/shard_map/ppermute | solution.py:205
  7.2 1.5 %collective-permute-start = (bf16[776,128]{1,0:T(8,128)(2,1)S(1)}, bf16[776,128]{1,0:T(8,128)(2,1)S(1)}, u32[]{:S(2)}, u32[]{:S(2)}) collective-permute-start(bf16[776,128]{1,0:T(8,128)(2,1)S(1)} %get-tuple-element.16.refs_0_.refs_3_), channel_id=1, source_target_pairs={{0,2},{1,3},{2,0},{3,1},{4,6},{5,7},{6,4},{7,5},{8,10},{9,11},{10,... | collective-permute-start | bytes 595976 | tf_op jit(solution)/shard_map/ppermute | solution.py:205
  8.7 1.6 %collective-permute-start.4 = (bf16[776,128]{1,0:T(8,128)(2,1)S(1)}, bf16[776,128]{1,0:T(8,128)(2,1)S(1)}, u32[]{:S(2)}, u32[]{:S(2)}) collective-permute-start(bf16[776,128]{1,0:T(8,128)(2,1)S(1)} %get-tuple-element.16.refs_0_.refs_3_), channel_id=1, source_target_pairs={{16,0},{17,1},{18,2},{19,3},{20,4},{21,5},{22,6},{23,7},{8,24},{9,... | collective-permute-start | bytes 595976 | tf_op jit(solution)/shard_map/ppermute | solution.py:201
  10.2 1.8 %collective-permute-done.1.refs_2_ = bf16[776,128]{1,0:T(8,128)(2,1)S(1)} collective-permute-done((bf16[776,128]{1,0:T(8,128)(2,1)S(1)}, bf16[776,128]{1,0:T(8,128)(2,1)S(1)}, u32[]{:S(2)}, u32[]{:S(2)}) %collective-permute-start.1) | collective-permute-done | bytes 198688 | tf_op jit(solution)/shard_map/ppermute | solution.py:205
  12.1 1.5 %collective-permute-start.3 = (bf16[776,128]{1,0:T(8,128)(2,1)S(1)}, bf16[776,128]{1,0:T(8,128)(2,1)S(1)}, u32[]{:S(2)}, u32[]{:S(2)}) collective-permute-start(bf16[776,128]{1,0:T(8,128)(2,1)S(1)} %collective-permute-done.1.refs_2_), channel_id=1, source_target_pairs={{0,2},{1,3},{2,0},{3,1},{4,6},{5,7},{6,4},{7,5},{8,10},{9,11},{10,... | collective-permute-start | bytes 595976 | tf_op jit(solution)/shard_map/ppermute | solution.py:205
  13.5 0.6 %score_soon.1 = (f32[2,128]{1,0:T(2,128)S(1)}, f32[4,128]{1,0:T(4,128)S(1)}, bf16[776,128]{1,0:T(8,128)(2,1)S(1)}) custom-call(bf16[776,128]{1,0:T(8,128)(2,1)S(1)} %get-tuple-element.16.refs_0_.refs_3_, bf16[776,128]{1,0:T(8,128)(2,1)S(1)} %collective-permute-done.refs_1_, bf16[776,128]{1,0:T(8,128)(2,1)S(1)} %collective-permute-done.1.refs_2_, ...), custom_call_target="tpu_custom_call" | custom-call | flops 150994944 | bytes 983040 | tf_op jit(solution)/shard_map/score_soon/pallas_call | solution.py:169
  14.1 3.0 %collective-permute-done.4.refs_6_ = bf16[776,128]{1,0:T(8,128)(2,1)S(1)} collective-permute-done((bf16[776,128]{1,0:T(8,128)(2,1)S(1)}, bf16[776,128]{1,0:T(8,128)(2,1)S(1)}, u32[]{:S(2)}, u32[]{:S(2)}) %collective-permute-start.4) | collective-permute-done | bytes 198688 | tf_op jit(solution)/shard_map/ppermute | solution.py:201
  17.1 0.0 collective-permute-start.7
  17.1 0.6 %collective-permute-done.3.refs_3_ = bf16[776,128]{1,0:T(8,128)(2,1)S(1)} collective-permute-done((bf16[776,128]{1,0:T(8,128)(2,1)S(1)}, bf16[776,128]{1,0:T(8,128)(2,1)S(1)}, u32[]{:S(2)}, u32[]{:S(2)}) %collective-permute-start.3) | collective-permute-done | bytes 198688 | tf_op jit(solution)/shard_map/ppermute | solution.py:205
  17.7 0.6 %score_late.1 = (f32[3,128]{1,0:T(4,128)S(1)}, f32[4,128]{1,0:T(4,128)S(1)}) custom-call(bf16[776,128]{1,0:T(8,128)(2,1)S(1)} %get-tuple-element.18.refs_0_.refs_4_, bf16[776,128]{1,0:T(8,128)(2,1)S(1)} %collective-permute-done.refs_1_, bf16[776,128]{1,0:T(8,128)(2,1)S(1)} %collective-permute-done.1.refs_2_, ...), custom_call_target="tpu_custom_call" | custom-call | flops 150994944 | bytes 1376256 | tf_op jit(solution)/shard_map/score_late/pallas_call | solution.py:169
  18.4 0.0 collective-permute-done.5.refs_4_
  18.4 0.2 collective-permute-done.7.refs_6_
  18.6 0.8 %score_partner.1 = (f32[3,128]{1,0:T(4,128)S(1)}, f32[2,128]{1,0:T(2,128)S(1)}, f32[2,128]{1,0:T(2,128)S(1)}) custom-call(bf16[776,128]{1,0:T(8,128)(2,1)S(1)} %get-tuple-element.18.refs_0_.refs_4_, bf16[776,128]{1,0:T(8,128)(2,1)S(1)} %collective-permute-done.refs_1_, bf16[776,128]{1,0:T(8,128)(2,1)S(1)} %collective-permute-done.1.refs_2_, ...), custom_call_target="tpu_custom_call" | custom-call | flops 301989888 | bytes 1376256 | tf_op jit(solution)/shard_map/score_partner/pallas_call | solution.py:169
  19.3 0.2 collective-permute-start.8
  19.5 1.5 %collective-permute-start.11 = (f32[2,128]{1,0:T(2,128)S(1)}, f32[2,128]{1,0:T(2,128)S(1)}, u32[]{:S(2)}, u32[]{:S(2)}) collective-permute-start(f32[2,128]{1,0:T(2,128)S(1)} %get-tuple-element.26), channel_id=1, source_target_pairs={{0,4},{1,5},{2,6},{3,7},{4,0},{5,1},{6,2},{7,3},{8,12},{9,13},{10,... | collective-permute-start | bytes 3080 | tf_op jit(solution)/shard_map/ppermute | solution.py:205
  21.0 0.0 collective-permute-done.8
  21.1 2.4 %collective-permute-start.9 = (f32[1,128]{1,0:T(1,128)S(1)}, f32[1,128]{1,0:T(1,128)S(1)}, u32[]{:S(2)}, u32[]{:S(2)}) collective-permute-start(f32[1,128]{1,0:T(1,128)S(1)} %get-tuple-element.27), channel_id=1, source_target_pairs={{0,16},{1,17},{2,18},{3,19},{4,20},{5,21},{6,22},{7,23},{24,8},{25... | collective-permute-start | bytes 1544 | tf_op jit(solution)/shard_map/ppermute | solution.py:201
  23.4 1.4 %collective-permute-start.10 = (f32[1,128]{1,0:T(1,128)S(1)}, f32[1,128]{1,0:T(1,128)S(1)}, u32[]{:S(2)}, u32[]{:S(2)}) collective-permute-start(f32[1,128]{1,0:T(1,128)S(1)} %get-tuple-element.28), channel_id=1, source_target_pairs={{8,0},{9,1},{10,2},{11,3},{12,4},{13,5},{14,6},{15,7},{16,8},{17,9... | collective-permute-start | bytes 1544 | tf_op jit(solution)/shard_map/ppermute | solution.py:201
  24.8 1.5 %collective-permute-start.12 = (f32[1,128]{1,0:T(1,128)S(1)}, f32[1,128]{1,0:T(1,128)S(1)}, u32[]{:S(2)}, u32[]{:S(2)}) collective-permute-start(f32[1,128]{1,0:T(1,128)S(1)} %slice.19), channel_id=1, source_target_pairs={{0,2},{1,3},{2,0},{3,1},{4,6},{5,7},{6,4},{7,5},{8,10},{9,11},{10,... | collective-permute-start | bytes 1544 | tf_op jit(solution)/shard_map/ppermute | solution.py:205
  26.3 0.6 %collective-permute-done.10 = f32[1,128]{1,0:T(1,128)S(1)} collective-permute-done((f32[1,128]{1,0:T(1,128)S(1)}, f32[1,128]{1,0:T(1,128)S(1)}, u32[]{:S(2)}, u32[]{:S(2)}) %collective-permute-start.10) | collective-permute-done | bytes 544 | tf_op jit(solution)/shard_map/ppermute | solution.py:201
  27.0 1.4 %collective-permute-done.12 = f32[1,128]{1,0:T(1,128)S(1)} collective-permute-done((f32[1,128]{1,0:T(1,128)S(1)}, f32[1,128]{1,0:T(1,128)S(1)}, u32[]{:S(2)}, u32[]{:S(2)}) %collective-permute-start.12) | collective-permute-done | bytes 544 | tf_op jit(solution)/shard_map/ppermute | solution.py:205
  28.4 0.5 %maximum_bitcast_fusion = f32[128]{0:T(128)} fusion(f32[1,128]{1,0:T(1,128)S(1)} %collective-permute-done.12, f32[1,128]{1,0:T(1,128)S(1)} %maximum_maximum_fusion, f32[2,128]{1,0:T(2,128)S(1)} %max.21), kind=kLoop, calls=%fused_computation | loop fusion | flops 256 | bytes 2048 | tf_op jit(solution)/shard_map/reshape | solution.py:247
  (12 shorter events, 0.0 us)
Async XLA Ops:
  2.6 11.0 %collective-permute-start.2 = (bf16[824,128]{1,0:T(8,128)(2,1)S(1)}, bf16[824,128]{1,0:T(8,128)(2,1)S(1)}, u32[]{:S(2)}, u32[]{:S(2)}) collective-permute-start(bf16[824,128]{1,0:T(8,128)(2,1)S(1)} %get-tuple-element.17), channel_id=1, source_target_pairs={{0,8},{1,9},{2,10},{3,11},{4,12},{5,13},{6,14},{7,15},{8,16},{9,17... | collective-permute-start | bytes 632840 | tf_op jit(solution)/shard_map/ppermute | solution.py:201
  5.6 6.4 %collective-permute-start.1 = (bf16[776,128]{1,0:T(8,128)(2,1)S(1)}, bf16[776,128]{1,0:T(8,128)(2,1)S(1)}, u32[]{:S(2)}, u32[]{:S(2)}) collective-permute-start(bf16[776,128]{1,0:T(8,128)(2,1)S(1)} %get-tuple-element.16.refs_0_.refs_3_), channel_id=1, source_target_pairs={{0,4},{1,5},{2,6},{3,7},{4,0},{5,1},{6,2},{7,3},{8,12},{9,13},{10,... | collective-permute-start | bytes 595976 | tf_op jit(solution)/shard_map/ppermute | solution.py:205
  7.2 6.4 %collective-permute-start = (bf16[776,128]{1,0:T(8,128)(2,1)S(1)}, bf16[776,128]{1,0:T(8,128)(2,1)S(1)}, u32[]{:S(2)}, u32[]{:S(2)}) collective-permute-start(bf16[776,128]{1,0:T(8,128)(2,1)S(1)} %get-tuple-element.16.refs_0_.refs_3_), channel_id=1, source_target_pairs={{0,2},{1,3},{2,0},{3,1},{4,6},{5,7},{6,4},{7,5},{8,10},{9,11},{10,... | collective-permute-start | bytes 595976 | tf_op jit(solution)/shard_map/ppermute | solution.py:205
  8.7 8.5 %collective-permute-start.4 = (bf16[776,128]{1,0:T(8,128)(2,1)S(1)}, bf16[776,128]{1,0:T(8,128)(2,1)S(1)}, u32[]{:S(2)}, u32[]{:S(2)}) collective-permute-start(bf16[776,128]{1,0:T(8,128)(2,1)S(1)} %get-tuple-element.16.refs_0_.refs_3_), channel_id=1, source_target_pairs={{16,0},{17,1},{18,2},{19,3},{20,4},{21,5},{22,6},{23,7},{8,24},{9,... | collective-permute-start | bytes 595976 | tf_op jit(solution)/shard_map/ppermute | solution.py:201
  10.2 8.1 %collective-permute-start.5 = (bf16[776,128]{1,0:T(8,128)(2,1)S(1)}, bf16[776,128]{1,0:T(8,128)(2,1)S(1)}, u32[]{:S(2)}, u32[]{:S(2)}) collective-permute-start(bf16[776,128]{1,0:T(8,128)(2,1)S(1)} %get-tuple-element.16.refs_0_.refs_3_), channel_id=1, source_target_pairs={{0,1},{1,0},{2,3},{3,2},{4,5},{5,4},{6,7},{7,6},{8,9},{9,8},{10,11... | collective-permute-start | bytes 595976 | tf_op jit(solution)/shard_map/ppermute | solution.py:205
  12.1 5.7 %collective-permute-start.3 = (bf16[776,128]{1,0:T(8,128)(2,1)S(1)}, bf16[776,128]{1,0:T(8,128)(2,1)S(1)}, u32[]{:S(2)}, u32[]{:S(2)}) collective-permute-start(bf16[776,128]{1,0:T(8,128)(2,1)S(1)} %collective-permute-done.1.refs_2_), channel_id=1, source_target_pairs={{0,2},{1,3},{2,0},{3,1},{4,6},{5,7},{6,4},{7,5},{8,10},{9,11},{10,... | collective-permute-start | bytes 595976 | tf_op jit(solution)/shard_map/ppermute | solution.py:205
  13.5 5.0 %collective-permute-start.6 = (bf16[824,128]{1,0:T(8,128)(2,1)S(1)}, bf16[824,128]{1,0:T(8,128)(2,1)S(1)}, u32[]{:S(2)}, u32[]{:S(2)}) collective-permute-start(bf16[824,128]{1,0:T(8,128)(2,1)S(1)} %collective-permute-done.2.refs_4_.refs_5_), channel_id=1, source_target_pairs={{0,1},{1,0},{2,3},{3,2},{4,5},{5,4},{6,7},{7,6},{8,9},{9,8},{10,11... | collective-permute-start | bytes 632840 | tf_op jit(solution)/shard_map/ppermute | solution.py:205
  17.1 1.4 %collective-permute-start.7 = (bf16[776,128]{1,0:T(8,128)(2,1)S(1)}, bf16[776,128]{1,0:T(8,128)(2,1)S(1)}, u32[]{:S(2)}, u32[]{:S(2)}) collective-permute-start(bf16[776,128]{1,0:T(8,128)(2,1)S(1)} %collective-permute-done.4.refs_6_), channel_id=1, source_target_pairs={{0,1},{1,0},{2,3},{3,2},{4,5},{5,4},{6,7},{7,6},{8,9},{9,8},{10,11... | collective-permute-start | bytes 595976 | tf_op jit(solution)/shard_map/ppermute | solution.py:205
  19.3 1.7 %collective-permute-start.8 = (f32[3,128]{1,0:T(4,128)S(1)}, f32[3,128]{1,0:T(4,128)S(1)}, u32[]{:S(2)}, u32[]{:S(2)}) collective-permute-start(f32[3,128]{1,0:T(4,128)S(1)} %get-tuple-element.24), channel_id=1, source_target_pairs={{0,1},{1,0},{2,3},{3,2},{4,5},{5,4},{6,7},{7,6},{8,9},{9,8},{10,11... | collective-permute-start | bytes 4616 | tf_op jit(solution)/shard_map/ppermute | solution.py:205
  19.5 5.3 %collective-permute-start.11 = (f32[2,128]{1,0:T(2,128)S(1)}, f32[2,128]{1,0:T(2,128)S(1)}, u32[]{:S(2)}, u32[]{:S(2)}) collective-permute-start(f32[2,128]{1,0:T(2,128)S(1)} %get-tuple-element.26), channel_id=1, source_target_pairs={{0,4},{1,5},{2,6},{3,7},{4,0},{5,1},{6,2},{7,3},{8,12},{9,13},{10,... | collective-permute-start | bytes 3080 | tf_op jit(solution)/shard_map/ppermute | solution.py:205
  21.1 5.3 %collective-permute-start.9 = (f32[1,128]{1,0:T(1,128)S(1)}, f32[1,128]{1,0:T(1,128)S(1)}, u32[]{:S(2)}, u32[]{:S(2)}) collective-permute-start(f32[1,128]{1,0:T(1,128)S(1)} %get-tuple-element.27), channel_id=1, source_target_pairs={{0,16},{1,17},{2,18},{3,19},{4,20},{5,21},{6,22},{7,23},{24,8},{25... | collective-permute-start | bytes 1544 | tf_op jit(solution)/shard_map/ppermute | solution.py:201
  23.4 3.5 %collective-permute-start.10 = (f32[1,128]{1,0:T(1,128)S(1)}, f32[1,128]{1,0:T(1,128)S(1)}, u32[]{:S(2)}, u32[]{:S(2)}) collective-permute-start(f32[1,128]{1,0:T(1,128)S(1)} %get-tuple-element.28), channel_id=1, source_target_pairs={{8,0},{9,1},{10,2},{11,3},{12,4},{13,5},{14,6},{15,7},{16,8},{17,9... | collective-permute-start | bytes 1544 | tf_op jit(solution)/shard_map/ppermute | solution.py:201
  24.8 3.6 %collective-permute-start.12 = (f32[1,128]{1,0:T(1,128)S(1)}, f32[1,128]{1,0:T(1,128)S(1)}, u32[]{:S(2)}, u32[]{:S(2)}) collective-permute-start(f32[1,128]{1,0:T(1,128)S(1)} %slice.19), channel_id=1, source_target_pairs={{0,2},{1,3},{2,0},{3,1},{4,6},{5,7},{6,4},{7,5},{8,10},{9,11},{10,... | collective-permute-start | bytes 1544 | tf_op jit(solution)/shard_map/ppermute | solution.py:205

commit v7 on v5

--- a/solution.py
+++ b/solution.py
@@ -9,7 +9,7 @@
 
 AXES = ("line", "mid", "grp")
 NOTE_ROWS = 8
-MORE_ROWS = 56
+MORE_ROWS = 48
 RADIX = 256
 CHUNKS = 4
 VMEM = pl.BlockSpec(memory_space=pltpu.VMEM)
@@ -34,7 +34,10 @@
         pltpu.make_async_copy(src, dst, small_sem.at[i])
         for i, (src, dst) in enumerate(((owner_hbm, owner), (sub_hbm, sub), (prio_hbm, prio)))
     ]
-    for copy in [whole] + copies + small:
+    whole.start(priority=1)
+    for i, copy in enumerate(copies):
+        copy.start(priority=1 if i < CHUNKS // 2 else 0)
+    for copy in small:
         copy.start()
     whole.wait()
     projected = None

time: 28.2 us -> 28.7 us (1.018)
  Pallas kernels: 4.31 us -> 4.81 us
    pallas_call x1, Pallas kernels: 2.56 us -> 3.07 us  [embed(): pl.pallas_call(embed_kernel, in_specs=[HBM] * 5, out_specs=[VMEM] * 2, ou...]
  transfers between devices with their start and end apart: 13 -> 13, of which waited for: 6 -> 6; matrix products, arithmetic and copies ran while one was open for 0% -> 0% of each run, Pallas kernels for 4% -> 3%
where the time goes in v7:
time: 28.7 us; the launch traced here: 28.6 us
  starting transfers between devices  15.9 us (55%)
  waiting for transfers between devices  7.32 us (26%)
  Pallas kernels  4.81 us (17%)
  other arithmetic  0.52 us (2%)
    ppermute x9, starting transfers between devices, swap(): return lax.ppermute(array, AXES, pairs)  8.34 us
    ppermute x4, starting transfers between devices, move(): return lax.ppermute(array, AXES, whole)  7.53 us
    ppermute x4, waiting for transfers between devices, move(): return lax.ppermute(array, AXES, whole)  4.19 us
    ppermute x9, waiting for transfers between devices, swap(): return lax.ppermute(array, AXES, pairs)  3.12 us
    pallas_call x1, Pallas kernels, embed(): pl.pallas_call(embed_kernel, in_specs=[HBM] * 5, out_specs=[VMEM] * 2, ou...  3.07 us
    pallas_call x3, Pallas kernels, score(): pl.pallas_call(lambda *refs: score_kernel(*counts, *rest, *refs), in_spec...  1.74 us
  transfers between devices with their start and end apart: 13, of which 6 were waited for; matrix products, arithmetic and copies ran while one was open for 0% of the time, Pallas kernels for 3%

profile of v7, /device:TPU:0, one launch (start us, length us, event | category | flops | bytes accessed | tf_op | source)
XLA Modules:
  0.0 28.6 jit_solution(16411898042438271267)
XLA Ops:
  0.0 3.1 %embed.1 = (bf16[776,128]{1,0:T(8,128)(2,1)S(1)}, bf16[824,128]{1,0:T(8,128)(2,1)S(1)}) custom-call(bf16[128,2048]{1,0:T(8,128)(2,1)} %states_hbm.1, bf16[2048,768]{1,0:T(8,128)(2,1)} %proj_hbm.1, s32[1,128]{1,0:T(1,128)} %bitcast.5, s32[1,128]{1,0:T(1,128)} %bitcast.6, s32[1,128]{1,0:T(1,128)} %bitcast.7), custom_call_target="tpu_custom_call" | custom-call | tf_op jit(solution)/shard_map/embed/pallas_call | solution.py:69
  3.1 3.1 %collective-permute-start.3 = (bf16[824,128]{1,0:T(8,128)(2,1)S(1)}, bf16[824,128]{1,0:T(8,128)(2,1)S(1)}, u32[]{:S(2)}, u32[]{:S(2)}) collective-permute-start(bf16[824,128]{1,0:T(8,128)(2,1)S(1)} %get-tuple-element.18), channel_id=1, source_target_pairs={{0,8},{1,9},{2,10},{3,11},{4,12},{5,13},{6,14},{7,15},{8,16},{9,17... | collective-permute-start | bytes 632840 | tf_op jit(solution)/shard_map/ppermute | solution.py:204
  6.2 1.5 %collective-permute-start = (bf16[776,128]{1,0:T(8,128)(2,1)S(1)}, bf16[776,128]{1,0:T(8,128)(2,1)S(1)}, u32[]{:S(2)}, u32[]{:S(2)}) collective-permute-start(bf16[776,128]{1,0:T(8,128)(2,1)S(1)} %get-tuple-element.16.refs_0_.refs_2_), channel_id=1, source_target_pairs={{0,4},{1,5},{2,6},{3,7},{4,0},{5,1},{6,2},{7,3},{8,12},{9,13},{10,... | collective-permute-start | bytes 595976 | tf_op jit(solution)/shard_map/ppermute | solution.py:208
  7.7 1.5 %collective-permute-start.1 = (bf16[776,128]{1,0:T(8,128)(2,1)S(1)}, bf16[776,128]{1,0:T(8,128)(2,1)S(1)}, u32[]{:S(2)}, u32[]{:S(2)}) collective-permute-start(bf16[776,128]{1,0:T(8,128)(2,1)S(1)} %get-tuple-element.16.refs_0_.refs_2_), channel_id=1, source_target_pairs={{0,2},{1,3},{2,0},{3,1},{4,6},{5,7},{6,4},{7,5},{8,10},{9,11},{10,... | collective-permute-start | bytes 595976 | tf_op jit(solution)/shard_map/ppermute | solution.py:208
  9.2 1.6 %collective-permute-start.4 = (bf16[776,128]{1,0:T(8,128)(2,1)S(1)}, bf16[776,128]{1,0:T(8,128)(2,1)S(1)}, u32[]{:S(2)}, u32[]{:S(2)}) collective-permute-start(bf16[776,128]{1,0:T(8,128)(2,1)S(1)} %get-tuple-element.16.refs_0_.refs_2_), channel_id=1, source_target_pairs={{16,0},{17,1},{18,2},{19,3},{20,4},{21,5},{22,6},{23,7},{8,24},{9,... | collective-permute-start | bytes 595976 | tf_op jit(solution)/shard_map/ppermute | solution.py:204
  10.7 1.8 %collective-permute-done.refs_1_.refs_2_ = bf16[776,128]{1,0:T(8,128)(2,1)S(1)} collective-permute-done((bf16[776,128]{1,0:T(8,128)(2,1)S(1)}, bf16[776,128]{1,0:T(8,128)(2,1)S(1)}, u32[]{:S(2)}, u32[]{:S(2)}) %collective-permute-start) | collective-permute-done | bytes 198688 | tf_op jit(solution)/shard_map/ppermute | solution.py:208
  12.6 1.5 %collective-permute-start.2 = (bf16[776,128]{1,0:T(8,128)(2,1)S(1)}, bf16[776,128]{1,0:T(8,128)(2,1)S(1)}, u32[]{:S(2)}, u32[]{:S(2)}) collective-permute-start(bf16[776,128]{1,0:T(8,128)(2,1)S(1)} %collective-permute-done.refs_1_.refs_2_), channel_id=1, source_target_pairs={{0,2},{1,3},{2,0},{3,1},{4,6},{5,7},{6,4},{7,5},{8,10},{9,11},{10,... | collective-permute-start | bytes 595976 | tf_op jit(solution)/shard_map/ppermute | solution.py:208
  14.1 0.3 %score_soon.1 = (f32[1,128]{1,0:T(1,128)S(1)}, bf16[776,128]{1,0:T(8,128)(2,1)S(1)}) custom-call(bf16[776,128]{1,0:T(8,128)(2,1)S(1)} %get-tuple-element.16.refs_0_.refs_2_, bf16[776,128]{1,0:T(8,128)(2,1)S(1)} %collective-permute-done.refs_1_.refs_2_, bf16[776,128]{1,0:T(8,128)(2,1)S(1)} %get-tuple-element.16.refs_0_.refs_2_), custom_call_target="tpu_custom_call" | custom-call | flops 50331648 | bytes 589824 | tf_op jit(solution)/shard_map/score_soon/pallas_call | solution.py:172
  14.4 0.0 collective-permute-done.3.refs_5_
  14.4 0.1 collective-permute-start.6
  14.5 0.5 %collective-permute-start.5 = (bf16[776,128]{1,0:T(8,128)(2,1)S(1)}, bf16[776,128]{1,0:T(8,128)(2,1)S(1)}, u32[]{:S(2)}, u32[]{:S(2)}) collective-permute-start(bf16[776,128]{1,0:T(8,128)(2,1)S(1)} %get-tuple-element.17.refs_0_.refs_4_), channel_id=1, source_target_pairs={{0,1},{1,0},{2,3},{3,2},{4,5},{5,4},{6,7},{7,6},{8,9},{9,8},{10,11... | collective-permute-start | bytes 595976 | tf_op jit(solution)/shard_map/ppermute | solution.py:208
  15.0 2.7 %collective-permute-done.4.refs_6_ = bf16[776,128]{1,0:T(8,128)(2,1)S(1)} collective-permute-done((bf16[776,128]{1,0:T(8,128)(2,1)S(1)}, bf16[776,128]{1,0:T(8,128)(2,1)S(1)}, u32[]{:S(2)}, u32[]{:S(2)}) %collective-permute-start.4) | collective-permute-done | bytes 198688 | tf_op jit(solution)/shard_map/ppermute | solution.py:204
  17.7 0.6 %collective-permute-done.2.refs_3_ = bf16[776,128]{1,0:T(8,128)(2,1)S(1)} collective-permute-done((bf16[776,128]{1,0:T(8,128)(2,1)S(1)}, bf16[776,128]{1,0:T(8,128)(2,1)S(1)}, u32[]{:S(2)}, u32[]{:S(2)}) %collective-permute-start.2) | collective-permute-done | bytes 198688 | tf_op jit(solution)/shard_map/ppermute | solution.py:208
  18.3 0.7 %score_late.1 = (f32[3,128]{1,0:T(4,128)S(1)}, f32[4,128]{1,0:T(4,128)S(1)}) custom-call(bf16[776,128]{1,0:T(8,128)(2,1)S(1)} %get-tuple-element.17.refs_0_.refs_4_, bf16[776,128]{1,0:T(8,128)(2,1)S(1)} %collective-permute-done.1.refs_1_, bf16[776,128]{1,0:T(8,128)(2,1)S(1)} %collective-permute-done.refs_1_.refs_2_, ...), custom_call_target="tpu_custom_call" | custom-call | flops 251658240 | bytes 1376256 | tf_op jit(solution)/shard_map/score_late/pallas_call | solution.py:172
  18.9 0.2 collective-permute-done.7.refs_6_
  19.1 0.8 %score_partner.1 = (f32[3,128]{1,0:T(4,128)S(1)}, f32[2,128]{1,0:T(2,128)S(1)}, f32[2,128]{1,0:T(2,128)S(1)}) custom-call(bf16[776,128]{1,0:T(8,128)(2,1)S(1)} %get-tuple-element.17.refs_0_.refs_4_, bf16[776,128]{1,0:T(8,128)(2,1)S(1)} %collective-permute-done.1.refs_1_, bf16[776,128]{1,0:T(8,128)(2,1)S(1)} %collective-permute-done.refs_1_.refs_2_, ...), custom_call_target="tpu_custom_call" | custom-call | flops 301989888 | bytes 1376256 | tf_op jit(solution)/shard_map/score_partner/pallas_call | solution.py:172
  19.9 0.2 collective-permute-start.8
  20.0 1.5 %collective-permute-start.11 = (f32[2,128]{1,0:T(2,128)S(1)}, f32[2,128]{1,0:T(2,128)S(1)}, u32[]{:S(2)}, u32[]{:S(2)}) collective-permute-start(f32[2,128]{1,0:T(2,128)S(1)} %get-tuple-element.26), channel_id=1, source_target_pairs={{0,4},{1,5},{2,6},{3,7},{4,0},{5,1},{6,2},{7,3},{8,12},{9,13},{10,... | collective-permute-start | bytes 3080 | tf_op jit(solution)/shard_map/ppermute | solution.py:208
  21.6 2.4 %collective-permute-start.10 = (f32[1,128]{1,0:T(1,128)S(1)}, f32[1,128]{1,0:T(1,128)S(1)}, u32[]{:S(2)}, u32[]{:S(2)}) collective-permute-start(f32[1,128]{1,0:T(1,128)S(1)} %get-tuple-element.28), channel_id=1, source_target_pairs={{8,0},{9,1},{10,2},{11,3},{12,4},{13,5},{14,6},{15,7},{16,8},{17,9... | collective-permute-start | bytes 1544 | tf_op jit(solution)/shard_map/ppermute | solution.py:204
  24.0 0.4 %collective-permute-start.9 = (f32[1,128]{1,0:T(1,128)S(1)}, f32[1,128]{1,0:T(1,128)S(1)}, u32[]{:S(2)}, u32[]{:S(2)}) collective-permute-start(f32[1,128]{1,0:T(1,128)S(1)} %get-tuple-element.27), channel_id=1, source_target_pairs={{0,16},{1,17},{2,18},{3,19},{4,20},{5,21},{6,22},{7,23},{24,8},{25... | collective-permute-start | bytes 1544 | tf_op jit(solution)/shard_map/ppermute | solution.py:204
  24.5 1.6 %collective-permute-start.12 = (f32[1,128]{1,0:T(1,128)S(1)}, f32[1,128]{1,0:T(1,128)S(1)}, u32[]{:S(2)}, u32[]{:S(2)}) collective-permute-start(f32[1,128]{1,0:T(1,128)S(1)} %slice.19), channel_id=1, source_target_pairs={{0,2},{1,3},{2,0},{3,1},{4,6},{5,7},{6,4},{7,5},{8,10},{9,11},{10,... | collective-permute-start | bytes 1544 | tf_op jit(solution)/shard_map/ppermute | solution.py:208
  26.0 1.5 %collective-permute-done.9 = f32[1,128]{1,0:T(1,128)S(1)} collective-permute-done((f32[1,128]{1,0:T(1,128)S(1)}, f32[1,128]{1,0:T(1,128)S(1)}, u32[]{:S(2)}, u32[]{:S(2)}) %collective-permute-start.9) | collective-permute-done | bytes 544 | tf_op jit(solution)/shard_map/ppermute | solution.py:204
  27.6 0.5 %collective-permute-done.12 = f32[1,128]{1,0:T(1,128)S(1)} collective-permute-done((f32[1,128]{1,0:T(1,128)S(1)}, f32[1,128]{1,0:T(1,128)S(1)}, u32[]{:S(2)}, u32[]{:S(2)}) %collective-permute-start.12) | collective-permute-done | bytes 544 | tf_op jit(solution)/shard_map/ppermute | solution.py:208
  28.1 0.5 %maximum_bitcast_fusion = f32[128]{0:T(128)} fusion(f32[1,128]{1,0:T(1,128)S(1)} %collective-permute-done.12, f32[1,128]{1,0:T(1,128)S(1)} %maximum_maximum_fusion, f32[2,128]{1,0:T(2,128)S(1)} %max.21), kind=kLoop, calls=%fused_computation | loop fusion | flops 256 | bytes 2048 | tf_op jit(solution)/shard_map/reshape | solution.py:252
  (12 shorter events, 0.0 us)
Async XLA Ops:
  3.1 11.3 %collective-permute-start.3 = (bf16[824,128]{1,0:T(8,128)(2,1)S(1)}, bf16[824,128]{1,0:T(8,128)(2,1)S(1)}, u32[]{:S(2)}, u32[]{:S(2)}) collective-permute-start(bf16[824,128]{1,0:T(8,128)(2,1)S(1)} %get-tuple-element.18), channel_id=1, source_target_pairs={{0,8},{1,9},{2,10},{3,11},{4,12},{5,13},{6,14},{7,15},{8,16},{9,17... | collective-permute-start | bytes 632840 | tf_op jit(solution)/shard_map/ppermute | solution.py:204
  6.2 6.4 %collective-permute-start = (bf16[776,128]{1,0:T(8,128)(2,1)S(1)}, bf16[776,128]{1,0:T(8,128)(2,1)S(1)}, u32[]{:S(2)}, u32[]{:S(2)}) collective-permute-start(bf16[776,128]{1,0:T(8,128)(2,1)S(1)} %get-tuple-element.16.refs_0_.refs_2_), channel_id=1, source_target_pairs={{0,4},{1,5},{2,6},{3,7},{4,0},{5,1},{6,2},{7,3},{8,12},{9,13},{10,... | collective-permute-start | bytes 595976 | tf_op jit(solution)/shard_map/ppermute | solution.py:208
  7.7 7.3 %collective-permute-start.1 = (bf16[776,128]{1,0:T(8,128)(2,1)S(1)}, bf16[776,128]{1,0:T(8,128)(2,1)S(1)}, u32[]{:S(2)}, u32[]{:S(2)}) collective-permute-start(bf16[776,128]{1,0:T(8,128)(2,1)S(1)} %get-tuple-element.16.refs_0_.refs_2_), channel_id=1, source_target_pairs={{0,2},{1,3},{2,0},{3,1},{4,6},{5,7},{6,4},{7,5},{8,10},{9,11},{10,... | collective-permute-start | bytes 595976 | tf_op jit(solution)/shard_map/ppermute | solution.py:208
  9.2 8.5 %collective-permute-start.4 = (bf16[776,128]{1,0:T(8,128)(2,1)S(1)}, bf16[776,128]{1,0:T(8,128)(2,1)S(1)}, u32[]{:S(2)}, u32[]{:S(2)}) collective-permute-start(bf16[776,128]{1,0:T(8,128)(2,1)S(1)} %get-tuple-element.16.refs_0_.refs_2_), channel_id=1, source_target_pairs={{16,0},{17,1},{18,2},{19,3},{20,4},{21,5},{22,6},{23,7},{8,24},{9,... | collective-permute-start | bytes 595976 | tf_op jit(solution)/shard_map/ppermute | solution.py:204
  12.6 5.7 %collective-permute-start.2 = (bf16[776,128]{1,0:T(8,128)(2,1)S(1)}, bf16[776,128]{1,0:T(8,128)(2,1)S(1)}, u32[]{:S(2)}, u32[]{:S(2)}) collective-permute-start(bf16[776,128]{1,0:T(8,128)(2,1)S(1)} %collective-permute-done.refs_1_.refs_2_), channel_id=1, source_target_pairs={{0,2},{1,3},{2,0},{3,1},{4,6},{5,7},{6,4},{7,5},{8,10},{9,11},{10,... | collective-permute-start | bytes 595976 | tf_op jit(solution)/shard_map/ppermute | solution.py:208
  14.4 4.7 %collective-permute-start.6 = (bf16[824,128]{1,0:T(8,128)(2,1)S(1)}, bf16[824,128]{1,0:T(8,128)(2,1)S(1)}, u32[]{:S(2)}, u32[]{:S(2)}) collective-permute-start(bf16[824,128]{1,0:T(8,128)(2,1)S(1)} %collective-permute-done.3.refs_5_), channel_id=1, source_target_pairs={{0,1},{1,0},{2,3},{3,2},{4,5},{5,4},{6,7},{7,6},{8,9},{9,8},{10,11... | collective-permute-start | bytes 632840 | tf_op jit(solution)/shard_map/ppermute | solution.py:208
  14.5 4.4 %collective-permute-start.5 = (bf16[776,128]{1,0:T(8,128)(2,1)S(1)}, bf16[776,128]{1,0:T(8,128)(2,1)S(1)}, u32[]{:S(2)}, u32[]{:S(2)}) collective-permute-start(bf16[776,128]{1,0:T(8,128)(2,1)S(1)} %get-tuple-element.17.refs_0_.refs_4_), channel_id=1, source_target_pairs={{0,1},{1,0},{2,3},{3,2},{4,5},{5,4},{6,7},{7,6},{8,9},{9,8},{10,11... | collective-permute-start | bytes 595976 | tf_op jit(solution)/shard_map/ppermute | solution.py:208
  17.7 1.4 %collective-permute-start.7 = (bf16[776,128]{1,0:T(8,128)(2,1)S(1)}, bf16[776,128]{1,0:T(8,128)(2,1)S(1)}, u32[]{:S(2)}, u32[]{:S(2)}) collective-permute-start(bf16[776,128]{1,0:T(8,128)(2,1)S(1)} %collective-permute-done.4.refs_6_), channel_id=1, source_target_pairs={{0,1},{1,0},{2,3},{3,2},{4,5},{5,4},{6,7},{7,6},{8,9},{9,8},{10,11... | collective-permute-start | bytes 595976 | tf_op jit(solution)/shard_map/ppermute | solution.py:208
  19.9 1.7 %collective-permute-start.8 = (f32[3,128]{1,0:T(4,128)S(1)}, f32[3,128]{1,0:T(4,128)S(1)}, u32[]{:S(2)}, u32[]{:S(2)}) collective-permute-start(f32[3,128]{1,0:T(4,128)S(1)} %get-tuple-element.24), channel_id=1, source_target_pairs={{0,1},{1,0},{2,3},{3,2},{4,5},{5,4},{6,7},{7,6},{8,9},{9,8},{10,11... | collective-permute-start | bytes 4616 | tf_op jit(solution)/shard_map/ppermute | solution.py:208
  20.0 4.4 %collective-permute-start.11 = (f32[2,128]{1,0:T(2,128)S(1)}, f32[2,128]{1,0:T(2,128)S(1)}, u32[]{:S(2)}, u32[]{:S(2)}) collective-permute-start(f32[2,128]{1,0:T(2,128)S(1)} %get-tuple-element.26), channel_id=1, source_target_pairs={{0,4},{1,5},{2,6},{3,7},{4,0},{5,1},{6,2},{7,3},{8,12},{9,13},{10,... | collective-permute-start | bytes 3080 | tf_op jit(solution)/shard_map/ppermute | solution.py:208
  21.6 4.5 %collective-permute-start.10 = (f32[1,128]{1,0:T(1,128)S(1)}, f32[1,128]{1,0:T(1,128)S(1)}, u32[]{:S(2)}, u32[]{:S(2)}) collective-permute-start(f32[1,128]{1,0:T(1,128)S(1)} %get-tuple-element.28), channel_id=1, source_target_pairs={{8,0},{9,1},{10,2},{11,3},{12,4},{13,5},{14,6},{15,7},{16,8},{17,9... | collective-permute-start | bytes 1544 | tf_op jit(solution)/shard_map/ppermute | solution.py:204
  24.0 3.5 %collective-permute-start.9 = (f32[1,128]{1,0:T(1,128)S(1)}, f32[1,128]{1,0:T(1,128)S(1)}, u32[]{:S(2)}, u32[]{:S(2)}) collective-permute-start(f32[1,128]{1,0:T(1,128)S(1)} %get-tuple-element.27), channel_id=1, source_target_pairs={{0,16},{1,17},{2,18},{3,19},{4,20},{5,21},{6,22},{7,23},{24,8},{25... | collective-permute-start | bytes 1544 | tf_op jit(solution)/shard_map/ppermute | solution.py:204
  24.5 3.6 %collective-permute-start.12 = (f32[1,128]{1,0:T(1,128)S(1)}, f32[1,128]{1,0:T(1,128)S(1)}, u32[]{:S(2)}, u32[]{:S(2)}) collective-permute-start(f32[1,128]{1,0:T(1,128)S(1)} %slice.19), channel_id=1, source_target_pairs={{0,2},{1,3},{2,0},{3,1},{4,6},{5,7},{6,4},{7,5},{8,10},{9,11},{10,... | collective-permute-start | bytes 1544 | tf_op jit(solution)/shard_map/ppermute | solution.py:208

commit v8 on v5

--- a/solution.py
+++ b/solution.py
@@ -100,21 +100,23 @@
     )
 
 
-def score_kernel(row_count, lane_count, products, parts, has_lines, seen_rows, hold, *refs):
+def score_kernel(row_count, lane_count, products, parts, has_lines, has_state, hand_on, hold, *refs):
     refs = list(refs)
     row_refs = [refs.pop(0) for _ in range(row_count)]
     lane_refs = [refs.pop(0) for _ in range(lane_count)]
     seen_lines = refs.pop(0) if has_lines else None
-    seen_backs = refs.pop(0) if seen_rows else None
+    seen_table, seen_columns = (refs.pop(0), refs.pop(0)) if has_state else (None, None)
     lines_out = refs.pop(0)
     rows = lines_out.shape[1]
     if hold:
         refs[-1][...] = row_refs[0][...]
-    row_notes = [read_notes(ref) for ref in row_refs]
     lane_notes = [read_notes(ref) for ref in lane_refs]
-    fill = jnp.zeros((-2 * row_count % 8, rows), jnp.float32)
-    lines = [line for pair in row_notes for line in pair]
-    columns = jnp.concatenate(lines + ([fill] if fill.size else []), axis=0).T
+    if has_state:
+        columns = seen_columns[...]
+    else:
+        fill = jnp.zeros((-2 * row_count % 8, rows), jnp.float32)
+        lines = [line for ref in row_refs for line in read_notes(ref)]
+        columns = jnp.concatenate(lines + ([fill] if fill.size else []), axis=0).T
     best, back = [None] * lane_count, [None] * row_count
 
     def top(old, new):
@@ -142,11 +144,15 @@
     for i, each in enumerate(back):
         if each is not None:
             table = jnp.where(lane_ids == i, jnp.max(each, axis=1, keepdims=True), table)
-    table = table.T
-    if seen_rows:
-        table = jnp.maximum(table[:row_count], seen_backs[...])
-    for first, stop in parts:
-        refs.pop(0)[...] = table[first:stop]
+    if has_state:
+        table = jnp.maximum(table, seen_table[...])
+    if hand_on:
+        refs.pop(0)[...] = table
+        refs.pop(0)[...] = columns
+    elif parts:
+        table = table.T
+        for first, stop in parts:
+            refs.pop(0)[...] = table[first:stop]
     lines = jnp.concatenate([jnp.max(b, axis=0, keepdims=True) for b in best], axis=0)
     if has_lines:
         count = seen_lines.shape[0]
@@ -155,16 +161,18 @@
     lines_out[...] = lines
 
 
-def score(name, row_blocks, lane_blocks, products, parts, lines=None, backs=None, hold=False):
+def score(name, row_blocks, lane_blocks, products, parts, lines=None, state=None, hand_on=False, hold=False):
     high, rows = row_blocks[0].shape
     width = high - NOTE_ROWS
-    inputs = [*row_blocks, *lane_blocks, *(seen for seen in (lines, backs) if seen is not None)]
+    inputs = [*row_blocks, *lane_blocks, *([] if lines is None else [lines]), *(state or ())]
     shapes = [(len(lane_blocks), rows)] + [(stop - first, rows) for first, stop in parts]
+    if hand_on:
+        shapes += [(rows, rows), (rows, -(-2 * len(row_blocks) // 8) * 8)]
     outs = [jax.ShapeDtypeStruct(shape, jnp.float32) for shape in shapes]
     if hold:
         outs.append(jax.ShapeDtypeStruct((high, rows), row_blocks[0].dtype))
     counts = len(row_blocks), len(lane_blocks)
-    rest = products, parts, lines is not None, backs is not None, hold
+    rest = products, parts, lines is not None, state is not None, hand_on, hold
     macs = sum(len(r) * len(c) for r, c in products) * rows * rows * width
     return pl.pallas_call(
         lambda *refs: score_kernel(*counts, *rest, *refs),
@@ -229,13 +237,13 @@
     )
     row_blocks[0] = lanes[0] = held
     products = [(rest, every), (soon, every[1:])]
-    lines, backs = score("score_late", row_blocks, lanes, products, [(0, count)], lines)
+    lines, *state = score("score_late", row_blocks, lanes, products, [], lines, hand_on=True)
     partner = [held]
     partner += [lax.optimization_barrier((visitor, held))[0] for visitor in visitors[:-1]]
     partner += [lax.optimization_barrier((visitors[-1], row_blocks[1]))[0]]
     partner = [swap(lane, 1) for lane in partner]
     products, parts = [(tuple(range(count)), every)], [(0, half), (half, count)]
-    theirs, near, far = score("score_partner", row_blocks, partner, products, parts, None, backs)
+    theirs, near, far = score("score_partner", row_blocks, partner, products, parts, state=state)
     lines = jnp.maximum(lines, swap(theirs, 1))
     for bit in bits[:0:-1]:
         near = jnp.maximum(near, swap(far, bit))

time: 28.2 us -> 28.1 us (level)
  transfers between devices with their start and end apart: 13 -> 13, of which waited for: 6 -> 6; matrix products, arithmetic and copies ran while one was open for 0% -> 0% of each run, Pallas kernels for 4% -> 3%
where the time goes in v8:
time: 28.1 us; the launch traced here: 28 us
  starting transfers between devices  15.8 us (56%)
  waiting for transfers between devices  7.42 us (26%)
  Pallas kernels  4.21 us (15%)
  other arithmetic  0.52 us (2%)
    ppermute x9, starting transfers between devices, swap(): return lax.ppermute(array, AXES, pairs)  8.32 us
    ppermute x4, starting transfers between devices, move(): return lax.ppermute(array, AXES, whole)  7.44 us
    ppermute x4, waiting for transfers between devices, move(): return lax.ppermute(array, AXES, whole)  4.33 us
    ppermute x9, waiting for transfers between devices, swap(): return lax.ppermute(array, AXES, pairs)  3.09 us
    pallas_call x1, Pallas kernels, embed(): pl.pallas_call(embed_kernel, in_specs=[HBM] * 5, out_specs=[VMEM] * 2, ou...  2.56 us
    pallas_call x3, Pallas kernels, score(): pl.pallas_call(lambda *refs: score_kernel(*counts, *rest, *refs), in_spec...  1.66 us
  transfers between devices with their start and end apart: 13, of which 6 were waited for; matrix products, arithmetic and copies ran while one was open for 0% of the time, Pallas kernels for 3%

profile of v8, /device:TPU:0, one launch (start us, length us, event | category | flops | bytes accessed | tf_op | source)
XLA Modules:
  0.0 28.0 jit_solution(16896933549161003656)
XLA Ops:
  0.0 2.6 %embed.1 = (bf16[776,128]{1,0:T(8,128)(2,1)S(1)}, bf16[832,128]{1,0:T(8,128)(2,1)S(1)}) custom-call(bf16[128,2048]{1,0:T(8,128)(2,1)} %states_hbm.1, bf16[2048,768]{1,0:T(8,128)(2,1)} %proj_hbm.1, s32[1,128]{1,0:T(1,128)} %bitcast.5, s32[1,128]{1,0:T(1,128)} %bitcast.6, s32[1,128]{1,0:T(1,128)} %bitcast.7), custom_call_target="tpu_custom_call" | custom-call | tf_op jit(solution)/shard_map/embed/pallas_call | solution.py:66
  2.6 3.1 %collective-permute-start.3 = (bf16[832,128]{1,0:T(8,128)(2,1)S(1)}, bf16[832,128]{1,0:T(8,128)(2,1)S(1)}, u32[]{:S(2)}, u32[]{:S(2)}) collective-permute-start(bf16[832,128]{1,0:T(8,128)(2,1)S(1)} %get-tuple-element.19), channel_id=1, source_target_pairs={{0,8},{1,9},{2,10},{3,11},{4,12},{5,13},{6,14},{7,15},{8,16},{9,17... | collective-permute-start | bytes 638984 | tf_op jit(solution)/shard_map/ppermute | solution.py:209
  5.6 1.5 %collective-permute-start = (bf16[776,128]{1,0:T(8,128)(2,1)S(1)}, bf16[776,128]{1,0:T(8,128)(2,1)S(1)}, u32[]{:S(2)}, u32[]{:S(2)}) collective-permute-start(bf16[776,128]{1,0:T(8,128)(2,1)S(1)} %get-tuple-element.17.refs_0_.refs_2_), channel_id=1, source_target_pairs={{0,4},{1,5},{2,6},{3,7},{4,0},{5,1},{6,2},{7,3},{8,12},{9,13},{10,... | collective-permute-start | bytes 595976 | tf_op jit(solution)/shard_map/ppermute | solution.py:213
  7.2 1.5 %collective-permute-start.1 = (bf16[776,128]{1,0:T(8,128)(2,1)S(1)}, bf16[776,128]{1,0:T(8,128)(2,1)S(1)}, u32[]{:S(2)}, u32[]{:S(2)}) collective-permute-start(bf16[776,128]{1,0:T(8,128)(2,1)S(1)} %get-tuple-element.17.refs_0_.refs_2_), channel_id=1, source_target_pairs={{0,2},{1,3},{2,0},{3,1},{4,6},{5,7},{6,4},{7,5},{8,10},{9,11},{10,... | collective-permute-start | bytes 595976 | tf_op jit(solution)/shard_map/ppermute | solution.py:213
  8.7 1.6 %collective-permute-start.4 = (bf16[776,128]{1,0:T(8,128)(2,1)S(1)}, bf16[776,128]{1,0:T(8,128)(2,1)S(1)}, u32[]{:S(2)}, u32[]{:S(2)}) collective-permute-start(bf16[776,128]{1,0:T(8,128)(2,1)S(1)} %get-tuple-element.17.refs_0_.refs_2_), channel_id=1, source_target_pairs={{16,0},{17,1},{18,2},{19,3},{20,4},{21,5},{22,6},{23,7},{8,24},{9,... | collective-permute-start | bytes 595976 | tf_op jit(solution)/shard_map/ppermute | solution.py:209
  10.2 1.8 %collective-permute-done.refs_1_.refs_2_ = bf16[776,128]{1,0:T(8,128)(2,1)S(1)} collective-permute-done((bf16[776,128]{1,0:T(8,128)(2,1)S(1)}, bf16[776,128]{1,0:T(8,128)(2,1)S(1)}, u32[]{:S(2)}, u32[]{:S(2)}) %collective-permute-start) | collective-permute-done | bytes 198688 | tf_op jit(solution)/shard_map/ppermute | solution.py:213
  12.1 1.5 %collective-permute-start.2 = (bf16[776,128]{1,0:T(8,128)(2,1)S(1)}, bf16[776,128]{1,0:T(8,128)(2,1)S(1)}, u32[]{:S(2)}, u32[]{:S(2)}) collective-permute-start(bf16[776,128]{1,0:T(8,128)(2,1)S(1)} %collective-permute-done.refs_1_.refs_2_), channel_id=1, source_target_pairs={{0,2},{1,3},{2,0},{3,1},{4,6},{5,7},{6,4},{7,5},{8,10},{9,11},{10,... | collective-permute-start | bytes 595976 | tf_op jit(solution)/shard_map/ppermute | solution.py:213
  13.5 0.3 %score_soon.1 = (f32[1,128]{1,0:T(1,128)S(1)}, bf16[776,128]{1,0:T(8,128)(2,1)S(1)}) custom-call(bf16[776,128]{1,0:T(8,128)(2,1)S(1)} %get-tuple-element.17.refs_0_.refs_2_, bf16[776,128]{1,0:T(8,128)(2,1)S(1)} %collective-permute-done.refs_1_.refs_2_, bf16[776,128]{1,0:T(8,128)(2,1)S(1)} %get-tuple-element.17.refs_0_.refs_2_), custom_call_target="tpu_custom_call" | custom-call | flops 50331648 | bytes 589824 | tf_op jit(solution)/shard_map/score_soon/pallas_call | solution.py:177
  13.9 0.0 collective-permute-done.3.refs_5_
  13.9 0.1 collective-permute-start.6
  14.0 0.5 %collective-permute-start.5 = (bf16[776,128]{1,0:T(8,128)(2,1)S(1)}, bf16[776,128]{1,0:T(8,128)(2,1)S(1)}, u32[]{:S(2)}, u32[]{:S(2)}) collective-permute-start(bf16[776,128]{1,0:T(8,128)(2,1)S(1)} %get-tuple-element.18.refs_0_.refs_4_), channel_id=1, source_target_pairs={{0,1},{1,0},{2,3},{3,2},{4,5},{5,4},{6,7},{7,6},{8,9},{9,8},{10,11... | collective-permute-start | bytes 595976 | tf_op jit(solution)/shard_map/ppermute | solution.py:213
  14.5 2.7 %collective-permute-done.4.refs_6_ = bf16[776,128]{1,0:T(8,128)(2,1)S(1)} collective-permute-done((bf16[776,128]{1,0:T(8,128)(2,1)S(1)}, bf16[776,128]{1,0:T(8,128)(2,1)S(1)}, u32[]{:S(2)}, u32[]{:S(2)}) %collective-permute-start.4) | collective-permute-done | bytes 198688 | tf_op jit(solution)/shard_map/ppermute | solution.py:209
  17.2 0.6 %collective-permute-done.2.refs_3_ = bf16[776,128]{1,0:T(8,128)(2,1)S(1)} collective-permute-done((bf16[776,128]{1,0:T(8,128)(2,1)S(1)}, bf16[776,128]{1,0:T(8,128)(2,1)S(1)}, u32[]{:S(2)}, u32[]{:S(2)}) %collective-permute-start.2) | collective-permute-done | bytes 198688 | tf_op jit(solution)/shard_map/ppermute | solution.py:213
  17.7 0.6 %score_late.1 = (f32[3,128]{1,0:T(4,128)S(1)}, f32[128,128]{1,0:T(8,128)S(1)}, f32[128,8]{1,0:T(8,128)S(1)}) custom-call(bf16[776,128]{1,0:T(8,128)(2,1)S(1)} %get-tuple-element.18.refs_0_.refs_4_, bf16[776,128]{1,0:T(8,128)(2,1)S(1)} %collective-permute-done.1.refs_1_, bf16[776,128]{1,0:T(8,128)(2,1)S(1)} %collective-permute-done.refs_1_.refs_2_, ...), custom_call_target="tpu_custom_call" | custom-call | flops 251658240 | bytes 1376256 | tf_op jit(solution)/shard_map/score_late/pallas_call | solution.py:177
  18.4 0.2 collective-permute-done.7.refs_6_
  18.6 0.7 %score_partner.1 = (f32[3,128]{1,0:T(4,128)S(1)}, f32[2,128]{1,0:T(2,128)S(1)}, f32[2,128]{1,0:T(2,128)S(1)}) custom-call(bf16[776,128]{1,0:T(8,128)(2,1)S(1)} %get-tuple-element.18.refs_0_.refs_4_, bf16[776,128]{1,0:T(8,128)(2,1)S(1)} %collective-permute-done.1.refs_1_, bf16[776,128]{1,0:T(8,128)(2,1)S(1)} %collective-permute-done.refs_1_.refs_2_, ...), custom_call_target="tpu_custom_call" | custom-call | flops 301989888 | bytes 1376256 | tf_op jit(solution)/shard_map/score_partner/pallas_call | solution.py:177
  19.3 0.2 collective-permute-start.8
  19.5 1.5 %collective-permute-start.11 = (f32[2,128]{1,0:T(2,128)S(1)}, f32[2,128]{1,0:T(2,128)S(1)}, u32[]{:S(2)}, u32[]{:S(2)}) collective-permute-start(f32[2,128]{1,0:T(2,128)S(1)} %get-tuple-element.28), channel_id=1, source_target_pairs={{0,4},{1,5},{2,6},{3,7},{4,0},{5,1},{6,2},{7,3},{8,12},{9,13},{10,... | collective-permute-start | bytes 3080 | tf_op jit(solution)/shard_map/ppermute | solution.py:213
  21.1 2.4 %collective-permute-start.10 = (f32[1,128]{1,0:T(1,128)S(1)}, f32[1,128]{1,0:T(1,128)S(1)}, u32[]{:S(2)}, u32[]{:S(2)}) collective-permute-start(f32[1,128]{1,0:T(1,128)S(1)} %get-tuple-element.30), channel_id=1, source_target_pairs={{8,0},{9,1},{10,2},{11,3},{12,4},{13,5},{14,6},{15,7},{16,8},{17,9... | collective-permute-start | bytes 1544 | tf_op jit(solution)/shard_map/ppermute | solution.py:209
  23.5 0.4 %collective-permute-start.9 = (f32[1,128]{1,0:T(1,128)S(1)}, f32[1,128]{1,0:T(1,128)S(1)}, u32[]{:S(2)}, u32[]{:S(2)}) collective-permute-start(f32[1,128]{1,0:T(1,128)S(1)} %get-tuple-element.29), channel_id=1, source_target_pairs={{0,16},{1,17},{2,18},{3,19},{4,20},{5,21},{6,22},{7,23},{24,8},{25... | collective-permute-start | bytes 1544 | tf_op jit(solution)/shard_map/ppermute | solution.py:209
  23.9 1.5 %collective-permute-start.12 = (f32[1,128]{1,0:T(1,128)S(1)}, f32[1,128]{1,0:T(1,128)S(1)}, u32[]{:S(2)}, u32[]{:S(2)}) collective-permute-start(f32[1,128]{1,0:T(1,128)S(1)} %slice.19), channel_id=1, source_target_pairs={{0,2},{1,3},{2,0},{3,1},{4,6},{5,7},{6,4},{7,5},{8,10},{9,11},{10,... | collective-permute-start | bytes 1544 | tf_op jit(solution)/shard_map/ppermute | solution.py:213
  25.4 1.6 %collective-permute-done.9 = f32[1,128]{1,0:T(1,128)S(1)} collective-permute-done((f32[1,128]{1,0:T(1,128)S(1)}, f32[1,128]{1,0:T(1,128)S(1)}, u32[]{:S(2)}, u32[]{:S(2)}) %collective-permute-start.9) | collective-permute-done | bytes 544 | tf_op jit(solution)/shard_map/ppermute | solution.py:209
  27.0 0.4 %collective-permute-done.12 = f32[1,128]{1,0:T(1,128)S(1)} collective-permute-done((f32[1,128]{1,0:T(1,128)S(1)}, f32[1,128]{1,0:T(1,128)S(1)}, u32[]{:S(2)}, u32[]{:S(2)}) %collective-permute-start.12) | collective-permute-done | bytes 544 | tf_op jit(solution)/shard_map/ppermute | solution.py:213
  27.5 0.5 %maximum_bitcast_fusion = f32[128]{0:T(128)} fusion(f32[1,128]{1,0:T(1,128)S(1)} %collective-permute-done.12, f32[1,128]{1,0:T(1,128)S(1)} %maximum_maximum_fusion, f32[2,128]{1,0:T(2,128)S(1)} %max.21), kind=kLoop, calls=%fused_computation | loop fusion | flops 256 | bytes 2048 | tf_op jit(solution)/shard_map/reshape | solution.py:257
  (12 shorter events, 0.0 us)
Async XLA Ops:
  2.6 11.3 %collective-permute-start.3 = (bf16[832,128]{1,0:T(8,128)(2,1)S(1)}, bf16[832,128]{1,0:T(8,128)(2,1)S(1)}, u32[]{:S(2)}, u32[]{:S(2)}) collective-permute-start(bf16[832,128]{1,0:T(8,128)(2,1)S(1)} %get-tuple-element.19), channel_id=1, source_target_pairs={{0,8},{1,9},{2,10},{3,11},{4,12},{5,13},{6,14},{7,15},{8,16},{9,17... | collective-permute-start | bytes 638984 | tf_op jit(solution)/shard_map/ppermute | solution.py:209
  5.6 6.4 %collective-permute-start = (bf16[776,128]{1,0:T(8,128)(2,1)S(1)}, bf16[776,128]{1,0:T(8,128)(2,1)S(1)}, u32[]{:S(2)}, u32[]{:S(2)}) collective-permute-start(bf16[776,128]{1,0:T(8,128)(2,1)S(1)} %get-tuple-element.17.refs_0_.refs_2_), channel_id=1, source_target_pairs={{0,4},{1,5},{2,6},{3,7},{4,0},{5,1},{6,2},{7,3},{8,12},{9,13},{10,... | collective-permute-start | bytes 595976 | tf_op jit(solution)/shard_map/ppermute | solution.py:213
  7.2 7.3 %collective-permute-start.1 = (bf16[776,128]{1,0:T(8,128)(2,1)S(1)}, bf16[776,128]{1,0:T(8,128)(2,1)S(1)}, u32[]{:S(2)}, u32[]{:S(2)}) collective-permute-start(bf16[776,128]{1,0:T(8,128)(2,1)S(1)} %get-tuple-element.17.refs_0_.refs_2_), channel_id=1, source_target_pairs={{0,2},{1,3},{2,0},{3,1},{4,6},{5,7},{6,4},{7,5},{8,10},{9,11},{10,... | collective-permute-start | bytes 595976 | tf_op jit(solution)/shard_map/ppermute | solution.py:213
  8.7 8.5 %collective-permute-start.4 = (bf16[776,128]{1,0:T(8,128)(2,1)S(1)}, bf16[776,128]{1,0:T(8,128)(2,1)S(1)}, u32[]{:S(2)}, u32[]{:S(2)}) collective-permute-start(bf16[776,128]{1,0:T(8,128)(2,1)S(1)} %get-tuple-element.17.refs_0_.refs_2_), channel_id=1, source_target_pairs={{16,0},{17,1},{18,2},{19,3},{20,4},{21,5},{22,6},{23,7},{8,24},{9,... | collective-permute-start | bytes 595976 | tf_op jit(solution)/shard_map/ppermute | solution.py:209
  12.1 5.7 %collective-permute-start.2 = (bf16[776,128]{1,0:T(8,128)(2,1)S(1)}, bf16[776,128]{1,0:T(8,128)(2,1)S(1)}, u32[]{:S(2)}, u32[]{:S(2)}) collective-permute-start(bf16[776,128]{1,0:T(8,128)(2,1)S(1)} %collective-permute-done.refs_1_.refs_2_), channel_id=1, source_target_pairs={{0,2},{1,3},{2,0},{3,1},{4,6},{5,7},{6,4},{7,5},{8,10},{9,11},{10,... | collective-permute-start | bytes 595976 | tf_op jit(solution)/shard_map/ppermute | solution.py:213
  13.9 4.8 %collective-permute-start.6 = (bf16[832,128]{1,0:T(8,128)(2,1)S(1)}, bf16[832,128]{1,0:T(8,128)(2,1)S(1)}, u32[]{:S(2)}, u32[]{:S(2)}) collective-permute-start(bf16[832,128]{1,0:T(8,128)(2,1)S(1)} %collective-permute-done.3.refs_5_), channel_id=1, source_target_pairs={{0,1},{1,0},{2,3},{3,2},{4,5},{5,4},{6,7},{7,6},{8,9},{9,8},{10,11... | collective-permute-start | bytes 638984 | tf_op jit(solution)/shard_map/ppermute | solution.py:213
  14.0 4.4 %collective-permute-start.5 = (bf16[776,128]{1,0:T(8,128)(2,1)S(1)}, bf16[776,128]{1,0:T(8,128)(2,1)S(1)}, u32[]{:S(2)}, u32[]{:S(2)}) collective-permute-start(bf16[776,128]{1,0:T(8,128)(2,1)S(1)} %get-tuple-element.18.refs_0_.refs_4_), channel_id=1, source_target_pairs={{0,1},{1,0},{2,3},{3,2},{4,5},{5,4},{6,7},{7,6},{8,9},{9,8},{10,11... | collective-permute-start | bytes 595976 | tf_op jit(solution)/shard_map/ppermute | solution.py:213
  17.2 1.4 %collective-permute-start.7 = (bf16[776,128]{1,0:T(8,128)(2,1)S(1)}, bf16[776,128]{1,0:T(8,128)(2,1)S(1)}, u32[]{:S(2)}, u32[]{:S(2)}) collective-permute-start(bf16[776,128]{1,0:T(8,128)(2,1)S(1)} %collective-permute-done.4.refs_6_), channel_id=1, source_target_pairs={{0,1},{1,0},{2,3},{3,2},{4,5},{5,4},{6,7},{7,6},{8,9},{9,8},{10,11... | collective-permute-start | bytes 595976 | tf_op jit(solution)/shard_map/ppermute | solution.py:213
  19.3 1.7 %collective-permute-start.8 = (f32[3,128]{1,0:T(4,128)S(1)}, f32[3,128]{1,0:T(4,128)S(1)}, u32[]{:S(2)}, u32[]{:S(2)}) collective-permute-start(f32[3,128]{1,0:T(4,128)S(1)} %get-tuple-element.26), channel_id=1, source_target_pairs={{0,1},{1,0},{2,3},{3,2},{4,5},{5,4},{6,7},{7,6},{8,9},{9,8},{10,11... | collective-permute-start | bytes 4616 | tf_op jit(solution)/shard_map/ppermute | solution.py:213
  19.5 4.3 %collective-permute-start.11 = (f32[2,128]{1,0:T(2,128)S(1)}, f32[2,128]{1,0:T(2,128)S(1)}, u32[]{:S(2)}, u32[]{:S(2)}) collective-permute-start(f32[2,128]{1,0:T(2,128)S(1)} %get-tuple-element.28), channel_id=1, source_target_pairs={{0,4},{1,5},{2,6},{3,7},{4,0},{5,1},{6,2},{7,3},{8,12},{9,13},{10,... | collective-permute-start | bytes 3080 | tf_op jit(solution)/shard_map/ppermute | solution.py:213
  21.1 4.4 %collective-permute-start.10 = (f32[1,128]{1,0:T(1,128)S(1)}, f32[1,128]{1,0:T(1,128)S(1)}, u32[]{:S(2)}, u32[]{:S(2)}) collective-permute-start(f32[1,128]{1,0:T(1,128)S(1)} %get-tuple-element.30), channel_id=1, source_target_pairs={{8,0},{9,1},{10,2},{11,3},{12,4},{13,5},{14,6},{15,7},{16,8},{17,9... | collective-permute-start | bytes 1544 | tf_op jit(solution)/shard_map/ppermute | solution.py:209
  23.5 3.5 %collective-permute-start.9 = (f32[1,128]{1,0:T(1,128)S(1)}, f32[1,128]{1,0:T(1,128)S(1)}, u32[]{:S(2)}, u32[]{:S(2)}) collective-permute-start(f32[1,128]{1,0:T(1,128)S(1)} %get-tuple-element.29), channel_id=1, source_target_pairs={{0,16},{1,17},{2,18},{3,19},{4,20},{5,21},{6,22},{7,23},{24,8},{25... | collective-permute-start | bytes 1544 | tf_op jit(solution)/shard_map/ppermute | solution.py:209
  23.9 3.6 %collective-permute-start.12 = (f32[1,128]{1,0:T(1,128)S(1)}, f32[1,128]{1,0:T(1,128)S(1)}, u32[]{:S(2)}, u32[]{:S(2)}) collective-permute-start(f32[1,128]{1,0:T(1,128)S(1)} %slice.19), channel_id=1, source_target_pairs={{0,2},{1,3},{2,0},{3,1},{4,6},{5,7},{6,4},{7,5},{8,10},{9,11},{10,... | collective-permute-start | bytes 1544 | tf_op jit(solution)/shard_map/ppermute | solution.py:213

commit v9 on v8

--- a/solution.py
+++ b/solution.py
@@ -8,8 +8,8 @@
 from jax.sharding import Mesh, PartitionSpec as P
 
 AXES = ("line", "mid", "grp")
-NOTE_ROWS = 8
-MORE_ROWS = 56
+NOTE_ROWS = 16
+MORE_ROWS = 48
 RADIX = 256
 CHUNKS = 4
 VMEM = pl.BlockSpec(memory_space=pltpu.VMEM)

time: 28.1 us -> 28.2 us (level)
  no operation moved by 1% of the time
where the time goes in v9:
time: 28.2 us; the launch traced here: 28.1 us
  starting transfers between devices  15.8 us (56%)
  waiting for transfers between devices  7.46 us (26%)
  Pallas kernels  4.22 us (15%)
  other arithmetic  0.52 us (2%)
    ppermute x9, starting transfers between devices, swap(): return lax.ppermute(array, AXES, pairs)  8.31 us
    ppermute x4, starting transfers between devices, move(): return lax.ppermute(array, AXES, whole)  7.47 us
    ppermute x4, waiting for transfers between devices, move(): return lax.ppermute(array, AXES, whole)  4.32 us
    ppermute x9, waiting for transfers between devices, swap(): return lax.ppermute(array, AXES, pairs)  3.14 us
    pallas_call x1, Pallas kernels, embed(): pl.pallas_call(embed_kernel, in_specs=[HBM] * 5, out_specs=[VMEM] * 2, ou...  2.56 us
    pallas_call x3, Pallas kernels, score(): pl.pallas_call(lambda *refs: score_kernel(*counts, *rest, *refs), in_spec...  1.67 us
  transfers between devices with their start and end apart: 13, of which 6 were waited for; matrix products, arithmetic and copies ran while one was open for 0% of the time, Pallas kernels for 3%

profile of v9, /device:TPU:0, one launch (start us, length us, event | category | flops | bytes accessed | tf_op | source)
XLA Modules:
  0.0 28.1 jit_solution(11229605164996970216)
XLA Ops:
  0.0 2.6 %embed.1 = (bf16[784,128]{1,0:T(8,128)(2,1)S(1)}, bf16[832,128]{1,0:T(8,128)(2,1)S(1)}) custom-call(bf16[128,2048]{1,0:T(8,128)(2,1)} %states_hbm.1, bf16[2048,768]{1,0:T(8,128)(2,1)} %proj_hbm.1, s32[1,128]{1,0:T(1,128)} %bitcast.5, s32[1,128]{1,0:T(1,128)} %bitcast.6, s32[1,128]{1,0:T(1,128)} %bitcast.7), custom_call_target="tpu_custom_call" | custom-call | tf_op jit(solution)/shard_map/embed/pallas_call | solution.py:66
  2.6 3.1 %collective-permute-start.3 = (bf16[832,128]{1,0:T(8,128)(2,1)S(1)}, bf16[832,128]{1,0:T(8,128)(2,1)S(1)}, u32[]{:S(2)}, u32[]{:S(2)}) collective-permute-start(bf16[832,128]{1,0:T(8,128)(2,1)S(1)} %get-tuple-element.19), channel_id=1, source_target_pairs={{0,8},{1,9},{2,10},{3,11},{4,12},{5,13},{6,14},{7,15},{8,16},{9,17... | collective-permute-start | bytes 638984 | tf_op jit(solution)/shard_map/ppermute | solution.py:209
  5.6 1.5 %collective-permute-start = (bf16[784,128]{1,0:T(8,128)(2,1)S(1)}, bf16[784,128]{1,0:T(8,128)(2,1)S(1)}, u32[]{:S(2)}, u32[]{:S(2)}) collective-permute-start(bf16[784,128]{1,0:T(8,128)(2,1)S(1)} %get-tuple-element.17.refs_0_.refs_2_), channel_id=1, source_target_pairs={{0,4},{1,5},{2,6},{3,7},{4,0},{5,1},{6,2},{7,3},{8,12},{9,13},{10,... | collective-permute-start | bytes 602120 | tf_op jit(solution)/shard_map/ppermute | solution.py:213
  7.2 1.5 %collective-permute-start.1 = (bf16[784,128]{1,0:T(8,128)(2,1)S(1)}, bf16[784,128]{1,0:T(8,128)(2,1)S(1)}, u32[]{:S(2)}, u32[]{:S(2)}) collective-permute-start(bf16[784,128]{1,0:T(8,128)(2,1)S(1)} %get-tuple-element.17.refs_0_.refs_2_), channel_id=1, source_target_pairs={{0,2},{1,3},{2,0},{3,1},{4,6},{5,7},{6,4},{7,5},{8,10},{9,11},{10,... | collective-permute-start | bytes 602120 | tf_op jit(solution)/shard_map/ppermute | solution.py:213
  8.7 1.6 %collective-permute-start.4 = (bf16[784,128]{1,0:T(8,128)(2,1)S(1)}, bf16[784,128]{1,0:T(8,128)(2,1)S(1)}, u32[]{:S(2)}, u32[]{:S(2)}) collective-permute-start(bf16[784,128]{1,0:T(8,128)(2,1)S(1)} %get-tuple-element.17.refs_0_.refs_2_), channel_id=1, source_target_pairs={{16,0},{17,1},{18,2},{19,3},{20,4},{21,5},{22,6},{23,7},{8,24},{9,... | collective-permute-start | bytes 602120 | tf_op jit(solution)/shard_map/ppermute | solution.py:209
  10.2 1.9 %collective-permute-done.refs_1_.refs_2_ = bf16[784,128]{1,0:T(8,128)(2,1)S(1)} collective-permute-done((bf16[784,128]{1,0:T(8,128)(2,1)S(1)}, bf16[784,128]{1,0:T(8,128)(2,1)S(1)}, u32[]{:S(2)}, u32[]{:S(2)}) %collective-permute-start) | collective-permute-done | bytes 200736 | tf_op jit(solution)/shard_map/ppermute | solution.py:213
  12.1 1.5 %collective-permute-start.2 = (bf16[784,128]{1,0:T(8,128)(2,1)S(1)}, bf16[784,128]{1,0:T(8,128)(2,1)S(1)}, u32[]{:S(2)}, u32[]{:S(2)}) collective-permute-start(bf16[784,128]{1,0:T(8,128)(2,1)S(1)} %collective-permute-done.refs_1_.refs_2_), channel_id=1, source_target_pairs={{0,2},{1,3},{2,0},{3,1},{4,6},{5,7},{6,4},{7,5},{8,10},{9,11},{10,... | collective-permute-start | bytes 602120 | tf_op jit(solution)/shard_map/ppermute | solution.py:213
  13.6 0.3 %score_soon.1 = (f32[1,128]{1,0:T(1,128)S(1)}, bf16[784,128]{1,0:T(8,128)(2,1)S(1)}) custom-call(bf16[784,128]{1,0:T(8,128)(2,1)S(1)} %get-tuple-element.17.refs_0_.refs_2_, bf16[784,128]{1,0:T(8,128)(2,1)S(1)} %collective-permute-done.refs_1_.refs_2_, bf16[784,128]{1,0:T(8,128)(2,1)S(1)} %get-tuple-element.17.refs_0_.refs_2_), custom_call_target="tpu_custom_call" | custom-call | flops 50331648 | bytes 589824 | tf_op jit(solution)/shard_map/score_soon/pallas_call | solution.py:177
  13.9 0.1 collective-permute-start.6
  14.0 0.5 %collective-permute-start.5 = (bf16[784,128]{1,0:T(8,128)(2,1)S(1)}, bf16[784,128]{1,0:T(8,128)(2,1)S(1)}, u32[]{:S(2)}, u32[]{:S(2)}) collective-permute-start(bf16[784,128]{1,0:T(8,128)(2,1)S(1)} %get-tuple-element.18.refs_0_.refs_4_), channel_id=1, source_target_pairs={{0,1},{1,0},{2,3},{3,2},{4,5},{5,4},{6,7},{7,6},{8,9},{9,8},{10,11... | collective-permute-start | bytes 602120 | tf_op jit(solution)/shard_map/ppermute | solution.py:213
  14.5 2.7 %collective-permute-done.4.refs_6_ = bf16[784,128]{1,0:T(8,128)(2,1)S(1)} collective-permute-done((bf16[784,128]{1,0:T(8,128)(2,1)S(1)}, bf16[784,128]{1,0:T(8,128)(2,1)S(1)}, u32[]{:S(2)}, u32[]{:S(2)}) %collective-permute-start.4) | collective-permute-done | bytes 200736 | tf_op jit(solution)/shard_map/ppermute | solution.py:209
  17.2 0.6 %collective-permute-done.2.refs_3_ = bf16[784,128]{1,0:T(8,128)(2,1)S(1)} collective-permute-done((bf16[784,128]{1,0:T(8,128)(2,1)S(1)}, bf16[784,128]{1,0:T(8,128)(2,1)S(1)}, u32[]{:S(2)}, u32[]{:S(2)}) %collective-permute-start.2) | collective-permute-done | bytes 200736 | tf_op jit(solution)/shard_map/ppermute | solution.py:213
  17.8 0.6 %score_late.1 = (f32[3,128]{1,0:T(4,128)S(1)}, f32[128,128]{1,0:T(8,128)S(1)}, f32[128,8]{1,0:T(8,128)S(1)}) custom-call(bf16[784,128]{1,0:T(8,128)(2,1)S(1)} %get-tuple-element.18.refs_0_.refs_4_, bf16[784,128]{1,0:T(8,128)(2,1)S(1)} %collective-permute-done.1.refs_1_, bf16[784,128]{1,0:T(8,128)(2,1)S(1)} %collective-permute-done.refs_1_.refs_2_, ...), custom_call_target="tpu_custom_call" | custom-call | flops 251658240 | bytes 1376256 | tf_op jit(solution)/shard_map/score_late/pallas_call | solution.py:177
  18.5 0.2 collective-permute-done.7.refs_6_
  18.7 0.0 collective-permute-done.6.refs_5_
  18.7 0.7 %score_partner.1 = (f32[3,128]{1,0:T(4,128)S(1)}, f32[2,128]{1,0:T(2,128)S(1)}, f32[2,128]{1,0:T(2,128)S(1)}) custom-call(bf16[784,128]{1,0:T(8,128)(2,1)S(1)} %get-tuple-element.18.refs_0_.refs_4_, bf16[784,128]{1,0:T(8,128)(2,1)S(1)} %collective-permute-done.1.refs_1_, bf16[784,128]{1,0:T(8,128)(2,1)S(1)} %collective-permute-done.refs_1_.refs_2_, ...), custom_call_target="tpu_custom_call" | custom-call | flops 301989888 | bytes 1376256 | tf_op jit(solution)/shard_map/score_partner/pallas_call | solution.py:177
  19.4 0.2 collective-permute-start.8
  19.6 1.5 %collective-permute-start.11 = (f32[2,128]{1,0:T(2,128)S(1)}, f32[2,128]{1,0:T(2,128)S(1)}, u32[]{:S(2)}, u32[]{:S(2)}) collective-permute-start(f32[2,128]{1,0:T(2,128)S(1)} %get-tuple-element.28), channel_id=1, source_target_pairs={{0,4},{1,5},{2,6},{3,7},{4,0},{5,1},{6,2},{7,3},{8,12},{9,13},{10,... | collective-permute-start | bytes 3080 | tf_op jit(solution)/shard_map/ppermute | solution.py:213
  21.1 2.4 %collective-permute-start.10 = (f32[1,128]{1,0:T(1,128)S(1)}, f32[1,128]{1,0:T(1,128)S(1)}, u32[]{:S(2)}, u32[]{:S(2)}) collective-permute-start(f32[1,128]{1,0:T(1,128)S(1)} %get-tuple-element.30), channel_id=1, source_target_pairs={{8,0},{9,1},{10,2},{11,3},{12,4},{13,5},{14,6},{15,7},{16,8},{17,9... | collective-permute-start | bytes 1544 | tf_op jit(solution)/shard_map/ppermute | solution.py:209
  23.5 0.4 %collective-permute-start.9 = (f32[1,128]{1,0:T(1,128)S(1)}, f32[1,128]{1,0:T(1,128)S(1)}, u32[]{:S(2)}, u32[]{:S(2)}) collective-permute-start(f32[1,128]{1,0:T(1,128)S(1)} %get-tuple-element.29), channel_id=1, source_target_pairs={{0,16},{1,17},{2,18},{3,19},{4,20},{5,21},{6,22},{7,23},{24,8},{25... | collective-permute-start | bytes 1544 | tf_op jit(solution)/shard_map/ppermute | solution.py:209
  23.9 1.5 %collective-permute-start.12 = (f32[1,128]{1,0:T(1,128)S(1)}, f32[1,128]{1,0:T(1,128)S(1)}, u32[]{:S(2)}, u32[]{:S(2)}) collective-permute-start(f32[1,128]{1,0:T(1,128)S(1)} %slice.19), channel_id=1, source_target_pairs={{0,2},{1,3},{2,0},{3,1},{4,6},{5,7},{6,4},{7,5},{8,10},{9,11},{10,... | collective-permute-start | bytes 1544 | tf_op jit(solution)/shard_map/ppermute | solution.py:213
  25.5 1.6 %collective-permute-done.9 = f32[1,128]{1,0:T(1,128)S(1)} collective-permute-done((f32[1,128]{1,0:T(1,128)S(1)}, f32[1,128]{1,0:T(1,128)S(1)}, u32[]{:S(2)}, u32[]{:S(2)}) %collective-permute-start.9) | collective-permute-done | bytes 544 | tf_op jit(solution)/shard_map/ppermute | solution.py:209
  27.1 0.5 %collective-permute-done.12 = f32[1,128]{1,0:T(1,128)S(1)} collective-permute-done((f32[1,128]{1,0:T(1,128)S(1)}, f32[1,128]{1,0:T(1,128)S(1)}, u32[]{:S(2)}, u32[]{:S(2)}) %collective-permute-start.12) | collective-permute-done | bytes 544 | tf_op jit(solution)/shard_map/ppermute | solution.py:213
  27.5 0.5 %maximum_bitcast_fusion = f32[128]{0:T(128)} fusion(f32[1,128]{1,0:T(1,128)S(1)} %collective-permute-done.12, f32[1,128]{1,0:T(1,128)S(1)} %maximum_maximum_fusion, f32[2,128]{1,0:T(2,128)S(1)} %max.21), kind=kLoop, calls=%fused_computation | loop fusion | flops 256 | bytes 2048 | tf_op jit(solution)/shard_map/reshape | solution.py:257
  (12 shorter events, 0.0 us)
Async XLA Ops:
  2.6 11.3 %collective-permute-start.3 = (bf16[832,128]{1,0:T(8,128)(2,1)S(1)}, bf16[832,128]{1,0:T(8,128)(2,1)S(1)}, u32[]{:S(2)}, u32[]{:S(2)}) collective-permute-start(bf16[832,128]{1,0:T(8,128)(2,1)S(1)} %get-tuple-element.19), channel_id=1, source_target_pairs={{0,8},{1,9},{2,10},{3,11},{4,12},{5,13},{6,14},{7,15},{8,16},{9,17... | collective-permute-start | bytes 638984 | tf_op jit(solution)/shard_map/ppermute | solution.py:209
  5.6 6.5 %collective-permute-start = (bf16[784,128]{1,0:T(8,128)(2,1)S(1)}, bf16[784,128]{1,0:T(8,128)(2,1)S(1)}, u32[]{:S(2)}, u32[]{:S(2)}) collective-permute-start(bf16[784,128]{1,0:T(8,128)(2,1)S(1)} %get-tuple-element.17.refs_0_.refs_2_), channel_id=1, source_target_pairs={{0,4},{1,5},{2,6},{3,7},{4,0},{5,1},{6,2},{7,3},{8,12},{9,13},{10,... | collective-permute-start | bytes 602120 | tf_op jit(solution)/shard_map/ppermute | solution.py:213
  7.2 7.3 %collective-permute-start.1 = (bf16[784,128]{1,0:T(8,128)(2,1)S(1)}, bf16[784,128]{1,0:T(8,128)(2,1)S(1)}, u32[]{:S(2)}, u32[]{:S(2)}) collective-permute-start(bf16[784,128]{1,0:T(8,128)(2,1)S(1)} %get-tuple-element.17.refs_0_.refs_2_), channel_id=1, source_target_pairs={{0,2},{1,3},{2,0},{3,1},{4,6},{5,7},{6,4},{7,5},{8,10},{9,11},{10,... | collective-permute-start | bytes 602120 | tf_op jit(solution)/shard_map/ppermute | solution.py:213
  8.7 8.6 %collective-permute-start.4 = (bf16[784,128]{1,0:T(8,128)(2,1)S(1)}, bf16[784,128]{1,0:T(8,128)(2,1)S(1)}, u32[]{:S(2)}, u32[]{:S(2)}) collective-permute-start(bf16[784,128]{1,0:T(8,128)(2,1)S(1)} %get-tuple-element.17.refs_0_.refs_2_), channel_id=1, source_target_pairs={{16,0},{17,1},{18,2},{19,3},{20,4},{21,5},{22,6},{23,7},{8,24},{9,... | collective-permute-start | bytes 602120 | tf_op jit(solution)/shard_map/ppermute | solution.py:209
  12.1 5.7 %collective-permute-start.2 = (bf16[784,128]{1,0:T(8,128)(2,1)S(1)}, bf16[784,128]{1,0:T(8,128)(2,1)S(1)}, u32[]{:S(2)}, u32[]{:S(2)}) collective-permute-start(bf16[784,128]{1,0:T(8,128)(2,1)S(1)} %collective-permute-done.refs_1_.refs_2_), channel_id=1, source_target_pairs={{0,2},{1,3},{2,0},{3,1},{4,6},{5,7},{6,4},{7,5},{8,10},{9,11},{10,... | collective-permute-start | bytes 602120 | tf_op jit(solution)/shard_map/ppermute | solution.py:213
  13.9 4.8 %collective-permute-start.6 = (bf16[832,128]{1,0:T(8,128)(2,1)S(1)}, bf16[832,128]{1,0:T(8,128)(2,1)S(1)}, u32[]{:S(2)}, u32[]{:S(2)}) collective-permute-start(bf16[832,128]{1,0:T(8,128)(2,1)S(1)} %collective-permute-done.3.refs_5_), channel_id=1, source_target_pairs={{0,1},{1,0},{2,3},{3,2},{4,5},{5,4},{6,7},{7,6},{8,9},{9,8},{10,11... | collective-permute-start | bytes 638984 | tf_op jit(solution)/shard_map/ppermute | solution.py:213
  14.0 4.4 %collective-permute-start.5 = (bf16[784,128]{1,0:T(8,128)(2,1)S(1)}, bf16[784,128]{1,0:T(8,128)(2,1)S(1)}, u32[]{:S(2)}, u32[]{:S(2)}) collective-permute-start(bf16[784,128]{1,0:T(8,128)(2,1)S(1)} %get-tuple-element.18.refs_0_.refs_4_), channel_id=1, source_target_pairs={{0,1},{1,0},{2,3},{3,2},{4,5},{5,4},{6,7},{7,6},{8,9},{9,8},{10,11... | collective-permute-start | bytes 602120 | tf_op jit(solution)/shard_map/ppermute | solution.py:213
  17.2 1.4 %collective-permute-start.7 = (bf16[784,128]{1,0:T(8,128)(2,1)S(1)}, bf16[784,128]{1,0:T(8,128)(2,1)S(1)}, u32[]{:S(2)}, u32[]{:S(2)}) collective-permute-start(bf16[784,128]{1,0:T(8,128)(2,1)S(1)} %collective-permute-done.4.refs_6_), channel_id=1, source_target_pairs={{0,1},{1,0},{2,3},{3,2},{4,5},{5,4},{6,7},{7,6},{8,9},{9,8},{10,11... | collective-permute-start | bytes 602120 | tf_op jit(solution)/shard_map/ppermute | solution.py:213
  19.4 1.7 %collective-permute-start.8 = (f32[3,128]{1,0:T(4,128)S(1)}, f32[3,128]{1,0:T(4,128)S(1)}, u32[]{:S(2)}, u32[]{:S(2)}) collective-permute-start(f32[3,128]{1,0:T(4,128)S(1)} %get-tuple-element.26), channel_id=1, source_target_pairs={{0,1},{1,0},{2,3},{3,2},{4,5},{5,4},{6,7},{7,6},{8,9},{9,8},{10,11... | collective-permute-start | bytes 4616 | tf_op jit(solution)/shard_map/ppermute | solution.py:213
  19.6 4.4 %collective-permute-start.11 = (f32[2,128]{1,0:T(2,128)S(1)}, f32[2,128]{1,0:T(2,128)S(1)}, u32[]{:S(2)}, u32[]{:S(2)}) collective-permute-start(f32[2,128]{1,0:T(2,128)S(1)} %get-tuple-element.28), channel_id=1, source_target_pairs={{0,4},{1,5},{2,6},{3,7},{4,0},{5,1},{6,2},{7,3},{8,12},{9,13},{10,... | collective-permute-start | bytes 3080 | tf_op jit(solution)/shard_map/ppermute | solution.py:213
  21.1 4.4 %collective-permute-start.10 = (f32[1,128]{1,0:T(1,128)S(1)}, f32[1,128]{1,0:T(1,128)S(1)}, u32[]{:S(2)}, u32[]{:S(2)}) collective-permute-start(f32[1,128]{1,0:T(1,128)S(1)} %get-tuple-element.30), channel_id=1, source_target_pairs={{8,0},{9,1},{10,2},{11,3},{12,4},{13,5},{14,6},{15,7},{16,8},{17,9... | collective-permute-start | bytes 1544 | tf_op jit(solution)/shard_map/ppermute | solution.py:209
  23.5 3.5 %collective-permute-start.9 = (f32[1,128]{1,0:T(1,128)S(1)}, f32[1,128]{1,0:T(1,128)S(1)}, u32[]{:S(2)}, u32[]{:S(2)}) collective-permute-start(f32[1,128]{1,0:T(1,128)S(1)} %get-tuple-element.29), channel_id=1, source_target_pairs={{0,16},{1,17},{2,18},{3,19},{4,20},{5,21},{6,22},{7,23},{24,8},{25... | collective-permute-start | bytes 1544 | tf_op jit(solution)/shard_map/ppermute | solution.py:209
  23.9 3.6 %collective-permute-start.12 = (f32[1,128]{1,0:T(1,128)S(1)}, f32[1,128]{1,0:T(1,128)S(1)}, u32[]{:S(2)}, u32[]{:S(2)}) collective-permute-start(f32[1,128]{1,0:T(1,128)S(1)} %slice.19), channel_id=1, source_target_pairs={{0,2},{1,3},{2,0},{3,1},{4,6},{5,7},{6,4},{7,5},{8,10},{9,11},{10,... | collective-permute-start | bytes 1544 | tf_op jit(solution)/shard_map/ppermute | solution.py:213

commit v10 on v9

--- a/solution.py
+++ b/solution.py
@@ -11,7 +11,7 @@
 NOTE_ROWS = 16
 MORE_ROWS = 48
 RADIX = 256
-CHUNKS = 4
+CHUNKS = 2
 VMEM = pl.BlockSpec(memory_space=pltpu.VMEM)
 HBM = pl.BlockSpec(memory_space=pltpu.HBM)
 
@@ -231,12 +231,11 @@
     every, count = tuple(range(len(lanes))), len(row_blocks)
     half = count // 2
     soon = (0, half)
-    rest = tuple(i for i in range(count) if i not in soon)
     lines, held = score(
         "score_soon", [row_blocks[i] for i in soon], lanes[:1], [((0, 1), (0,))], [], hold=True
     )
     row_blocks[0] = lanes[0] = held
-    products = [(rest, every), (soon, every[1:])]
+    products = [(tuple(range(count)), every)]
     lines, *state = score("score_late", row_blocks, lanes, products, [], lines, hand_on=True)
     partner = [held]
     partner += [lax.optimization_barrier((visitor, held))[0] for visitor in visitors[:-1]]

time: 28.2 us -> 28.9 us (1.025)
  waiting for transfers between devices: 7.46 us -> 9.14 us
  starting transfers between devices: 15.8 us -> 14.4 us
  Pallas kernels: 4.22 us -> 4.62 us
    ppermute x4, waiting for transfers between devices: 4.32 us -> 7.13 us  [move(): return lax.ppermute(array, AXES, whole)]
    ppermute x4, starting transfers between devices: 7.47 us -> 5.49 us  [move(): return lax.ppermute(array, AXES, whole)]
    ppermute x9, waiting for transfers between devices: 3.14 us -> 2.01 us  [swap(): return lax.ppermute(array, AXES, pairs)]
    ppermute x9, starting transfers between devices: 8.31 us -> 8.93 us  [swap(): return lax.ppermute(array, AXES, pairs)]
  transfers between devices with their start and end apart: 13 -> 13, of which waited for: 6 -> 8; matrix products, arithmetic and copies ran while one was open for 0% -> 0% of each run, Pallas kernels for 3% -> 4%
where the time goes in v10:
time: 28.9 us; the launch traced here: 28.8 us
  starting transfers between devices  14.4 us (50%)
  waiting for transfers between devices  9.14 us (32%)
  Pallas kernels  4.62 us (16%)
  other arithmetic  0.52 us (2%)
    ppermute x9, starting transfers between devices, swap(): return lax.ppermute(array, AXES, pairs)  8.93 us
    ppermute x4, waiting for transfers between devices, move(): return lax.ppermute(array, AXES, whole)  7.13 us
    ppermute x4, starting transfers between devices, move(): return lax.ppermute(array, AXES, whole)  5.49 us
    pallas_call x1, Pallas kernels, embed(): pl.pallas_call(embed_kernel, in_specs=[HBM] * 5, out_specs=[VMEM] * 2, ou...  2.84 us
    ppermute x9, waiting for transfers between devices, swap(): return lax.ppermute(array, AXES, pairs)  2.01 us
    pallas_call x3, Pallas kernels, score(): pl.pallas_call(lambda *refs: score_kernel(*counts, *rest, *refs), in_spec...  1.77 us
  transfers between devices with their start and end apart: 13, of which 8 were waited for; matrix products, arithmetic and copies ran while one was open for 0% of the time, Pallas kernels for 4%

profile of v10, /device:TPU:0, one launch (start us, length us, event | category | flops | bytes accessed | tf_op | source)
XLA Modules:
  0.0 28.8 jit_solution(9439559287323624603)
XLA Ops:
  0.0 2.8 %embed.1 = (bf16[784,128]{1,0:T(8,128)(2,1)S(1)}, bf16[832,128]{1,0:T(8,128)(2,1)S(1)}) custom-call(bf16[128,2048]{1,0:T(8,128)(2,1)} %states_hbm.1, bf16[2048,768]{1,0:T(8,128)(2,1)} %proj_hbm.1, s32[1,128]{1,0:T(1,128)} %bitcast.5, s32[1,128]{1,0:T(1,128)} %bitcast.6, s32[1,128]{1,0:T(1,128)} %bitcast.7), custom_call_target="tpu_custom_call" | custom-call | tf_op jit(solution)/shard_map/embed/pallas_call | solution.py:66
  2.9 3.0 %collective-permute-start = (bf16[784,128]{1,0:T(8,128)(2,1)S(1)}, bf16[784,128]{1,0:T(8,128)(2,1)S(1)}, u32[]{:S(2)}, u32[]{:S(2)}) collective-permute-start(bf16[784,128]{1,0:T(8,128)(2,1)S(1)} %get-tuple-element.17.refs_0_.refs_2_), channel_id=1, source_target_pairs={{0,4},{1,5},{2,6},{3,7},{4,0},{5,1},{6,2},{7,3},{8,12},{9,13},{10,... | collective-permute-start | bytes 602120 | tf_op jit(solution)/shard_map/ppermute | solution.py:213
  5.9 1.6 %collective-permute-start.3 = (bf16[832,128]{1,0:T(8,128)(2,1)S(1)}, bf16[832,128]{1,0:T(8,128)(2,1)S(1)}, u32[]{:S(2)}, u32[]{:S(2)}) collective-permute-start(bf16[832,128]{1,0:T(8,128)(2,1)S(1)} %get-tuple-element.19), channel_id=1, source_target_pairs={{0,8},{1,9},{2,10},{3,11},{4,12},{5,13},{6,14},{7,15},{8,16},{9,17... | collective-permute-start | bytes 638984 | tf_op jit(solution)/shard_map/ppermute | solution.py:209
  7.5 1.5 %collective-permute-start.1 = (bf16[784,128]{1,0:T(8,128)(2,1)S(1)}, bf16[784,128]{1,0:T(8,128)(2,1)S(1)}, u32[]{:S(2)}, u32[]{:S(2)}) collective-permute-start(bf16[784,128]{1,0:T(8,128)(2,1)S(1)} %get-tuple-element.17.refs_0_.refs_2_), channel_id=1, source_target_pairs={{0,2},{1,3},{2,0},{3,1},{4,6},{5,7},{6,4},{7,5},{8,10},{9,11},{10,... | collective-permute-start | bytes 602120 | tf_op jit(solution)/shard_map/ppermute | solution.py:213
  9.0 1.6 %collective-permute-start.4 = (bf16[784,128]{1,0:T(8,128)(2,1)S(1)}, bf16[784,128]{1,0:T(8,128)(2,1)S(1)}, u32[]{:S(2)}, u32[]{:S(2)}) collective-permute-start(bf16[784,128]{1,0:T(8,128)(2,1)S(1)} %get-tuple-element.17.refs_0_.refs_2_), channel_id=1, source_target_pairs={{16,0},{17,1},{18,2},{19,3},{20,4},{21,5},{22,6},{23,7},{8,24},{9,... | collective-permute-start | bytes 602120 | tf_op jit(solution)/shard_map/ppermute | solution.py:209
  10.5 0.3 %collective-permute-done.refs_1_.refs_2_ = bf16[784,128]{1,0:T(8,128)(2,1)S(1)} collective-permute-done((bf16[784,128]{1,0:T(8,128)(2,1)S(1)}, bf16[784,128]{1,0:T(8,128)(2,1)S(1)}, u32[]{:S(2)}, u32[]{:S(2)}) %collective-permute-start) | collective-permute-done | bytes 200736 | tf_op jit(solution)/shard_map/ppermute | solution.py:213
  10.9 1.7 %collective-permute-start.2 = (bf16[784,128]{1,0:T(8,128)(2,1)S(1)}, bf16[784,128]{1,0:T(8,128)(2,1)S(1)}, u32[]{:S(2)}, u32[]{:S(2)}) collective-permute-start(bf16[784,128]{1,0:T(8,128)(2,1)S(1)} %collective-permute-done.refs_1_.refs_2_), channel_id=1, source_target_pairs={{0,2},{1,3},{2,0},{3,1},{4,6},{5,7},{6,4},{7,5},{8,10},{9,11},{10,... | collective-permute-start | bytes 602120 | tf_op jit(solution)/shard_map/ppermute | solution.py:213
  12.6 0.3 %score_soon.1 = (f32[1,128]{1,0:T(1,128)S(1)}, bf16[784,128]{1,0:T(8,128)(2,1)S(1)}) custom-call(bf16[784,128]{1,0:T(8,128)(2,1)S(1)} %get-tuple-element.17.refs_0_.refs_2_, bf16[784,128]{1,0:T(8,128)(2,1)S(1)} %collective-permute-done.refs_1_.refs_2_, bf16[784,128]{1,0:T(8,128)(2,1)S(1)} %get-tuple-element.17.refs_0_.refs_2_), custom_call_target="tpu_custom_call" | custom-call | flops 50331648 | bytes 589824 | tf_op jit(solution)/shard_map/score_soon/pallas_call | solution.py:177
  12.9 3.0 %collective-permute-done.3.refs_5_ = bf16[832,128]{1,0:T(8,128)(2,1)S(1)} collective-permute-done((bf16[832,128]{1,0:T(8,128)(2,1)S(1)}, bf16[832,128]{1,0:T(8,128)(2,1)S(1)}, u32[]{:S(2)}, u32[]{:S(2)}) %collective-permute-start.3) | collective-permute-done | bytes 213024 | tf_op jit(solution)/shard_map/ppermute | solution.py:209
  15.9 0.0 collective-permute-start.6
  15.9 0.5 %collective-permute-start.5 = (bf16[784,128]{1,0:T(8,128)(2,1)S(1)}, bf16[784,128]{1,0:T(8,128)(2,1)S(1)}, u32[]{:S(2)}, u32[]{:S(2)}) collective-permute-start(bf16[784,128]{1,0:T(8,128)(2,1)S(1)} %get-tuple-element.18.refs_0_.refs_4_), channel_id=1, source_target_pairs={{0,1},{1,0},{2,3},{3,2},{4,5},{5,4},{6,7},{7,6},{8,9},{9,8},{10,11... | collective-permute-start | bytes 602120 | tf_op jit(solution)/shard_map/ppermute | solution.py:213
  16.4 2.4 %collective-permute-done.4.refs_6_ = bf16[784,128]{1,0:T(8,128)(2,1)S(1)} collective-permute-done((bf16[784,128]{1,0:T(8,128)(2,1)S(1)}, bf16[784,128]{1,0:T(8,128)(2,1)S(1)}, u32[]{:S(2)}, u32[]{:S(2)}) %collective-permute-start.4) | collective-permute-done | bytes 200736 | tf_op jit(solution)/shard_map/ppermute | solution.py:209
  18.8 0.7 %score_late.1 = (f32[3,128]{1,0:T(4,128)S(1)}, f32[128,128]{1,0:T(8,128)S(1)}, f32[128,8]{1,0:T(8,128)S(1)}) custom-call(bf16[784,128]{1,0:T(8,128)(2,1)S(1)} %get-tuple-element.18.refs_0_.refs_4_, bf16[784,128]{1,0:T(8,128)(2,1)S(1)} %collective-permute-done.1.refs_1_, bf16[784,128]{1,0:T(8,128)(2,1)S(1)} %collective-permute-done.refs_1_.refs_2_, ...), custom_call_target="tpu_custom_call" | custom-call | flops 301989888 | bytes 1376256 | tf_op jit(solution)/shard_map/score_late/pallas_call | solution.py:177
  19.5 0.7 %collective-permute-done.7.refs_6_ = bf16[784,128]{1,0:T(8,128)(2,1)S(1)} collective-permute-done((bf16[784,128]{1,0:T(8,128)(2,1)S(1)}, bf16[784,128]{1,0:T(8,128)(2,1)S(1)}, u32[]{:S(2)}, u32[]{:S(2)}) %collective-permute-start.7) | collective-permute-done | bytes 200736 | tf_op jit(solution)/shard_map/ppermute | solution.py:213
  20.2 0.7 %score_partner.1 = (f32[3,128]{1,0:T(4,128)S(1)}, f32[2,128]{1,0:T(2,128)S(1)}, f32[2,128]{1,0:T(2,128)S(1)}) custom-call(bf16[784,128]{1,0:T(8,128)(2,1)S(1)} %get-tuple-element.18.refs_0_.refs_4_, bf16[784,128]{1,0:T(8,128)(2,1)S(1)} %collective-permute-done.1.refs_1_, bf16[784,128]{1,0:T(8,128)(2,1)S(1)} %collective-permute-done.refs_1_.refs_2_, ...), custom_call_target="tpu_custom_call" | custom-call | flops 301989888 | bytes 1376256 | tf_op jit(solution)/shard_map/score_partner/pallas_call | solution.py:177
  20.9 0.2 collective-permute-start.8
  21.1 0.5 %collective-permute-start.11 = (f32[2,128]{1,0:T(2,128)S(1)}, f32[2,128]{1,0:T(2,128)S(1)}, u32[]{:S(2)}, u32[]{:S(2)}) collective-permute-start(f32[2,128]{1,0:T(2,128)S(1)} %get-tuple-element.28), channel_id=1, source_target_pairs={{0,4},{1,5},{2,6},{3,7},{4,0},{5,1},{6,2},{7,3},{8,12},{9,13},{10,... | collective-permute-start | bytes 3080 | tf_op jit(solution)/shard_map/ppermute | solution.py:213
  21.6 0.5 %collective-permute-done.8 = f32[3,128]{1,0:T(4,128)S(1)} collective-permute-done((f32[3,128]{1,0:T(4,128)S(1)}, f32[3,128]{1,0:T(4,128)S(1)}, u32[]{:S(2)}, u32[]{:S(2)}) %collective-permute-start.8) | collective-permute-done | bytes 1568 | tf_op jit(solution)/shard_map/ppermute | solution.py:213
  22.1 2.3 %collective-permute-start.10 = (f32[1,128]{1,0:T(1,128)S(1)}, f32[1,128]{1,0:T(1,128)S(1)}, u32[]{:S(2)}, u32[]{:S(2)}) collective-permute-start(f32[1,128]{1,0:T(1,128)S(1)} %get-tuple-element.30), channel_id=1, source_target_pairs={{8,0},{9,1},{10,2},{11,3},{12,4},{13,5},{14,6},{15,7},{16,8},{17,9... | collective-permute-start | bytes 1544 | tf_op jit(solution)/shard_map/ppermute | solution.py:209
  24.5 0.2 collective-permute-done.11
  24.7 1.5 %collective-permute-start.12 = (f32[1,128]{1,0:T(1,128)S(1)}, f32[1,128]{1,0:T(1,128)S(1)}, u32[]{:S(2)}, u32[]{:S(2)}) collective-permute-start(f32[1,128]{1,0:T(1,128)S(1)} %slice.19), channel_id=1, source_target_pairs={{0,2},{1,3},{2,0},{3,1},{4,6},{5,7},{6,4},{7,5},{8,10},{9,11},{10,... | collective-permute-start | bytes 1544 | tf_op jit(solution)/shard_map/ppermute | solution.py:213
  26.2 1.8 %collective-permute-done.9 = f32[1,128]{1,0:T(1,128)S(1)} collective-permute-done((f32[1,128]{1,0:T(1,128)S(1)}, f32[1,128]{1,0:T(1,128)S(1)}, u32[]{:S(2)}, u32[]{:S(2)}) %collective-permute-start.9) | collective-permute-done | bytes 544 | tf_op jit(solution)/shard_map/ppermute | solution.py:209
  28.0 0.2 collective-permute-done.12
  28.2 0.5 %maximum_bitcast_fusion = f32[128]{0:T(128)} fusion(f32[1,128]{1,0:T(1,128)S(1)} %collective-permute-done.12, f32[1,128]{1,0:T(1,128)S(1)} %maximum_maximum_fusion, f32[2,128]{1,0:T(2,128)S(1)} %max.21), kind=kLoop, calls=%fused_computation | loop fusion | flops 256 | bytes 2048 | tf_op jit(solution)/shard_map/reshape | solution.py:256
  (12 shorter events, 0.0 us)
Async XLA Ops:
  2.9 8.0 %collective-permute-start = (bf16[784,128]{1,0:T(8,128)(2,1)S(1)}, bf16[784,128]{1,0:T(8,128)(2,1)S(1)}, u32[]{:S(2)}, u32[]{:S(2)}) collective-permute-start(bf16[784,128]{1,0:T(8,128)(2,1)S(1)} %get-tuple-element.17.refs_0_.refs_2_), channel_id=1, source_target_pairs={{0,4},{1,5},{2,6},{3,7},{4,0},{5,1},{6,2},{7,3},{8,12},{9,13},{10,... | collective-permute-start | bytes 602120 | tf_op jit(solution)/shard_map/ppermute | solution.py:213
  5.9 10.0 %collective-permute-start.3 = (bf16[832,128]{1,0:T(8,128)(2,1)S(1)}, bf16[832,128]{1,0:T(8,128)(2,1)S(1)}, u32[]{:S(2)}, u32[]{:S(2)}) collective-permute-start(bf16[832,128]{1,0:T(8,128)(2,1)S(1)} %get-tuple-element.19), channel_id=1, source_target_pairs={{0,8},{1,9},{2,10},{3,11},{4,12},{5,13},{6,14},{7,15},{8,16},{9,17... | collective-permute-start | bytes 638984 | tf_op jit(solution)/shard_map/ppermute | solution.py:209
  7.5 8.9 %collective-permute-start.1 = (bf16[784,128]{1,0:T(8,128)(2,1)S(1)}, bf16[784,128]{1,0:T(8,128)(2,1)S(1)}, u32[]{:S(2)}, u32[]{:S(2)}) collective-permute-start(bf16[784,128]{1,0:T(8,128)(2,1)S(1)} %get-tuple-element.17.refs_0_.refs_2_), channel_id=1, source_target_pairs={{0,2},{1,3},{2,0},{3,1},{4,6},{5,7},{6,4},{7,5},{8,10},{9,11},{10,... | collective-permute-start | bytes 602120 | tf_op jit(solution)/shard_map/ppermute | solution.py:213
  9.0 9.8 %collective-permute-start.4 = (bf16[784,128]{1,0:T(8,128)(2,1)S(1)}, bf16[784,128]{1,0:T(8,128)(2,1)S(1)}, u32[]{:S(2)}, u32[]{:S(2)}) collective-permute-start(bf16[784,128]{1,0:T(8,128)(2,1)S(1)} %get-tuple-element.17.refs_0_.refs_2_), channel_id=1, source_target_pairs={{16,0},{17,1},{18,2},{19,3},{20,4},{21,5},{22,6},{23,7},{8,24},{9,... | collective-permute-start | bytes 602120 | tf_op jit(solution)/shard_map/ppermute | solution.py:209
  10.9 7.9 %collective-permute-start.2 = (bf16[784,128]{1,0:T(8,128)(2,1)S(1)}, bf16[784,128]{1,0:T(8,128)(2,1)S(1)}, u32[]{:S(2)}, u32[]{:S(2)}) collective-permute-start(bf16[784,128]{1,0:T(8,128)(2,1)S(1)} %collective-permute-done.refs_1_.refs_2_), channel_id=1, source_target_pairs={{0,2},{1,3},{2,0},{3,1},{4,6},{5,7},{6,4},{7,5},{8,10},{9,11},{10,... | collective-permute-start | bytes 602120 | tf_op jit(solution)/shard_map/ppermute | solution.py:213
  15.9 4.3 %collective-permute-start.6 = (bf16[832,128]{1,0:T(8,128)(2,1)S(1)}, bf16[832,128]{1,0:T(8,128)(2,1)S(1)}, u32[]{:S(2)}, u32[]{:S(2)}) collective-permute-start(bf16[832,128]{1,0:T(8,128)(2,1)S(1)} %collective-permute-done.3.refs_5_), channel_id=1, source_target_pairs={{0,1},{1,0},{2,3},{3,2},{4,5},{5,4},{6,7},{7,6},{8,9},{9,8},{10,11... | collective-permute-start | bytes 638984 | tf_op jit(solution)/shard_map/ppermute | solution.py:213
  15.9 3.6 %collective-permute-start.5 = (bf16[784,128]{1,0:T(8,128)(2,1)S(1)}, bf16[784,128]{1,0:T(8,128)(2,1)S(1)}, u32[]{:S(2)}, u32[]{:S(2)}) collective-permute-start(bf16[784,128]{1,0:T(8,128)(2,1)S(1)} %get-tuple-element.18.refs_0_.refs_4_), channel_id=1, source_target_pairs={{0,1},{1,0},{2,3},{3,2},{4,5},{5,4},{6,7},{7,6},{8,9},{9,8},{10,11... | collective-permute-start | bytes 602120 | tf_op jit(solution)/shard_map/ppermute | solution.py:213
  18.8 1.4 %collective-permute-start.7 = (bf16[784,128]{1,0:T(8,128)(2,1)S(1)}, bf16[784,128]{1,0:T(8,128)(2,1)S(1)}, u32[]{:S(2)}, u32[]{:S(2)}) collective-permute-start(bf16[784,128]{1,0:T(8,128)(2,1)S(1)} %collective-permute-done.4.refs_6_), channel_id=1, source_target_pairs={{0,1},{1,0},{2,3},{3,2},{4,5},{5,4},{6,7},{7,6},{8,9},{9,8},{10,11... | collective-permute-start | bytes 602120 | tf_op jit(solution)/shard_map/ppermute | solution.py:213
  20.9 1.2 %collective-permute-start.8 = (f32[3,128]{1,0:T(4,128)S(1)}, f32[3,128]{1,0:T(4,128)S(1)}, u32[]{:S(2)}, u32[]{:S(2)}) collective-permute-start(f32[3,128]{1,0:T(4,128)S(1)} %get-tuple-element.26), channel_id=1, source_target_pairs={{0,1},{1,0},{2,3},{3,2},{4,5},{5,4},{6,7},{7,6},{8,9},{9,8},{10,11... | collective-permute-start | bytes 4616 | tf_op jit(solution)/shard_map/ppermute | solution.py:213
  21.1 3.6 %collective-permute-start.11 = (f32[2,128]{1,0:T(2,128)S(1)}, f32[2,128]{1,0:T(2,128)S(1)}, u32[]{:S(2)}, u32[]{:S(2)}) collective-permute-start(f32[2,128]{1,0:T(2,128)S(1)} %get-tuple-element.28), channel_id=1, source_target_pairs={{0,4},{1,5},{2,6},{3,7},{4,0},{5,1},{6,2},{7,3},{8,12},{9,13},{10,... | collective-permute-start | bytes 3080 | tf_op jit(solution)/shard_map/ppermute | solution.py:213
  22.1 4.1 %collective-permute-start.10 = (f32[1,128]{1,0:T(1,128)S(1)}, f32[1,128]{1,0:T(1,128)S(1)}, u32[]{:S(2)}, u32[]{:S(2)}) collective-permute-start(f32[1,128]{1,0:T(1,128)S(1)} %get-tuple-element.30), channel_id=1, source_target_pairs={{8,0},{9,1},{10,2},{11,3},{12,4},{13,5},{14,6},{15,7},{16,8},{17,9... | collective-permute-start | bytes 1544 | tf_op jit(solution)/shard_map/ppermute | solution.py:209
  24.5 3.5 %collective-permute-start.9 = (f32[1,128]{1,0:T(1,128)S(1)}, f32[1,128]{1,0:T(1,128)S(1)}, u32[]{:S(2)}, u32[]{:S(2)}) collective-permute-start(f32[1,128]{1,0:T(1,128)S(1)} %get-tuple-element.29), channel_id=1, source_target_pairs={{0,16},{1,17},{2,18},{3,19},{4,20},{5,21},{6,22},{7,23},{24,8},{25... | collective-permute-start | bytes 1544 | tf_op jit(solution)/shard_map/ppermute | solution.py:209
  24.7 3.5 %collective-permute-start.12 = (f32[1,128]{1,0:T(1,128)S(1)}, f32[1,128]{1,0:T(1,128)S(1)}, u32[]{:S(2)}, u32[]{:S(2)}) collective-permute-start(f32[1,128]{1,0:T(1,128)S(1)} %slice.19), channel_id=1, source_target_pairs={{0,2},{1,3},{2,0},{3,1},{4,6},{5,7},{6,4},{7,5},{8,10},{9,11},{10,... | collective-permute-start | bytes 1544 | tf_op jit(solution)/shard_map/ppermute | solution.py:213

commit v11 on v9

--- a/solution.py
+++ b/solution.py
@@ -11,7 +11,7 @@
 NOTE_ROWS = 16
 MORE_ROWS = 48
 RADIX = 256
-CHUNKS = 4
+CHUNKS = 8
 VMEM = pl.BlockSpec(memory_space=pltpu.VMEM)
 HBM = pl.BlockSpec(memory_space=pltpu.HBM)
 

time: 28.2 us -> 28.3 us (level)
  no operation moved by 1% of the time
where the time goes in v11:
time: 28.3 us; the launch traced here: 28.1 us
  starting transfers between devices  15.8 us (56%)
  waiting for transfers between devices  7.42 us (26%)
  Pallas kernels  4.31 us (15%)
  other arithmetic  0.52 us (2%)
    ppermute x9, starting transfers between devices, swap(): return lax.ppermute(array, AXES, pairs)  8.34 us
    ppermute x4, starting transfers between devices, move(): return lax.ppermute(array, AXES, whole)  7.47 us
    ppermute x4, waiting for transfers between devices, move(): return lax.ppermute(array, AXES, whole)  4.3 us
    ppermute x9, waiting for transfers between devices, swap(): return lax.ppermute(array, AXES, pairs)  3.12 us
    pallas_call x1, Pallas kernels, embed(): pl.pallas_call(embed_kernel, in_specs=[HBM] * 5, out_specs=[VMEM] * 2, ou...  2.64 us
    pallas_call x3, Pallas kernels, score(): pl.pallas_call(lambda *refs: score_kernel(*counts, *rest, *refs), in_spec...  1.67 us
  transfers between devices with their start and end apart: 13, of which 6 were waited for; matrix products, arithmetic and copies ran while one was open for 0% of the time, Pallas kernels for 3%

profile of v11, /device:TPU:0, one launch (start us, length us, event | category | flops | bytes accessed | tf_op | source)
XLA Modules:
  0.0 28.1 jit_solution(10399295943131342867)
XLA Ops:
  0.0 2.6 %embed.1 = (bf16[784,128]{1,0:T(8,128)(2,1)S(1)}, bf16[832,128]{1,0:T(8,128)(2,1)S(1)}) custom-call(bf16[128,2048]{1,0:T(8,128)(2,1)} %states_hbm.1, bf16[2048,768]{1,0:T(8,128)(2,1)} %proj_hbm.1, s32[1,128]{1,0:T(1,128)} %bitcast.5, s32[1,128]{1,0:T(1,128)} %bitcast.6, s32[1,128]{1,0:T(1,128)} %bitcast.7), custom_call_target="tpu_custom_call" | custom-call | tf_op jit(solution)/shard_map/embed/pallas_call | solution.py:66
  2.6 3.1 %collective-permute-start.3 = (bf16[832,128]{1,0:T(8,128)(2,1)S(1)}, bf16[832,128]{1,0:T(8,128)(2,1)S(1)}, u32[]{:S(2)}, u32[]{:S(2)}) collective-permute-start(bf16[832,128]{1,0:T(8,128)(2,1)S(1)} %get-tuple-element.19), channel_id=1, source_target_pairs={{0,8},{1,9},{2,10},{3,11},{4,12},{5,13},{6,14},{7,15},{8,16},{9,17... | collective-permute-start | bytes 638984 | tf_op jit(solution)/shard_map/ppermute | solution.py:209
  5.7 1.5 %collective-permute-start = (bf16[784,128]{1,0:T(8,128)(2,1)S(1)}, bf16[784,128]{1,0:T(8,128)(2,1)S(1)}, u32[]{:S(2)}, u32[]{:S(2)}) collective-permute-start(bf16[784,128]{1,0:T(8,128)(2,1)S(1)} %get-tuple-element.17.refs_0_.refs_2_), channel_id=1, source_target_pairs={{0,4},{1,5},{2,6},{3,7},{4,0},{5,1},{6,2},{7,3},{8,12},{9,13},{10,... | collective-permute-start | bytes 602120 | tf_op jit(solution)/shard_map/ppermute | solution.py:213
  7.2 1.5 %collective-permute-start.1 = (bf16[784,128]{1,0:T(8,128)(2,1)S(1)}, bf16[784,128]{1,0:T(8,128)(2,1)S(1)}, u32[]{:S(2)}, u32[]{:S(2)}) collective-permute-start(bf16[784,128]{1,0:T(8,128)(2,1)S(1)} %get-tuple-element.17.refs_0_.refs_2_), channel_id=1, source_target_pairs={{0,2},{1,3},{2,0},{3,1},{4,6},{5,7},{6,4},{7,5},{8,10},{9,11},{10,... | collective-permute-start | bytes 602120 | tf_op jit(solution)/shard_map/ppermute | solution.py:213
  8.7 1.6 %collective-permute-start.4 = (bf16[784,128]{1,0:T(8,128)(2,1)S(1)}, bf16[784,128]{1,0:T(8,128)(2,1)S(1)}, u32[]{:S(2)}, u32[]{:S(2)}) collective-permute-start(bf16[784,128]{1,0:T(8,128)(2,1)S(1)} %get-tuple-element.17.refs_0_.refs_2_), channel_id=1, source_target_pairs={{16,0},{17,1},{18,2},{19,3},{20,4},{21,5},{22,6},{23,7},{8,24},{9,... | collective-permute-start | bytes 602120 | tf_op jit(solution)/shard_map/ppermute | solution.py:209
  10.3 1.9 %collective-permute-done.refs_1_.refs_2_ = bf16[784,128]{1,0:T(8,128)(2,1)S(1)} collective-permute-done((bf16[784,128]{1,0:T(8,128)(2,1)S(1)}, bf16[784,128]{1,0:T(8,128)(2,1)S(1)}, u32[]{:S(2)}, u32[]{:S(2)}) %collective-permute-start) | collective-permute-done | bytes 200736 | tf_op jit(solution)/shard_map/ppermute | solution.py:213
  12.2 1.5 %collective-permute-start.2 = (bf16[784,128]{1,0:T(8,128)(2,1)S(1)}, bf16[784,128]{1,0:T(8,128)(2,1)S(1)}, u32[]{:S(2)}, u32[]{:S(2)}) collective-permute-start(bf16[784,128]{1,0:T(8,128)(2,1)S(1)} %collective-permute-done.refs_1_.refs_2_), channel_id=1, source_target_pairs={{0,2},{1,3},{2,0},{3,1},{4,6},{5,7},{6,4},{7,5},{8,10},{9,11},{10,... | collective-permute-start | bytes 602120 | tf_op jit(solution)/shard_map/ppermute | solution.py:213
  13.7 0.3 %score_soon.1 = (f32[1,128]{1,0:T(1,128)S(1)}, bf16[784,128]{1,0:T(8,128)(2,1)S(1)}) custom-call(bf16[784,128]{1,0:T(8,128)(2,1)S(1)} %get-tuple-element.17.refs_0_.refs_2_, bf16[784,128]{1,0:T(8,128)(2,1)S(1)} %collective-permute-done.refs_1_.refs_2_, bf16[784,128]{1,0:T(8,128)(2,1)S(1)} %get-tuple-element.17.refs_0_.refs_2_), custom_call_target="tpu_custom_call" | custom-call | flops 50331648 | bytes 589824 | tf_op jit(solution)/shard_map/score_soon/pallas_call | solution.py:177
  14.0 0.0 collective-permute-done.3.refs_5_
  14.0 0.1 collective-permute-start.6
  14.1 0.5 %collective-permute-start.5 = (bf16[784,128]{1,0:T(8,128)(2,1)S(1)}, bf16[784,128]{1,0:T(8,128)(2,1)S(1)}, u32[]{:S(2)}, u32[]{:S(2)}) collective-permute-start(bf16[784,128]{1,0:T(8,128)(2,1)S(1)} %get-tuple-element.18.refs_0_.refs_4_), channel_id=1, source_target_pairs={{0,1},{1,0},{2,3},{3,2},{4,5},{5,4},{6,7},{7,6},{8,9},{9,8},{10,11... | collective-permute-start | bytes 602120 | tf_op jit(solution)/shard_map/ppermute | solution.py:213
  14.6 2.7 %collective-permute-done.4.refs_6_ = bf16[784,128]{1,0:T(8,128)(2,1)S(1)} collective-permute-done((bf16[784,128]{1,0:T(8,128)(2,1)S(1)}, bf16[784,128]{1,0:T(8,128)(2,1)S(1)}, u32[]{:S(2)}, u32[]{:S(2)}) %collective-permute-start.4) | collective-permute-done | bytes 200736 | tf_op jit(solution)/shard_map/ppermute | solution.py:209
  17.3 0.6 %collective-permute-done.2.refs_3_ = bf16[784,128]{1,0:T(8,128)(2,1)S(1)} collective-permute-done((bf16[784,128]{1,0:T(8,128)(2,1)S(1)}, bf16[784,128]{1,0:T(8,128)(2,1)S(1)}, u32[]{:S(2)}, u32[]{:S(2)}) %collective-permute-start.2) | collective-permute-done | bytes 200736 | tf_op jit(solution)/shard_map/ppermute | solution.py:213
  17.9 0.6 %score_late.1 = (f32[3,128]{1,0:T(4,128)S(1)}, f32[128,128]{1,0:T(8,128)S(1)}, f32[128,8]{1,0:T(8,128)S(1)}) custom-call(bf16[784,128]{1,0:T(8,128)(2,1)S(1)} %get-tuple-element.18.refs_0_.refs_4_, bf16[784,128]{1,0:T(8,128)(2,1)S(1)} %collective-permute-done.1.refs_1_, bf16[784,128]{1,0:T(8,128)(2,1)S(1)} %collective-permute-done.refs_1_.refs_2_, ...), custom_call_target="tpu_custom_call" | custom-call | flops 251658240 | bytes 1376256 | tf_op jit(solution)/shard_map/score_late/pallas_call | solution.py:177
  18.5 0.2 collective-permute-done.7.refs_6_
  18.8 0.7 %score_partner.1 = (f32[3,128]{1,0:T(4,128)S(1)}, f32[2,128]{1,0:T(2,128)S(1)}, f32[2,128]{1,0:T(2,128)S(1)}) custom-call(bf16[784,128]{1,0:T(8,128)(2,1)S(1)} %get-tuple-element.18.refs_0_.refs_4_, bf16[784,128]{1,0:T(8,128)(2,1)S(1)} %collective-permute-done.1.refs_1_, bf16[784,128]{1,0:T(8,128)(2,1)S(1)} %collective-permute-done.refs_1_.refs_2_, ...), custom_call_target="tpu_custom_call" | custom-call | flops 301989888 | bytes 1376256 | tf_op jit(solution)/shard_map/score_partner/pallas_call | solution.py:177
  19.5 0.2 collective-permute-start.8
  19.6 1.5 %collective-permute-start.11 = (f32[2,128]{1,0:T(2,128)S(1)}, f32[2,128]{1,0:T(2,128)S(1)}, u32[]{:S(2)}, u32[]{:S(2)}) collective-permute-start(f32[2,128]{1,0:T(2,128)S(1)} %get-tuple-element.28), channel_id=1, source_target_pairs={{0,4},{1,5},{2,6},{3,7},{4,0},{5,1},{6,2},{7,3},{8,12},{9,13},{10,... | collective-permute-start | bytes 3080 | tf_op jit(solution)/shard_map/ppermute | solution.py:213
  21.2 2.4 %collective-permute-start.10 = (f32[1,128]{1,0:T(1,128)S(1)}, f32[1,128]{1,0:T(1,128)S(1)}, u32[]{:S(2)}, u32[]{:S(2)}) collective-permute-start(f32[1,128]{1,0:T(1,128)S(1)} %get-tuple-element.30), channel_id=1, source_target_pairs={{8,0},{9,1},{10,2},{11,3},{12,4},{13,5},{14,6},{15,7},{16,8},{17,9... | collective-permute-start | bytes 1544 | tf_op jit(solution)/shard_map/ppermute | solution.py:209
  23.6 0.4 %collective-permute-start.9 = (f32[1,128]{1,0:T(1,128)S(1)}, f32[1,128]{1,0:T(1,128)S(1)}, u32[]{:S(2)}, u32[]{:S(2)}) collective-permute-start(f32[1,128]{1,0:T(1,128)S(1)} %get-tuple-element.29), channel_id=1, source_target_pairs={{0,16},{1,17},{2,18},{3,19},{4,20},{5,21},{6,22},{7,23},{24,8},{25... | collective-permute-start | bytes 1544 | tf_op jit(solution)/shard_map/ppermute | solution.py:209
  24.0 1.6 %collective-permute-start.12 = (f32[1,128]{1,0:T(1,128)S(1)}, f32[1,128]{1,0:T(1,128)S(1)}, u32[]{:S(2)}, u32[]{:S(2)}) collective-permute-start(f32[1,128]{1,0:T(1,128)S(1)} %slice.19), channel_id=1, source_target_pairs={{0,2},{1,3},{2,0},{3,1},{4,6},{5,7},{6,4},{7,5},{8,10},{9,11},{10,... | collective-permute-start | bytes 1544 | tf_op jit(solution)/shard_map/ppermute | solution.py:213
  25.6 1.6 %collective-permute-done.9 = f32[1,128]{1,0:T(1,128)S(1)} collective-permute-done((f32[1,128]{1,0:T(1,128)S(1)}, f32[1,128]{1,0:T(1,128)S(1)}, u32[]{:S(2)}, u32[]{:S(2)}) %collective-permute-start.9) | collective-permute-done | bytes 544 | tf_op jit(solution)/shard_map/ppermute | solution.py:209
  27.2 0.4 %collective-permute-done.12 = f32[1,128]{1,0:T(1,128)S(1)} collective-permute-done((f32[1,128]{1,0:T(1,128)S(1)}, f32[1,128]{1,0:T(1,128)S(1)}, u32[]{:S(2)}, u32[]{:S(2)}) %collective-permute-start.12) | collective-permute-done | bytes 544 | tf_op jit(solution)/shard_map/ppermute | solution.py:213
  27.6 0.5 %maximum_bitcast_fusion = f32[128]{0:T(128)} fusion(f32[1,128]{1,0:T(1,128)S(1)} %collective-permute-done.12, f32[1,128]{1,0:T(1,128)S(1)} %maximum_maximum_fusion, f32[2,128]{1,0:T(2,128)S(1)} %max.21), kind=kLoop, calls=%fused_computation | loop fusion | flops 256 | bytes 2048 | tf_op jit(solution)/shard_map/reshape | solution.py:257
  (12 shorter events, 0.0 us)
Async XLA Ops:
  2.6 11.4 %collective-permute-start.3 = (bf16[832,128]{1,0:T(8,128)(2,1)S(1)}, bf16[832,128]{1,0:T(8,128)(2,1)S(1)}, u32[]{:S(2)}, u32[]{:S(2)}) collective-permute-start(bf16[832,128]{1,0:T(8,128)(2,1)S(1)} %get-tuple-element.19), channel_id=1, source_target_pairs={{0,8},{1,9},{2,10},{3,11},{4,12},{5,13},{6,14},{7,15},{8,16},{9,17... | collective-permute-start | bytes 638984 | tf_op jit(solution)/shard_map/ppermute | solution.py:209
  5.7 6.4 %collective-permute-start = (bf16[784,128]{1,0:T(8,128)(2,1)S(1)}, bf16[784,128]{1,0:T(8,128)(2,1)S(1)}, u32[]{:S(2)}, u32[]{:S(2)}) collective-permute-start(bf16[784,128]{1,0:T(8,128)(2,1)S(1)} %get-tuple-element.17.refs_0_.refs_2_), channel_id=1, source_target_pairs={{0,4},{1,5},{2,6},{3,7},{4,0},{5,1},{6,2},{7,3},{8,12},{9,13},{10,... | collective-permute-start | bytes 602120 | tf_op jit(solution)/shard_map/ppermute | solution.py:213
  7.2 7.3 %collective-permute-start.1 = (bf16[784,128]{1,0:T(8,128)(2,1)S(1)}, bf16[784,128]{1,0:T(8,128)(2,1)S(1)}, u32[]{:S(2)}, u32[]{:S(2)}) collective-permute-start(bf16[784,128]{1,0:T(8,128)(2,1)S(1)} %get-tuple-element.17.refs_0_.refs_2_), channel_id=1, source_target_pairs={{0,2},{1,3},{2,0},{3,1},{4,6},{5,7},{6,4},{7,5},{8,10},{9,11},{10,... | collective-permute-start | bytes 602120 | tf_op jit(solution)/shard_map/ppermute | solution.py:213
  8.7 8.6 %collective-permute-start.4 = (bf16[784,128]{1,0:T(8,128)(2,1)S(1)}, bf16[784,128]{1,0:T(8,128)(2,1)S(1)}, u32[]{:S(2)}, u32[]{:S(2)}) collective-permute-start(bf16[784,128]{1,0:T(8,128)(2,1)S(1)} %get-tuple-element.17.refs_0_.refs_2_), channel_id=1, source_target_pairs={{16,0},{17,1},{18,2},{19,3},{20,4},{21,5},{22,6},{23,7},{8,24},{9,... | collective-permute-start | bytes 602120 | tf_op jit(solution)/shard_map/ppermute | solution.py:209
  12.2 5.7 %collective-permute-start.2 = (bf16[784,128]{1,0:T(8,128)(2,1)S(1)}, bf16[784,128]{1,0:T(8,128)(2,1)S(1)}, u32[]{:S(2)}, u32[]{:S(2)}) collective-permute-start(bf16[784,128]{1,0:T(8,128)(2,1)S(1)} %collective-permute-done.refs_1_.refs_2_), channel_id=1, source_target_pairs={{0,2},{1,3},{2,0},{3,1},{4,6},{5,7},{6,4},{7,5},{8,10},{9,11},{10,... | collective-permute-start | bytes 602120 | tf_op jit(solution)/shard_map/ppermute | solution.py:213
  14.0 4.7 %collective-permute-start.6 = (bf16[832,128]{1,0:T(8,128)(2,1)S(1)}, bf16[832,128]{1,0:T(8,128)(2,1)S(1)}, u32[]{:S(2)}, u32[]{:S(2)}) collective-permute-start(bf16[832,128]{1,0:T(8,128)(2,1)S(1)} %collective-permute-done.3.refs_5_), channel_id=1, source_target_pairs={{0,1},{1,0},{2,3},{3,2},{4,5},{5,4},{6,7},{7,6},{8,9},{9,8},{10,11... | collective-permute-start | bytes 638984 | tf_op jit(solution)/shard_map/ppermute | solution.py:213
  14.1 4.4 %collective-permute-start.5 = (bf16[784,128]{1,0:T(8,128)(2,1)S(1)}, bf16[784,128]{1,0:T(8,128)(2,1)S(1)}, u32[]{:S(2)}, u32[]{:S(2)}) collective-permute-start(bf16[784,128]{1,0:T(8,128)(2,1)S(1)} %get-tuple-element.18.refs_0_.refs_4_), channel_id=1, source_target_pairs={{0,1},{1,0},{2,3},{3,2},{4,5},{5,4},{6,7},{7,6},{8,9},{9,8},{10,11... | collective-permute-start | bytes 602120 | tf_op jit(solution)/shard_map/ppermute | solution.py:213
  17.3 1.4 %collective-permute-start.7 = (bf16[784,128]{1,0:T(8,128)(2,1)S(1)}, bf16[784,128]{1,0:T(8,128)(2,1)S(1)}, u32[]{:S(2)}, u32[]{:S(2)}) collective-permute-start(bf16[784,128]{1,0:T(8,128)(2,1)S(1)} %collective-permute-done.4.refs_6_), channel_id=1, source_target_pairs={{0,1},{1,0},{2,3},{3,2},{4,5},{5,4},{6,7},{7,6},{8,9},{9,8},{10,11... | collective-permute-start | bytes 602120 | tf_op jit(solution)/shard_map/ppermute | solution.py:213
  19.5 1.7 %collective-permute-start.8 = (f32[3,128]{1,0:T(4,128)S(1)}, f32[3,128]{1,0:T(4,128)S(1)}, u32[]{:S(2)}, u32[]{:S(2)}) collective-permute-start(f32[3,128]{1,0:T(4,128)S(1)} %get-tuple-element.26), channel_id=1, source_target_pairs={{0,1},{1,0},{2,3},{3,2},{4,5},{5,4},{6,7},{7,6},{8,9},{9,8},{10,11... | collective-permute-start | bytes 4616 | tf_op jit(solution)/shard_map/ppermute | solution.py:213
  19.6 4.4 %collective-permute-start.11 = (f32[2,128]{1,0:T(2,128)S(1)}, f32[2,128]{1,0:T(2,128)S(1)}, u32[]{:S(2)}, u32[]{:S(2)}) collective-permute-start(f32[2,128]{1,0:T(2,128)S(1)} %get-tuple-element.28), channel_id=1, source_target_pairs={{0,4},{1,5},{2,6},{3,7},{4,0},{5,1},{6,2},{7,3},{8,12},{9,13},{10,... | collective-permute-start | bytes 3080 | tf_op jit(solution)/shard_map/ppermute | solution.py:213
  21.2 4.4 %collective-permute-start.10 = (f32[1,128]{1,0:T(1,128)S(1)}, f32[1,128]{1,0:T(1,128)S(1)}, u32[]{:S(2)}, u32[]{:S(2)}) collective-permute-start(f32[1,128]{1,0:T(1,128)S(1)} %get-tuple-element.30), channel_id=1, source_target_pairs={{8,0},{9,1},{10,2},{11,3},{12,4},{13,5},{14,6},{15,7},{16,8},{17,9... | collective-permute-start | bytes 1544 | tf_op jit(solution)/shard_map/ppermute | solution.py:209
  23.6 3.5 %collective-permute-start.9 = (f32[1,128]{1,0:T(1,128)S(1)}, f32[1,128]{1,0:T(1,128)S(1)}, u32[]{:S(2)}, u32[]{:S(2)}) collective-permute-start(f32[1,128]{1,0:T(1,128)S(1)} %get-tuple-element.29), channel_id=1, source_target_pairs={{0,16},{1,17},{2,18},{3,19},{4,20},{5,21},{6,22},{7,23},{24,8},{25... | collective-permute-start | bytes 1544 | tf_op jit(solution)/shard_map/ppermute | solution.py:209
  24.0 3.6 %collective-permute-start.12 = (f32[1,128]{1,0:T(1,128)S(1)}, f32[1,128]{1,0:T(1,128)S(1)}, u32[]{:S(2)}, u32[]{:S(2)}) collective-permute-start(f32[1,128]{1,0:T(1,128)S(1)} %slice.19), channel_id=1, source_target_pairs={{0,2},{1,3},{2,0},{3,1},{4,6},{5,7},{6,4},{7,5},{8,10},{9,11},{10,... | collective-permute-start | bytes 1544 | tf_op jit(solution)/shard_map/ppermute | solution.py:213

commit v12 on v9

--- a/solution.py
+++ b/solution.py
@@ -34,7 +34,7 @@
         pltpu.make_async_copy(src, dst, small_sem.at[i])
         for i, (src, dst) in enumerate(((owner_hbm, owner), (sub_hbm, sub), (prio_hbm, prio)))
     ]
-    for copy in [whole] + copies + small:
+    for copy in small + [whole] + copies:
         copy.start()
     whole.wait()
     projected = None

time: 28.2 us -> 28.2 us (level)
  no operation moved by 1% of the time
where the time goes in v12:
time: 28.2 us; the launch traced here: 28.1 us
  starting transfers between devices  15.8 us (56%)
  waiting for transfers between devices  7.44 us (26%)
  Pallas kernels  4.24 us (15%)
  other arithmetic  0.52 us (2%)
    ppermute x9, starting transfers between devices, swap(): return lax.ppermute(array, AXES, pairs)  8.33 us
    ppermute x4, starting transfers between devices, move(): return lax.ppermute(array, AXES, whole)  7.46 us
    ppermute x4, waiting for transfers between devices, move(): return lax.ppermute(array, AXES, whole)  4.33 us
    ppermute x9, waiting for transfers between devices, swap(): return lax.ppermute(array, AXES, pairs)  3.11 us
    pallas_call x1, Pallas kernels, embed(): pl.pallas_call(embed_kernel, in_specs=[HBM] * 5, out_specs=[VMEM] * 2, ou...  2.57 us
    pallas_call x3, Pallas kernels, score(): pl.pallas_call(lambda *refs: score_kernel(*counts, *rest, *refs), in_spec...  1.67 us
  transfers between devices with their start and end apart: 13, of which 6 were waited for; matrix products, arithmetic and copies ran while one was open for 0% of the time, Pallas kernels for 3%

profile of v12, /device:TPU:0, one launch (start us, length us, event | category | flops | bytes accessed | tf_op | source)
XLA Modules:
  0.0 28.1 jit_solution(3288966500614599198)
XLA Ops:
  0.0 2.6 %embed.1 = (bf16[784,128]{1,0:T(8,128)(2,1)S(1)}, bf16[832,128]{1,0:T(8,128)(2,1)S(1)}) custom-call(bf16[128,2048]{1,0:T(8,128)(2,1)} %states_hbm.1, bf16[2048,768]{1,0:T(8,128)(2,1)} %proj_hbm.1, s32[1,128]{1,0:T(1,128)} %bitcast.5, s32[1,128]{1,0:T(1,128)} %bitcast.6, s32[1,128]{1,0:T(1,128)} %bitcast.7), custom_call_target="tpu_custom_call" | custom-call | tf_op jit(solution)/shard_map/embed/pallas_call | solution.py:66
  2.6 3.1 %collective-permute-start.3 = (bf16[832,128]{1,0:T(8,128)(2,1)S(1)}, bf16[832,128]{1,0:T(8,128)(2,1)S(1)}, u32[]{:S(2)}, u32[]{:S(2)}) collective-permute-start(bf16[832,128]{1,0:T(8,128)(2,1)S(1)} %get-tuple-element.19), channel_id=1, source_target_pairs={{0,8},{1,9},{2,10},{3,11},{4,12},{5,13},{6,14},{7,15},{8,16},{9,17... | collective-permute-start | bytes 638984 | tf_op jit(solution)/shard_map/ppermute | solution.py:209
  5.7 1.5 %collective-permute-start = (bf16[784,128]{1,0:T(8,128)(2,1)S(1)}, bf16[784,128]{1,0:T(8,128)(2,1)S(1)}, u32[]{:S(2)}, u32[]{:S(2)}) collective-permute-start(bf16[784,128]{1,0:T(8,128)(2,1)S(1)} %get-tuple-element.17.refs_0_.refs_2_), channel_id=1, source_target_pairs={{0,4},{1,5},{2,6},{3,7},{4,0},{5,1},{6,2},{7,3},{8,12},{9,13},{10,... | collective-permute-start | bytes 602120 | tf_op jit(solution)/shard_map/ppermute | solution.py:213
  7.2 1.5 %collective-permute-start.1 = (bf16[784,128]{1,0:T(8,128)(2,1)S(1)}, bf16[784,128]{1,0:T(8,128)(2,1)S(1)}, u32[]{:S(2)}, u32[]{:S(2)}) collective-permute-start(bf16[784,128]{1,0:T(8,128)(2,1)S(1)} %get-tuple-element.17.refs_0_.refs_2_), channel_id=1, source_target_pairs={{0,2},{1,3},{2,0},{3,1},{4,6},{5,7},{6,4},{7,5},{8,10},{9,11},{10,... | collective-permute-start | bytes 602120 | tf_op jit(solution)/shard_map/ppermute | solution.py:213
  8.7 1.6 %collective-permute-start.4 = (bf16[784,128]{1,0:T(8,128)(2,1)S(1)}, bf16[784,128]{1,0:T(8,128)(2,1)S(1)}, u32[]{:S(2)}, u32[]{:S(2)}) collective-permute-start(bf16[784,128]{1,0:T(8,128)(2,1)S(1)} %get-tuple-element.17.refs_0_.refs_2_), channel_id=1, source_target_pairs={{16,0},{17,1},{18,2},{19,3},{20,4},{21,5},{22,6},{23,7},{8,24},{9,... | collective-permute-start | bytes 602120 | tf_op jit(solution)/shard_map/ppermute | solution.py:209
  10.2 1.9 %collective-permute-done.refs_1_.refs_2_ = bf16[784,128]{1,0:T(8,128)(2,1)S(1)} collective-permute-done((bf16[784,128]{1,0:T(8,128)(2,1)S(1)}, bf16[784,128]{1,0:T(8,128)(2,1)S(1)}, u32[]{:S(2)}, u32[]{:S(2)}) %collective-permute-start) | collective-permute-done | bytes 200736 | tf_op jit(solution)/shard_map/ppermute | solution.py:213
  12.1 1.5 %collective-permute-start.2 = (bf16[784,128]{1,0:T(8,128)(2,1)S(1)}, bf16[784,128]{1,0:T(8,128)(2,1)S(1)}, u32[]{:S(2)}, u32[]{:S(2)}) collective-permute-start(bf16[784,128]{1,0:T(8,128)(2,1)S(1)} %collective-permute-done.refs_1_.refs_2_), channel_id=1, source_target_pairs={{0,2},{1,3},{2,0},{3,1},{4,6},{5,7},{6,4},{7,5},{8,10},{9,11},{10,... | collective-permute-start | bytes 602120 | tf_op jit(solution)/shard_map/ppermute | solution.py:213
  13.6 0.3 %score_soon.1 = (f32[1,128]{1,0:T(1,128)S(1)}, bf16[784,128]{1,0:T(8,128)(2,1)S(1)}) custom-call(bf16[784,128]{1,0:T(8,128)(2,1)S(1)} %get-tuple-element.17.refs_0_.refs_2_, bf16[784,128]{1,0:T(8,128)(2,1)S(1)} %collective-permute-done.refs_1_.refs_2_, bf16[784,128]{1,0:T(8,128)(2,1)S(1)} %get-tuple-element.17.refs_0_.refs_2_), custom_call_target="tpu_custom_call" | custom-call | flops 50331648 | bytes 589824 | tf_op jit(solution)/shard_map/score_soon/pallas_call | solution.py:177
  13.9 0.1 collective-permute-start.6
  14.0 0.5 %collective-permute-start.5 = (bf16[784,128]{1,0:T(8,128)(2,1)S(1)}, bf16[784,128]{1,0:T(8,128)(2,1)S(1)}, u32[]{:S(2)}, u32[]{:S(2)}) collective-permute-start(bf16[784,128]{1,0:T(8,128)(2,1)S(1)} %get-tuple-element.18.refs_0_.refs_4_), channel_id=1, source_target_pairs={{0,1},{1,0},{2,3},{3,2},{4,5},{5,4},{6,7},{7,6},{8,9},{9,8},{10,11... | collective-permute-start | bytes 602120 | tf_op jit(solution)/shard_map/ppermute | solution.py:213
  14.5 2.7 %collective-permute-done.4.refs_6_ = bf16[784,128]{1,0:T(8,128)(2,1)S(1)} collective-permute-done((bf16[784,128]{1,0:T(8,128)(2,1)S(1)}, bf16[784,128]{1,0:T(8,128)(2,1)S(1)}, u32[]{:S(2)}, u32[]{:S(2)}) %collective-permute-start.4) | collective-permute-done | bytes 200736 | tf_op jit(solution)/shard_map/ppermute | solution.py:209
  17.2 0.6 %collective-permute-done.2.refs_3_ = bf16[784,128]{1,0:T(8,128)(2,1)S(1)} collective-permute-done((bf16[784,128]{1,0:T(8,128)(2,1)S(1)}, bf16[784,128]{1,0:T(8,128)(2,1)S(1)}, u32[]{:S(2)}, u32[]{:S(2)}) %collective-permute-start.2) | collective-permute-done | bytes 200736 | tf_op jit(solution)/shard_map/ppermute | solution.py:213
  17.8 0.6 %score_late.1 = (f32[3,128]{1,0:T(4,128)S(1)}, f32[128,128]{1,0:T(8,128)S(1)}, f32[128,8]{1,0:T(8,128)S(1)}) custom-call(bf16[784,128]{1,0:T(8,128)(2,1)S(1)} %get-tuple-element.18.refs_0_.refs_4_, bf16[784,128]{1,0:T(8,128)(2,1)S(1)} %collective-permute-done.1.refs_1_, bf16[784,128]{1,0:T(8,128)(2,1)S(1)} %collective-permute-done.refs_1_.refs_2_, ...), custom_call_target="tpu_custom_call" | custom-call | flops 251658240 | bytes 1376256 | tf_op jit(solution)/shard_map/score_late/pallas_call | solution.py:177
  18.5 0.2 collective-permute-done.7.refs_6_
  18.7 0.7 %score_partner.1 = (f32[3,128]{1,0:T(4,128)S(1)}, f32[2,128]{1,0:T(2,128)S(1)}, f32[2,128]{1,0:T(2,128)S(1)}) custom-call(bf16[784,128]{1,0:T(8,128)(2,1)S(1)} %get-tuple-element.18.refs_0_.refs_4_, bf16[784,128]{1,0:T(8,128)(2,1)S(1)} %collective-permute-done.1.refs_1_, bf16[784,128]{1,0:T(8,128)(2,1)S(1)} %collective-permute-done.refs_1_.refs_2_, ...), custom_call_target="tpu_custom_call" | custom-call | flops 301989888 | bytes 1376256 | tf_op jit(solution)/shard_map/score_partner/pallas_call | solution.py:177
  19.4 0.2 collective-permute-start.8
  19.6 1.5 %collective-permute-start.11 = (f32[2,128]{1,0:T(2,128)S(1)}, f32[2,128]{1,0:T(2,128)S(1)}, u32[]{:S(2)}, u32[]{:S(2)}) collective-permute-start(f32[2,128]{1,0:T(2,128)S(1)} %get-tuple-element.28), channel_id=1, source_target_pairs={{0,4},{1,5},{2,6},{3,7},{4,0},{5,1},{6,2},{7,3},{8,12},{9,13},{10,... | collective-permute-start | bytes 3080 | tf_op jit(solution)/shard_map/ppermute | solution.py:213
  21.1 2.4 %collective-permute-start.10 = (f32[1,128]{1,0:T(1,128)S(1)}, f32[1,128]{1,0:T(1,128)S(1)}, u32[]{:S(2)}, u32[]{:S(2)}) collective-permute-start(f32[1,128]{1,0:T(1,128)S(1)} %get-tuple-element.30), channel_id=1, source_target_pairs={{8,0},{9,1},{10,2},{11,3},{12,4},{13,5},{14,6},{15,7},{16,8},{17,9... | collective-permute-start | bytes 1544 | tf_op jit(solution)/shard_map/ppermute | solution.py:209
  23.6 0.4 %collective-permute-start.9 = (f32[1,128]{1,0:T(1,128)S(1)}, f32[1,128]{1,0:T(1,128)S(1)}, u32[]{:S(2)}, u32[]{:S(2)}) collective-permute-start(f32[1,128]{1,0:T(1,128)S(1)} %get-tuple-element.29), channel_id=1, source_target_pairs={{0,16},{1,17},{2,18},{3,19},{4,20},{5,21},{6,22},{7,23},{24,8},{25... | collective-permute-start | bytes 1544 | tf_op jit(solution)/shard_map/ppermute | solution.py:209
  23.9 0.0 collective-permute-done.11
  24.0 1.6 %collective-permute-start.12 = (f32[1,128]{1,0:T(1,128)S(1)}, f32[1,128]{1,0:T(1,128)S(1)}, u32[]{:S(2)}, u32[]{:S(2)}) collective-permute-start(f32[1,128]{1,0:T(1,128)S(1)} %slice.19), channel_id=1, source_target_pairs={{0,2},{1,3},{2,0},{3,1},{4,6},{5,7},{6,4},{7,5},{8,10},{9,11},{10,... | collective-permute-start | bytes 1544 | tf_op jit(solution)/shard_map/ppermute | solution.py:213
  25.5 1.6 %collective-permute-done.9 = f32[1,128]{1,0:T(1,128)S(1)} collective-permute-done((f32[1,128]{1,0:T(1,128)S(1)}, f32[1,128]{1,0:T(1,128)S(1)}, u32[]{:S(2)}, u32[]{:S(2)}) %collective-permute-start.9) | collective-permute-done | bytes 544 | tf_op jit(solution)/shard_map/ppermute | solution.py:209
  27.1 0.4 %collective-permute-done.12 = f32[1,128]{1,0:T(1,128)S(1)} collective-permute-done((f32[1,128]{1,0:T(1,128)S(1)}, f32[1,128]{1,0:T(1,128)S(1)}, u32[]{:S(2)}, u32[]{:S(2)}) %collective-permute-start.12) | collective-permute-done | bytes 544 | tf_op jit(solution)/shard_map/ppermute | solution.py:213
  27.6 0.5 %maximum_bitcast_fusion = f32[128]{0:T(128)} fusion(f32[1,128]{1,0:T(1,128)S(1)} %collective-permute-done.12, f32[1,128]{1,0:T(1,128)S(1)} %maximum_maximum_fusion, f32[2,128]{1,0:T(2,128)S(1)} %max.21), kind=kLoop, calls=%fused_computation | loop fusion | flops 256 | bytes 2048 | tf_op jit(solution)/shard_map/reshape | solution.py:257
  (12 shorter events, 0.0 us)
Async XLA Ops:
  2.6 11.3 %collective-permute-start.3 = (bf16[832,128]{1,0:T(8,128)(2,1)S(1)}, bf16[832,128]{1,0:T(8,128)(2,1)S(1)}, u32[]{:S(2)}, u32[]{:S(2)}) collective-permute-start(bf16[832,128]{1,0:T(8,128)(2,1)S(1)} %get-tuple-element.19), channel_id=1, source_target_pairs={{0,8},{1,9},{2,10},{3,11},{4,12},{5,13},{6,14},{7,15},{8,16},{9,17... | collective-permute-start | bytes 638984 | tf_op jit(solution)/shard_map/ppermute | solution.py:209
  5.7 6.4 %collective-permute-start = (bf16[784,128]{1,0:T(8,128)(2,1)S(1)}, bf16[784,128]{1,0:T(8,128)(2,1)S(1)}, u32[]{:S(2)}, u32[]{:S(2)}) collective-permute-start(bf16[784,128]{1,0:T(8,128)(2,1)S(1)} %get-tuple-element.17.refs_0_.refs_2_), channel_id=1, source_target_pairs={{0,4},{1,5},{2,6},{3,7},{4,0},{5,1},{6,2},{7,3},{8,12},{9,13},{10,... | collective-permute-start | bytes 602120 | tf_op jit(solution)/shard_map/ppermute | solution.py:213
  7.2 7.3 %collective-permute-start.1 = (bf16[784,128]{1,0:T(8,128)(2,1)S(1)}, bf16[784,128]{1,0:T(8,128)(2,1)S(1)}, u32[]{:S(2)}, u32[]{:S(2)}) collective-permute-start(bf16[784,128]{1,0:T(8,128)(2,1)S(1)} %get-tuple-element.17.refs_0_.refs_2_), channel_id=1, source_target_pairs={{0,2},{1,3},{2,0},{3,1},{4,6},{5,7},{6,4},{7,5},{8,10},{9,11},{10,... | collective-permute-start | bytes 602120 | tf_op jit(solution)/shard_map/ppermute | solution.py:213
  8.7 8.6 %collective-permute-start.4 = (bf16[784,128]{1,0:T(8,128)(2,1)S(1)}, bf16[784,128]{1,0:T(8,128)(2,1)S(1)}, u32[]{:S(2)}, u32[]{:S(2)}) collective-permute-start(bf16[784,128]{1,0:T(8,128)(2,1)S(1)} %get-tuple-element.17.refs_0_.refs_2_), channel_id=1, source_target_pairs={{16,0},{17,1},{18,2},{19,3},{20,4},{21,5},{22,6},{23,7},{8,24},{9,... | collective-permute-start | bytes 602120 | tf_op jit(solution)/shard_map/ppermute | solution.py:209
  12.1 5.7 %collective-permute-start.2 = (bf16[784,128]{1,0:T(8,128)(2,1)S(1)}, bf16[784,128]{1,0:T(8,128)(2,1)S(1)}, u32[]{:S(2)}, u32[]{:S(2)}) collective-permute-start(bf16[784,128]{1,0:T(8,128)(2,1)S(1)} %collective-permute-done.refs_1_.refs_2_), channel_id=1, source_target_pairs={{0,2},{1,3},{2,0},{3,1},{4,6},{5,7},{6,4},{7,5},{8,10},{9,11},{10,... | collective-permute-start | bytes 602120 | tf_op jit(solution)/shard_map/ppermute | solution.py:213
  13.9 4.8 %collective-permute-start.6 = (bf16[832,128]{1,0:T(8,128)(2,1)S(1)}, bf16[832,128]{1,0:T(8,128)(2,1)S(1)}, u32[]{:S(2)}, u32[]{:S(2)}) collective-permute-start(bf16[832,128]{1,0:T(8,128)(2,1)S(1)} %collective-permute-done.3.refs_5_), channel_id=1, source_target_pairs={{0,1},{1,0},{2,3},{3,2},{4,5},{5,4},{6,7},{7,6},{8,9},{9,8},{10,11... | collective-permute-start | bytes 638984 | tf_op jit(solution)/shard_map/ppermute | solution.py:213
  14.0 4.4 %collective-permute-start.5 = (bf16[784,128]{1,0:T(8,128)(2,1)S(1)}, bf16[784,128]{1,0:T(8,128)(2,1)S(1)}, u32[]{:S(2)}, u32[]{:S(2)}) collective-permute-start(bf16[784,128]{1,0:T(8,128)(2,1)S(1)} %get-tuple-element.18.refs_0_.refs_4_), channel_id=1, source_target_pairs={{0,1},{1,0},{2,3},{3,2},{4,5},{5,4},{6,7},{7,6},{8,9},{9,8},{10,11... | collective-permute-start | bytes 602120 | tf_op jit(solution)/shard_map/ppermute | solution.py:213
  17.2 1.4 %collective-permute-start.7 = (bf16[784,128]{1,0:T(8,128)(2,1)S(1)}, bf16[784,128]{1,0:T(8,128)(2,1)S(1)}, u32[]{:S(2)}, u32[]{:S(2)}) collective-permute-start(bf16[784,128]{1,0:T(8,128)(2,1)S(1)} %collective-permute-done.4.refs_6_), channel_id=1, source_target_pairs={{0,1},{1,0},{2,3},{3,2},{4,5},{5,4},{6,7},{7,6},{8,9},{9,8},{10,11... | collective-permute-start | bytes 602120 | tf_op jit(solution)/shard_map/ppermute | solution.py:213
  19.4 1.7 %collective-permute-start.8 = (f32[3,128]{1,0:T(4,128)S(1)}, f32[3,128]{1,0:T(4,128)S(1)}, u32[]{:S(2)}, u32[]{:S(2)}) collective-permute-start(f32[3,128]{1,0:T(4,128)S(1)} %get-tuple-element.26), channel_id=1, source_target_pairs={{0,1},{1,0},{2,3},{3,2},{4,5},{5,4},{6,7},{7,6},{8,9},{9,8},{10,11... | collective-permute-start | bytes 4616 | tf_op jit(solution)/shard_map/ppermute | solution.py:213
  19.6 4.4 %collective-permute-start.11 = (f32[2,128]{1,0:T(2,128)S(1)}, f32[2,128]{1,0:T(2,128)S(1)}, u32[]{:S(2)}, u32[]{:S(2)}) collective-permute-start(f32[2,128]{1,0:T(2,128)S(1)} %get-tuple-element.28), channel_id=1, source_target_pairs={{0,4},{1,5},{2,6},{3,7},{4,0},{5,1},{6,2},{7,3},{8,12},{9,13},{10,... | collective-permute-start | bytes 3080 | tf_op jit(solution)/shard_map/ppermute | solution.py:213
  21.1 4.4 %collective-permute-start.10 = (f32[1,128]{1,0:T(1,128)S(1)}, f32[1,128]{1,0:T(1,128)S(1)}, u32[]{:S(2)}, u32[]{:S(2)}) collective-permute-start(f32[1,128]{1,0:T(1,128)S(1)} %get-tuple-element.30), channel_id=1, source_target_pairs={{8,0},{9,1},{10,2},{11,3},{12,4},{13,5},{14,6},{15,7},{16,8},{17,9... | collective-permute-start | bytes 1544 | tf_op jit(solution)/shard_map/ppermute | solution.py:209
  23.6 3.5 %collective-permute-start.9 = (f32[1,128]{1,0:T(1,128)S(1)}, f32[1,128]{1,0:T(1,128)S(1)}, u32[]{:S(2)}, u32[]{:S(2)}) collective-permute-start(f32[1,128]{1,0:T(1,128)S(1)} %get-tuple-element.29), channel_id=1, source_target_pairs={{0,16},{1,17},{2,18},{3,19},{4,20},{5,21},{6,22},{7,23},{24,8},{25... | collective-permute-start | bytes 1544 | tf_op jit(solution)/shard_map/ppermute | solution.py:209
  24.0 3.6 %collective-permute-start.12 = (f32[1,128]{1,0:T(1,128)S(1)}, f32[1,128]{1,0:T(1,128)S(1)}, u32[]{:S(2)}, u32[]{:S(2)}) collective-permute-start(f32[1,128]{1,0:T(1,128)S(1)} %slice.19), channel_id=1, source_target_pairs={{0,2},{1,3},{2,0},{3,1},{4,6},{5,7},{6,4},{7,5},{8,10},{9,11},{10,... | collective-permute-start | bytes 1544 | tf_op jit(solution)/shard_map/ppermute | solution.py:213
